TPU v7x, 128 devices: a whole 4x4x4 slice. The times are simulated.
128 devices in a mesh: section: 16 (over z_lo, y, core), tensor: 8 (over z_hi, x).
Axes of the slice: x: 4, y: 4, z: 4 (z_hi: 2, z_lo: 2; z = z_hi * 2 + z_lo), core: 2. Of those that a mesh axis runs over, the one named last changes fastest.
Arguments:
- grad_top: bfloat16 [2, 64, 6144], P(None, None, 'tensor'), may hold values from -6 to 6
- query: bfloat16 [16, 2, 64, 6144], P('section', None, None, 'tensor'), as said below
- keys: bfloat16 [16, 2, 64, 1024], P('section', None, None, 'tensor'), as said below
- values: bfloat16 [16, 2, 64, 1024], P('section', None, None, 'tensor'), may hold values from -6 to 6
- out_weight: bfloat16 [16, 6144, 6144], P('section', 'tensor'), may hold values from -0.078125 to 0.078125
- value_weight: bfloat16 [16, 6144, 1024], P('section', 'tensor'), may hold values from -0.046875 to 0.046875
Outputs:
- section_grads: bfloat16 [16, 2, 64, 6144], P('section', None, None, 'tensor')
- weight_grads: bfloat16 [16, 6144, 6144], P('section', 'tensor')
Inputs may be any that keep to these rules, and one draw needn't show every extreme that they name: `query`: entries of order one; in some draws some queries nearly repeat an earlier key, several times over. `keys`: entries of order one.
All inputs are finite; a program needn't handle non-finite values.
Results may differ from a plain program's by a relative error of at most 0.035.
Values may be sent and summed in bfloat16 or wider, within the bound.
No kernel may reach another device: no remote copies, remote signals or barrier semaphores. Data moves between devices by JAX's collectives and lax.ppermute only.
A program may use at most 128 MiB of HBM per device.

v0:
```python
import math

import jax
import jax.numpy as jnp
from jax import lax
from jax.sharding import PartitionSpec as P


def from_behind(value, axis, by):
    length = lax.axis_size(axis)
    pairs = [(i, i + by) for i in range(length) if 0 <= i + by < length]
    return lax.ppermute(value, axis, pairs)


def causal_probs(query_heads, key_rows):
    head_size = key_rows.shape[-1]
    length = key_rows.shape[0]
    logits = jnp.einsum("qgd,pd->gqp", query_heads, key_rows, preferred_element_type=jnp.float32)
    logits = logits * (1.0 / math.sqrt(head_size))
    row_pos = lax.broadcasted_iota(jnp.int32, (length, length), 0)
    col_pos = lax.broadcasted_iota(jnp.int32, (length, length), 1)
    logits = jnp.where(col_pos <= row_pos, logits, -jnp.inf)
    return jax.nn.softmax(logits, axis=-1).astype(jnp.bfloat16)


def on_device(grad_top, query, keys, values, out_weight, value_weight):
    sections = lax.axis_size("section")
    place = lax.axis_index("section")
    micro_batch = query.shape[1]
    length = query.shape[2]
    head_size = keys.shape[3]
    group = query.shape[3] // head_size
    width = out_weight.shape[2]
    feat_local = grad_top.shape[2]
    query_heads = query[0].reshape(micro_batch, length, group, head_size)
    attention_probs = jax.vmap(causal_probs)(query_heads, keys[0])
    mixed_values = jnp.einsum(
        "mgqp,mpd->mqgd", attention_probs, values[0], preferred_element_type=jnp.float32
    )
    mixed_values = mixed_values.astype(jnp.bfloat16).reshape(micro_batch, length, group * head_size)
    out_mat = out_weight[0]
    value_local = value_weight[0]
    grads_init = jnp.zeros((micro_batch, length, feat_local), jnp.bfloat16)
    saved_init = jnp.zeros((micro_batch, length, width), jnp.bfloat16)

    def advance(turn, carry):
        arriving, grads_buf, saved = carry
        slot = turn - (sections - 1 - place)
        active = jnp.logical_and(slot >= 0, slot < micro_batch)
        slot_now = jnp.clip(slot, 0, micro_batch - 1)
        top_rows = lax.dynamic_index_in_dim(grad_top, slot_now, 0, keepdims=False)
        grad_rows = jnp.where(place == sections - 1, top_rows, arriving)
        grad_full = lax.all_gather(grad_rows, "tensor", axis=1, tiled=True)
        attn_grad = lax.dot_general(
            grad_full, out_mat, (((1,), (1,)), ((), ())), preferred_element_type=jnp.float32
        )
        attn_grad = attn_grad.astype(jnp.bfloat16).reshape(length, group, head_size)
        probs_now = lax.dynamic_index_in_dim(attention_probs, slot_now, 0, keepdims=False)
        value_grad = jnp.einsum(
            "gqp,qgd->pd", probs_now, attn_grad, preferred_element_type=jnp.float32
        ).astype(jnp.bfloat16)
        every_head = lax.all_gather(value_grad, "tensor", axis=1, tiled=True)
        branch = lax.dot_general(
            every_head, value_local, (((1,), (1,)), ((), ())), preferred_element_type=jnp.float32
        )
        new_rows = (grad_rows.astype(jnp.float32) + branch).astype(jnp.bfloat16)
        grads_buf = jnp.where(
            active, lax.dynamic_update_index_in_dim(grads_buf, new_rows, slot_now, 0), grads_buf
        )
        saved = jnp.where(
            active, lax.dynamic_update_index_in_dim(saved, grad_full, slot_now, 0), saved
        )
        arriving = from_behind(new_rows, "section", -1)
        return (arriving, grads_buf, saved)

    start_rows = jnp.zeros((length, feat_local), jnp.bfloat16)
    final_rows, grads_buf, saved = lax.fori_loop(
        0, sections + micro_batch - 1, advance, (start_rows, grads_init, saved_init)
    )
    weight_grad = jnp.einsum(
        "mqh,mqd->hd", mixed_values, saved, preferred_element_type=jnp.float32
    ).astype(jnp.bfloat16)
    return (grads_buf[None], weight_grad[None])


def solution(mesh):
    placed = (
        P(None, None, "tensor"),
        P("section", None, None, "tensor"),
        P("section", None, None, "tensor"),
        P("section", None, None, "tensor"),
        P("section", "tensor", None),
        P("section", "tensor", None),
    )
    return jax.shard_map(
        on_device,
        mesh=mesh,
        in_specs=placed,
        out_specs=(P("section", None, None, "tensor"), P("section", "tensor", None)),
        check_vma=False,
    )
```

profile of v0, /device:TPU:0, one launch (start us, length us, event | category | flops | bytes accessed | tf_op | source)
XLA Modules:
  0.0 1318.7 jit_solution(15400055181348979232)
XLA Ops:
  5.4 1305.4 %while.19 = (s32[]{:T(128)}, bf16[64,768]{1,0:T(8,128)(2,1)S(1)}, bf16[2,64,768]{2,1,0:T(8,128)(2,1)S(1)}, bf16[2,64,6144]{2,1,0:T(8,128)(2,1)}, pred[]{:T(512)}...) while((s32[]{:T(128)}, bf16[64,768]{1,0:T(8,128)(2,1)S(1)}, ...), condition=%wide.region_3.4_spmd, body=%wide.region_2.3_spmd.sunk | while | flops 711630848 | bytes 16711921 | solution.py:77
  5.4 37.0 %all_gather.20 = bf16[64,6144]{1,0:T(8,128)(2,1)S(1)} all-gather(bf16[64,768]{1,0:T(8,128)(2,1)S(1)} %bitcast_select_fusion.4), channel_id=1, replica_groups=mesh['section'=16,'tensor'=8] {'tensor'}, dimensions={1}, use_global_device_ids=true | all-gather | bytes 884736 | tf_op jit(solution)/shard_map/while/body/eval_jaxpr/all_gather | solution.py:53
  49.3 29.8 %all_gather.21 = bf16[64,1024]{1,0:T(8,128)(2,1)S(1)} all-gather(bf16[64,128]{1,0:T(8,128)(2,1)S(1)} %fusion.61), channel_id=1, replica_groups=mesh['section'=16,'tensor'=8] {'tensor'}, dimensions={1}, use_global_device_ids=true | all-gather | bytes 147456 | tf_op jit(solution)/shard_map/while/body/eval_jaxpr/all_gather | solution.py:62
  83.2 35.6 %all_gather.20 = bf16[64,6144]{1,0:T(8,128)(2,1)S(1)} all-gather(bf16[64,768]{1,0:T(8,128)(2,1)S(1)} %bitcast_select_fusion.4), channel_id=1, replica_groups=mesh['section'=16,'tensor'=8] {'tensor'}, dimensions={1}, use_global_device_ids=true | all-gather | bytes 884736 | tf_op jit(solution)/shard_map/while/body/eval_jaxpr/all_gather | solution.py:53
  125.7 29.8 %all_gather.21 = bf16[64,1024]{1,0:T(8,128)(2,1)S(1)} all-gather(bf16[64,128]{1,0:T(8,128)(2,1)S(1)} %fusion.61), channel_id=1, replica_groups=mesh['section'=16,'tensor'=8] {'tensor'}, dimensions={1}, use_global_device_ids=true | all-gather | bytes 147456 | tf_op jit(solution)/shard_map/while/body/eval_jaxpr/all_gather | solution.py:62
  159.6 35.8 %all_gather.20 = bf16[64,6144]{1,0:T(8,128)(2,1)S(1)} all-gather(bf16[64,768]{1,0:T(8,128)(2,1)S(1)} %bitcast_select_fusion.4), channel_id=1, replica_groups=mesh['section'=16,'tensor'=8] {'tensor'}, dimensions={1}, use_global_device_ids=true | all-gather | bytes 884736 | tf_op jit(solution)/shard_map/while/body/eval_jaxpr/all_gather | solution.py:53
  202.3 29.8 %all_gather.21 = bf16[64,1024]{1,0:T(8,128)(2,1)S(1)} all-gather(bf16[64,128]{1,0:T(8,128)(2,1)S(1)} %fusion.61), channel_id=1, replica_groups=mesh['section'=16,'tensor'=8] {'tensor'}, dimensions={1}, use_global_device_ids=true | all-gather | bytes 147456 | tf_op jit(solution)/shard_map/while/body/eval_jaxpr/all_gather | solution.py:62
  236.2 35.4 %all_gather.20 = bf16[64,6144]{1,0:T(8,128)(2,1)S(1)} all-gather(bf16[64,768]{1,0:T(8,128)(2,1)S(1)} %bitcast_select_fusion.4), channel_id=1, replica_groups=mesh['section'=16,'tensor'=8] {'tensor'}, dimensions={1}, use_global_device_ids=true | all-gather | bytes 884736 | tf_op jit(solution)/shard_map/while/body/eval_jaxpr/all_gather | solution.py:53
  278.5 29.8 %all_gather.21 = bf16[64,1024]{1,0:T(8,128)(2,1)S(1)} all-gather(bf16[64,128]{1,0:T(8,128)(2,1)S(1)} %fusion.61), channel_id=1, replica_groups=mesh['section'=16,'tensor'=8] {'tensor'}, dimensions={1}, use_global_device_ids=true | all-gather | bytes 147456 | tf_op jit(solution)/shard_map/while/body/eval_jaxpr/all_gather | solution.py:62
  312.4 35.6 %all_gather.20 = bf16[64,6144]{1,0:T(8,128)(2,1)S(1)} all-gather(bf16[64,768]{1,0:T(8,128)(2,1)S(1)} %bitcast_select_fusion.4), channel_id=1, replica_groups=mesh['section'=16,'tensor'=8] {'tensor'}, dimensions={1}, use_global_device_ids=true | all-gather | bytes 884736 | tf_op jit(solution)/shard_map/while/body/eval_jaxpr/all_gather | solution.py:53
  354.9 29.8 %all_gather.21 = bf16[64,1024]{1,0:T(8,128)(2,1)S(1)} all-gather(bf16[64,128]{1,0:T(8,128)(2,1)S(1)} %fusion.61), channel_id=1, replica_groups=mesh['section'=16,'tensor'=8] {'tensor'}, dimensions={1}, use_global_device_ids=true | all-gather | bytes 147456 | tf_op jit(solution)/shard_map/while/body/eval_jaxpr/all_gather | solution.py:62
  388.8 35.5 %all_gather.20 = bf16[64,6144]{1,0:T(8,128)(2,1)S(1)} all-gather(bf16[64,768]{1,0:T(8,128)(2,1)S(1)} %bitcast_select_fusion.4), channel_id=1, replica_groups=mesh['section'=16,'tensor'=8] {'tensor'}, dimensions={1}, use_global_device_ids=true | all-gather | bytes 884736 | tf_op jit(solution)/shard_map/while/body/eval_jaxpr/all_gather | solution.py:53
  431.1 29.9 %all_gather.21 = bf16[64,1024]{1,0:T(8,128)(2,1)S(1)} all-gather(bf16[64,128]{1,0:T(8,128)(2,1)S(1)} %fusion.61), channel_id=1, replica_groups=mesh['section'=16,'tensor'=8] {'tensor'}, dimensions={1}, use_global_device_ids=true | all-gather | bytes 147456 | tf_op jit(solution)/shard_map/while/body/eval_jaxpr/all_gather | solution.py:62
  465.2 35.3 %all_gather.20 = bf16[64,6144]{1,0:T(8,128)(2,1)S(1)} all-gather(bf16[64,768]{1,0:T(8,128)(2,1)S(1)} %bitcast_select_fusion.4), channel_id=1, replica_groups=mesh['section'=16,'tensor'=8] {'tensor'}, dimensions={1}, use_global_device_ids=true | all-gather | bytes 884736 | tf_op jit(solution)/shard_map/while/body/eval_jaxpr/all_gather | solution.py:53
  507.4 29.9 %all_gather.21 = bf16[64,1024]{1,0:T(8,128)(2,1)S(1)} all-gather(bf16[64,128]{1,0:T(8,128)(2,1)S(1)} %fusion.61), channel_id=1, replica_groups=mesh['section'=16,'tensor'=8] {'tensor'}, dimensions={1}, use_global_device_ids=true | all-gather | bytes 147456 | tf_op jit(solution)/shard_map/while/body/eval_jaxpr/all_gather | solution.py:62
  541.4 35.7 %all_gather.20 = bf16[64,6144]{1,0:T(8,128)(2,1)S(1)} all-gather(bf16[64,768]{1,0:T(8,128)(2,1)S(1)} %bitcast_select_fusion.4), channel_id=1, replica_groups=mesh['section'=16,'tensor'=8] {'tensor'}, dimensions={1}, use_global_device_ids=true | all-gather | bytes 884736 | tf_op jit(solution)/shard_map/while/body/eval_jaxpr/all_gather | solution.py:53
  584.0 29.8 %all_gather.21 = bf16[64,1024]{1,0:T(8,128)(2,1)S(1)} all-gather(bf16[64,128]{1,0:T(8,128)(2,1)S(1)} %fusion.61), channel_id=1, replica_groups=mesh['section'=16,'tensor'=8] {'tensor'}, dimensions={1}, use_global_device_ids=true | all-gather | bytes 147456 | tf_op jit(solution)/shard_map/while/body/eval_jaxpr/all_gather | solution.py:62
  617.9 35.7 %all_gather.20 = bf16[64,6144]{1,0:T(8,128)(2,1)S(1)} all-gather(bf16[64,768]{1,0:T(8,128)(2,1)S(1)} %bitcast_select_fusion.4), channel_id=1, replica_groups=mesh['section'=16,'tensor'=8] {'tensor'}, dimensions={1}, use_global_device_ids=true | all-gather | bytes 884736 | tf_op jit(solution)/shard_map/while/body/eval_jaxpr/all_gather | solution.py:53
  660.4 29.8 %all_gather.21 = bf16[64,1024]{1,0:T(8,128)(2,1)S(1)} all-gather(bf16[64,128]{1,0:T(8,128)(2,1)S(1)} %fusion.61), channel_id=1, replica_groups=mesh['section'=16,'tensor'=8] {'tensor'}, dimensions={1}, use_global_device_ids=true | all-gather | bytes 147456 | tf_op jit(solution)/shard_map/while/body/eval_jaxpr/all_gather | solution.py:62
  694.4 35.8 %all_gather.20 = bf16[64,6144]{1,0:T(8,128)(2,1)S(1)} all-gather(bf16[64,768]{1,0:T(8,128)(2,1)S(1)} %bitcast_select_fusion.4), channel_id=1, replica_groups=mesh['section'=16,'tensor'=8] {'tensor'}, dimensions={1}, use_global_device_ids=true | all-gather | bytes 884736 | tf_op jit(solution)/shard_map/while/body/eval_jaxpr/all_gather | solution.py:53
  737.1 29.8 %all_gather.21 = bf16[64,1024]{1,0:T(8,128)(2,1)S(1)} all-gather(bf16[64,128]{1,0:T(8,128)(2,1)S(1)} %fusion.61), channel_id=1, replica_groups=mesh['section'=16,'tensor'=8] {'tensor'}, dimensions={1}, use_global_device_ids=true | all-gather | bytes 147456 | tf_op jit(solution)/shard_map/while/body/eval_jaxpr/all_gather | solution.py:62
  771.1 35.9 %all_gather.20 = bf16[64,6144]{1,0:T(8,128)(2,1)S(1)} all-gather(bf16[64,768]{1,0:T(8,128)(2,1)S(1)} %bitcast_select_fusion.4), channel_id=1, replica_groups=mesh['section'=16,'tensor'=8] {'tensor'}, dimensions={1}, use_global_device_ids=true | all-gather | bytes 884736 | tf_op jit(solution)/shard_map/while/body/eval_jaxpr/all_gather | solution.py:53
  813.9 29.8 %all_gather.21 = bf16[64,1024]{1,0:T(8,128)(2,1)S(1)} all-gather(bf16[64,128]{1,0:T(8,128)(2,1)S(1)} %fusion.61), channel_id=1, replica_groups=mesh['section'=16,'tensor'=8] {'tensor'}, dimensions={1}, use_global_device_ids=true | all-gather | bytes 147456 | tf_op jit(solution)/shard_map/while/body/eval_jaxpr/all_gather | solution.py:62
  847.8 35.9 %all_gather.20 = bf16[64,6144]{1,0:T(8,128)(2,1)S(1)} all-gather(bf16[64,768]{1,0:T(8,128)(2,1)S(1)} %bitcast_select_fusion.4), channel_id=1, replica_groups=mesh['section'=16,'tensor'=8] {'tensor'}, dimensions={1}, use_global_device_ids=true | all-gather | bytes 884736 | tf_op jit(solution)/shard_map/while/body/eval_jaxpr/all_gather | solution.py:53
  890.5 29.9 %all_gather.21 = bf16[64,1024]{1,0:T(8,128)(2,1)S(1)} all-gather(bf16[64,128]{1,0:T(8,128)(2,1)S(1)} %fusion.61), channel_id=1, replica_groups=mesh['section'=16,'tensor'=8] {'tensor'}, dimensions={1}, use_global_device_ids=true | all-gather | bytes 147456 | tf_op jit(solution)/shard_map/while/body/eval_jaxpr/all_gather | solution.py:62
  924.6 35.9 %all_gather.20 = bf16[64,6144]{1,0:T(8,128)(2,1)S(1)} all-gather(bf16[64,768]{1,0:T(8,128)(2,1)S(1)} %bitcast_select_fusion.4), channel_id=1, replica_groups=mesh['section'=16,'tensor'=8] {'tensor'}, dimensions={1}, use_global_device_ids=true | all-gather | bytes 884736 | tf_op jit(solution)/shard_map/while/body/eval_jaxpr/all_gather | solution.py:53
  1001.6 35.9 %all_gather.20 = bf16[64,6144]{1,0:T(8,128)(2,1)S(1)} all-gather(bf16[64,768]{1,0:T(8,128)(2,1)S(1)} %bitcast_select_fusion.4), channel_id=1, replica_groups=mesh['section'=16,'tensor'=8] {'tensor'}, dimensions={1}, use_global_device_ids=true | all-gather | bytes 884736 | tf_op jit(solution)/shard_map/while/body/eval_jaxpr/all_gather | solution.py:53
  1078.6 35.8 %all_gather.20 = bf16[64,6144]{1,0:T(8,128)(2,1)S(1)} all-gather(bf16[64,768]{1,0:T(8,128)(2,1)S(1)} %bitcast_select_fusion.4), channel_id=1, replica_groups=mesh['section'=16,'tensor'=8] {'tensor'}, dimensions={1}, use_global_device_ids=true | all-gather | bytes 884736 | tf_op jit(solution)/shard_map/while/body/eval_jaxpr/all_gather | solution.py:53
  1121.3 29.8 %all_gather.21 = bf16[64,1024]{1,0:T(8,128)(2,1)S(1)} all-gather(bf16[64,128]{1,0:T(8,128)(2,1)S(1)} %fusion.61), channel_id=1, replica_groups=mesh['section'=16,'tensor'=8] {'tensor'}, dimensions={1}, use_global_device_ids=true | all-gather | bytes 147456 | tf_op jit(solution)/shard_map/while/body/eval_jaxpr/all_gather | solution.py:62
  1156.6 35.9 %all_gather.20 = bf16[64,6144]{1,0:T(8,128)(2,1)S(1)} all-gather(bf16[64,768]{1,0:T(8,128)(2,1)S(1)} %bitcast_select_fusion.4), channel_id=1, replica_groups=mesh['section'=16,'tensor'=8] {'tensor'}, dimensions={1}, use_global_device_ids=true | all-gather | bytes 884736 | tf_op jit(solution)/shard_map/while/body/eval_jaxpr/all_gather | solution.py:53
  1233.5 35.9 %all_gather.20 = bf16[64,6144]{1,0:T(8,128)(2,1)S(1)} all-gather(bf16[64,768]{1,0:T(8,128)(2,1)S(1)} %bitcast_select_fusion.4), channel_id=1, replica_groups=mesh['section'=16,'tensor'=8] {'tensor'}, dimensions={1}, use_global_device_ids=true | all-gather | bytes 884736 | tf_op jit(solution)/shard_map/while/body/eval_jaxpr/all_gather | solution.py:53
  1276.2 29.8 %all_gather.21 = bf16[64,1024]{1,0:T(8,128)(2,1)S(1)} all-gather(bf16[64,128]{1,0:T(8,128)(2,1)S(1)} %fusion.61), channel_id=1, replica_groups=mesh['section'=16,'tensor'=8] {'tensor'}, dimensions={1}, use_global_device_ids=true | all-gather | bytes 147456 | tf_op jit(solution)/shard_map/while/body/eval_jaxpr/all_gather | solution.py:62
  (139 shorter events, 291.6 us)
Async XLA Ops:
  0.6 2.4 copy-start
  3.0 2.4 copy-start.1
  3.0 2.4 copy-start.3
  79.7 3.5 collective-permute-start
  156.1 3.5 collective-permute-start
  232.7 3.5 collective-permute-start
  308.9 3.5 collective-permute-start
  385.2 3.5 collective-permute-start
  461.7 3.5 collective-permute-start
  537.9 3.5 collective-permute-start
  614.4 3.5 collective-permute-start
  690.9 3.5 collective-permute-start
  767.5 3.5 collective-permute-start
  844.2 3.5 collective-permute-start
  921.0 3.5 collective-permute-start
  997.7 3.8 collective-permute-start
  1074.7 3.9 collective-permute-start
  1151.7 4.9 collective-permute-start
  1229.8 3.7 collective-permute-start
  1306.6 4.1 collective-permute-start
  1310.7 8.0 copy-start.2
where the time goes:
time: 1330 us; the launch traced here: 1320 us
  blocking collectives  1120 us (84%)
  matrix products  137 us (10%)
  other arithmetic  37.9 us (3%)
  starting transfers between devices  22 us (2%)
    all_gather x17, blocking collectives, advance(): grad_full = lax.all_gather(grad_rows, 'tensor', axis=1, tiled=True)  608 us
    all_gather x17, blocking collectives, advance(): every_head = lax.all_gather(value_grad, 'tensor', axis=1, tiled=True)  507 us
    dot_general x17, matrix products, advance(): lax.dot_general(grad_full, out_mat, (((1,), (1,)), ((), ())), preferred_e...  113 us
    select_n x17, other arithmetic, advance(): jnp.where(active, lax.dynamic_update_index_in_dim(saved, grad_full, slot_...  37.6 us
  transfers between devices with their start and end apart: 17, of which 5 were waited for; matrix products, arithmetic and copies ran while one was open for 3% of the time, Pallas kernels for 0%

commit v1 on v0

v1 whole, which is shorter than its diff:
```python
import math

import jax
import jax.numpy as jnp
from jax import lax
from jax.sharding import PartitionSpec as P


def causal_probs(query_heads, key_rows):
    head_size = key_rows.shape[-1]
    length = key_rows.shape[0]
    logits = jnp.einsum("qgd,pd->gqp", query_heads, key_rows, preferred_element_type=jnp.float32)
    logits = logits * (1.0 / math.sqrt(head_size))
    row_pos = lax.broadcasted_iota(jnp.int32, (length, length), 0)
    col_pos = lax.broadcasted_iota(jnp.int32, (length, length), 1)
    logits = jnp.where(col_pos <= row_pos, logits, -jnp.inf)
    return jax.nn.softmax(logits, axis=-1).astype(jnp.bfloat16)


def shift(value, axis, by):
    length = lax.axis_size(axis)
    return lax.ppermute(value, axis, [(i, (i + by) % length) for i in range(length)])


def blocks_of_all(value):
    copies = jnp.broadcast_to(value[None], (lax.axis_size("tensor"),) + value.shape)
    return lax.all_to_all(copies, "tensor", 0, 0)


def side_by_side(blocks):
    count, rows, columns = blocks.shape
    return blocks.transpose(1, 0, 2).reshape(rows, count * columns)


def gather_rows(value):
    count = lax.axis_size("tensor")
    me = lax.axis_index("tensor")
    out = jnp.zeros((count,) + value.shape, value.dtype)
    out = lax.dynamic_update_index_in_dim(out, value, me, 0)
    for by in range(1, count):
        got = shift(value, "tensor", by)
        out = lax.dynamic_update_index_in_dim(out, got, (me - by) % count, 0)
    return out.reshape(count * value.shape[0], value.shape[1])


def on_device(grad_top, query, keys, values, out_weight, value_weight):
    sections = lax.axis_size("section")
    place = lax.axis_index("section")
    me = lax.axis_index("tensor")
    micro_batch, length = query.shape[1], query.shape[2]
    rows = micro_batch * length
    head_size = keys.shape[3]
    group = query.shape[3] // head_size
    feat_local = grad_top.shape[2]
    query_heads = query[0].reshape(micro_batch, length, group, head_size)
    probs = jax.vmap(causal_probs)(query_heads, keys[0])
    mixed = jnp.einsum("mgqp,mpd->mqgd", probs, values[0], preferred_element_type=jnp.float32)
    mixed = mixed.astype(jnp.bfloat16).reshape(rows, group * head_size)
    out_mat = out_weight[0]
    value_full = gather_rows(shift(value_weight[0], "section", -1))
    incoming = side_by_side(blocks_of_all(grad_top.reshape(rows, feat_local)))
    saved = incoming
    for turn in range(sections):
        if turn:
            saved = jnp.where(turn == sections - 1 - place, incoming, saved)
        attn_grad = lax.dot_general(
            incoming, out_mat, (((1,), (1,)), ((), ())), preferred_element_type=jnp.float32
        )
        attn_grad = attn_grad.astype(jnp.bfloat16).reshape(micro_batch, length, group, head_size)
        value_grad = jnp.einsum(
            "mgqp,mqgd->mpd", probs, attn_grad, preferred_element_type=jnp.float32
        ).astype(jnp.bfloat16)
        moved = shift(value_grad.reshape(rows, head_size), "section", -1)
        incoming = shift(incoming, "section", -1)
        every_head = side_by_side(blocks_of_all(moved))
        branch = lax.dot_general(
            every_head, value_full, (((1,), (1,)), ((), ())), preferred_element_type=jnp.float32
        )
        incoming = (incoming.astype(jnp.float32) + branch).astype(jnp.bfloat16)
    weight_grad = lax.dot_general(
        mixed, saved, (((0,), (0,)), ((), ())), preferred_element_type=jnp.float32
    ).astype(jnp.bfloat16)
    final = jnp.where(place == sections - 1, incoming, saved)
    grads = shift(lax.dynamic_slice_in_dim(final, me * feat_local, feat_local, 1), "section", 1)
    return (grads.reshape(1, micro_batch, length, feat_local), weight_grad[None])


def solution(mesh):
    placed = (
        P(None, None, "tensor"),
        P("section", None, None, "tensor"),
        P("section", None, None, "tensor"),
        P("section", None, None, "tensor"),
        P("section", "tensor", None),
        P("section", "tensor", None),
    )
    return jax.shard_map(
        on_device,
        mesh=mesh,
        in_specs=placed,
        out_specs=(P("section", None, None, "tensor"), P("section", "tensor", None)),
        check_vma=False,
    )
```

time: 1330 us -> 935 us (0.70)
  the two profiles are of different devices: /device:TPU:0 before, /device:TPU:32 now
where the time goes in v1:
time: 935 us; the launch traced here: 927 us
  matrix products  312 us (33%)
  waiting for transfers between devices  204 us (22%)
  starting transfers between devices  199 us (21%)
  blocking collectives  150 us (16%)
  local copies, waits for them, and re-layouts  60.7 us (6%)
    ppermute x41, waiting for transfers between devices, shift(): lax.ppermute(value, axis, [(i, (i + by) % length) for i in range(length)])  187 us
    ppermute x41, starting transfers between devices, shift(): lax.ppermute(value, axis, [(i, (i + by) % length) for i in range(length)])  179 us
    dot_general x16, matrix products, on_device(): lax.dot_general(every_head, value_full, (((1,), (1,)), ((), ())), preferr...  163 us
    all_to_all x13, blocking collectives, blocks_of_all(): return lax.all_to_all(copies, 'tensor', 0, 0)  150 us
    dot_general x16, matrix products, on_device(): lax.dot_general(incoming, out_mat, (((1,), (1,)), ((), ())), preferred_el...  127 us
    reshape x16, local copies, waits for them, and re-layouts, on_device(): attn_grad.astype(jnp.bfloat16)  26.6 us
    all_to_all x4, starting transfers between devices, blocks_of_all(): return lax.all_to_all(copies, 'tensor', 0, 0)  19.9 us
  transfers between devices with their start and end apart: 45, of which 23 were waited for; matrix products, arithmetic and copies ran while one was open for 23% of the time, Pallas kernels for 0%

profile of v1, /device:TPU:32, one launch (start us, length us, event | category | flops | bytes accessed | tf_op | source)
XLA Modules:
  0.0 927.1 jit_solution(16553692028636180767)
XLA Ops:
  11.9 12.8 %collective-permute-done.2 = bf16[768,1024]{1,0:T(8,128)(2,1)} collective-permute-done((bf16[768,1024]{1,0:T(8,128)(2,1)}, bf16[768,1024]{1,0:T(8,128)(2,1)}, u32[]{:S(2)}, u32[]{:S(2)}) %collective-permute-start.2) | collective-permute-done | bytes 1572896 | tf_op jit(solution)/shard_map/ppermute | solution.py:22
  24.9 10.4 %collective-permute-start.4 = (bf16[768,1024]{1,0:T(8,128)(2,1)}, bf16[768,1024]{1,0:T(8,128)(2,1)}, u32[]{:S(2)}, u32[]{:S(2)}) collective-permute-start(bf16[768,1024]{1,0:T(8,128)(2,1)} %collective-permute-done.2), channel_id=1, source_target_pairs={{0,2},{1,3},{2,4},{3,5},{4,6},{5,7},{6,0},{7,1},{8,10},{9,11},{10,... | collective-permute-start | bytes 4718600 | tf_op jit(solution)/shard_map/ppermute | solution.py:22
  49.1 72.0 %collective-permute-start.1 = (bf16[128,128]{1,0:T(8,128)(2,1)S(1)}, bf16[128,128]{1,0:T(8,128)(2,1)S(1)}, u32[]{:S(2)}, u32[]{:S(2)}) collective-permute-start(bf16[128,128]{1,0:T(8,128)(2,1)S(1)} %bitcast.377), channel_id=1, source_target_pairs={{0,120},{8,0},{16,8},{24,16},{32,24},{40,32},{48,40},{56,48},{64,5... | collective-permute-start | bytes 98312 | tf_op jit(solution)/shard_map/ppermute | solution.py:22
  159.3 10.5 %collective-permute-done.6 = bf16[768,1024]{1,0:T(8,128)(2,1)} collective-permute-done((bf16[768,1024]{1,0:T(8,128)(2,1)}, bf16[768,1024]{1,0:T(8,128)(2,1)}, u32[]{:S(2)}, u32[]{:S(2)}) %collective-permute-start.6) | collective-permute-done | bytes 1572896 | tf_op jit(solution)/shard_map/ppermute | solution.py:22
  175.2 23.7 %collective-permute-done.8 = bf16[768,1024]{1,0:T(8,128)(2,1)S(1)} collective-permute-done((bf16[768,1024]{1,0:T(8,128)(2,1)}, bf16[768,1024]{1,0:T(8,128)(2,1)S(1)}, u32[]{:S(2)}, u32[]{:S(2)}) %collective-permute-start.8) | collective-permute-done | bytes 1572896 | tf_op jit(solution)/shard_map/ppermute | solution.py:22
  200.2 11.9 %collective-permute-done.9 = bf16[768,1024]{1,0:T(8,128)(2,1)S(1)} collective-permute-done((bf16[768,1024]{1,0:T(8,128)(2,1)}, bf16[768,1024]{1,0:T(8,128)(2,1)S(1)}, u32[]{:S(2)}, u32[]{:S(2)}) %collective-permute-start.9) | collective-permute-done | bytes 1572896 | tf_op jit(solution)/shard_map/ppermute | solution.py:22
  222.2 23.7 %collective-permute-start.10 = (bf16[128,6144]{1,0:T(8,128)(2,1)S(1)}, bf16[128,6144]{1,0:T(8,128)(2,1)S(1)}, u32[]{:S(2)}, u32[]{:S(2)}) collective-permute-start(bf16[128,6144]{1,0:T(8,128)(2,1)S(1)} %fusion.34), channel_id=1, source_target_pairs={{0,120},{8,0},{16,8},{24,16},{32,24},{40,32},{48,40},{56,48},{64,5... | collective-permute-start | bytes 4718600 | tf_op jit(solution)/shard_map/ppermute | solution.py:22
  264.3 14.1 %all_to_all.85 = bf16[8,128,128]{1,2,0:T(8,128)(2,1)S(1)} all-to-all(bf16[8,128,128]{1,2,0:T(8,128)(2,1)S(1)} %broadcast_in_dim.158), channel_id=1, replica_groups=mesh['section'=16,'tensor'=8] {'tensor'}, dimensions={0} | all-to-all | bytes 524288 | tf_op jit(solution)/shard_map/all_to_all | solution.py:27
  310.7 11.2 %all_to_all.86 = bf16[8,128,128]{1,2,0:T(8,128)(2,1)S(1)} all-to-all(bf16[8,128,128]{1,2,0:T(8,128)(2,1)S(1)} %broadcast_in_dim.159), channel_id=1, replica_groups=mesh['section'=16,'tensor'=8] {'tensor'}, dimensions={0} | all-to-all | bytes 524288 | tf_op jit(solution)/shard_map/all_to_all | solution.py:27
  321.9 10.4 %fusion.36 = bf16[128,6144]{1,0:T(8,128)(2,1)} fusion(bf16[128,1024]{0,1:T(8,128)(2,1)S(1)} %bitcast.360, bf16[6144,1024]{1,0:T(8,128)(2,1)} %bitcast.339, bf16[128,6144]{1,0:T(8,128)(2,1)} %collective-permute-done.12), kind=kOutput, calls=%fused_computation.52 | convolution fusion | flops 1612972032 | bytes 15990784 | tf_op jit(solution)/shard_map/dot_general | solution.py:76
  354.0 11.4 %all_to_all.87 = bf16[8,128,128]{1,2,0:T(8,128)(2,1)S(1)} all-to-all(bf16[8,128,128]{1,2,0:T(8,128)(2,1)S(1)} %broadcast_in_dim.160), channel_id=1, replica_groups=mesh['section'=16,'tensor'=8] {'tensor'}, dimensions={0} | all-to-all | bytes 524288 | tf_op jit(solution)/shard_map/all_to_all | solution.py:27
  365.4 10.4 %fusion.37 = bf16[128,6144]{1,0:T(8,128)(2,1)} fusion(bf16[128,1024]{0,1:T(8,128)(2,1)S(1)} %bitcast.361, bf16[6144,1024]{1,0:T(8,128)(2,1)} %bitcast.340, bf16[128,6144]{1,0:T(8,128)(2,1)} %collective-permute-done.14), kind=kOutput, calls=%fused_computation.53 | convolution fusion | flops 1612972032 | bytes 15990784 | tf_op jit(solution)/shard_map/dot_general | solution.py:76
  397.8 11.2 %all_to_all.88 = bf16[8,128,128]{1,2,0:T(8,128)(2,1)S(1)} all-to-all(bf16[8,128,128]{1,2,0:T(8,128)(2,1)S(1)} %broadcast_in_dim.161), channel_id=1, replica_groups=mesh['section'=16,'tensor'=8] {'tensor'}, dimensions={0} | all-to-all | bytes 524288 | tf_op jit(solution)/shard_map/all_to_all | solution.py:27
  409.0 10.4 %fusion.38 = bf16[128,6144]{1,0:T(8,128)(2,1)} fusion(bf16[128,1024]{0,1:T(8,128)(2,1)S(1)} %bitcast.362, bf16[6144,1024]{1,0:T(8,128)(2,1)} %bitcast.341, bf16[128,6144]{1,0:T(8,128)(2,1)} %collective-permute-done.16), kind=kOutput, calls=%fused_computation.54 | convolution fusion | flops 1612972032 | bytes 15990784 | tf_op jit(solution)/shard_map/dot_general | solution.py:76
  443.4 11.2 %all_to_all.89 = bf16[8,128,128]{1,2,0:T(8,128)(2,1)S(1)} all-to-all(bf16[8,128,128]{1,2,0:T(8,128)(2,1)S(1)} %broadcast_in_dim.162), channel_id=1, replica_groups=mesh['section'=16,'tensor'=8] {'tensor'}, dimensions={0} | all-to-all | bytes 524288 | tf_op jit(solution)/shard_map/all_to_all | solution.py:27
  487.7 11.4 %all_to_all.90 = bf16[8,128,128]{1,2,0:T(8,128)(2,1)S(1)} all-to-all(bf16[8,128,128]{1,2,0:T(8,128)(2,1)S(1)} %broadcast_in_dim.163), channel_id=1, replica_groups=mesh['section'=16,'tensor'=8] {'tensor'}, dimensions={0} | all-to-all | bytes 524288 | tf_op jit(solution)/shard_map/all_to_all | solution.py:27
  499.1 10.4 %fusion.40 = bf16[128,6144]{1,0:T(8,128)(2,1)} fusion(bf16[128,1024]{0,1:T(8,128)(2,1)S(1)} %bitcast.364, bf16[6144,1024]{1,0:T(8,128)(2,1)} %bitcast.343, bf16[128,6144]{1,0:T(8,128)(2,1)} %collective-permute-done.20), kind=kOutput, calls=%fused_computation.56 | convolution fusion | flops 1612972032 | bytes 15990784 | tf_op jit(solution)/shard_map/dot_general | solution.py:76
  532.3 11.2 %all_to_all.91 = bf16[8,128,128]{1,2,0:T(8,128)(2,1)S(1)} all-to-all(bf16[8,128,128]{1,2,0:T(8,128)(2,1)S(1)} %broadcast_in_dim.164), channel_id=1, replica_groups=mesh['section'=16,'tensor'=8] {'tensor'}, dimensions={0} | all-to-all | bytes 524288 | tf_op jit(solution)/shard_map/all_to_all | solution.py:27
  543.5 10.5 %fusion.41 = bf16[128,6144]{1,0:T(8,128)(2,1)} fusion(bf16[128,1024]{0,1:T(8,128)(2,1)S(1)} %bitcast.365, bf16[6144,1024]{1,0:T(8,128)(2,1)} %bitcast.344, bf16[128,6144]{1,0:T(8,128)(2,1)} %collective-permute-done.22), kind=kOutput, calls=%fused_computation.57 | convolution fusion | flops 1612972032 | bytes 15990784 | tf_op jit(solution)/shard_map/dot_general | solution.py:76
  576.8 11.2 %all_to_all.92 = bf16[8,128,128]{1,2,0:T(8,128)(2,1)S(1)} all-to-all(bf16[8,128,128]{1,2,0:T(8,128)(2,1)S(1)} %broadcast_in_dim.165), channel_id=1, replica_groups=mesh['section'=16,'tensor'=8] {'tensor'}, dimensions={0} | all-to-all | bytes 524288 | tf_op jit(solution)/shard_map/all_to_all | solution.py:27
  588.0 10.5 %fusion.42 = bf16[128,6144]{1,0:T(8,128)(2,1)} fusion(bf16[128,1024]{0,1:T(8,128)(2,1)S(1)} %bitcast.366, bf16[6144,1024]{1,0:T(8,128)(2,1)} %bitcast.345, bf16[128,6144]{1,0:T(8,128)(2,1)} %collective-permute-done.24), kind=kOutput, calls=%fused_computation.58 | convolution fusion | flops 1612972032 | bytes 15990784 | tf_op jit(solution)/shard_map/dot_general | solution.py:76
  621.3 11.6 %all_to_all.93 = bf16[8,128,128]{1,2,0:T(8,128)(2,1)S(1)} all-to-all(bf16[8,128,128]{1,2,0:T(8,128)(2,1)S(1)} %broadcast_in_dim.166), channel_id=1, replica_groups=mesh['section'=16,'tensor'=8] {'tensor'}, dimensions={0} | all-to-all | bytes 524288 | tf_op jit(solution)/shard_map/all_to_all | solution.py:27
  633.0 10.5 %fusion.43 = bf16[128,6144]{1,0:T(8,128)(2,1)} fusion(bf16[128,1024]{0,1:T(8,128)(2,1)S(1)} %bitcast.367, bf16[6144,1024]{1,0:T(8,128)(2,1)} %bitcast.346, bf16[128,6144]{1,0:T(8,128)(2,1)} %collective-permute-done.26), kind=kOutput, calls=%fused_computation.59 | convolution fusion | flops 1612972032 | bytes 15990784 | tf_op jit(solution)/shard_map/dot_general | solution.py:76
  666.6 11.2 %all_to_all.94 = bf16[8,128,128]{1,2,0:T(8,128)(2,1)S(1)} all-to-all(bf16[8,128,128]{1,2,0:T(8,128)(2,1)S(1)} %broadcast_in_dim.167), channel_id=1, replica_groups=mesh['section'=16,'tensor'=8] {'tensor'}, dimensions={0} | all-to-all | bytes 524288 | tf_op jit(solution)/shard_map/all_to_all | solution.py:27
  677.8 10.4 %fusion.44 = bf16[128,6144]{1,0:T(8,128)(2,1)} fusion(bf16[128,1024]{0,1:T(8,128)(2,1)S(1)} %bitcast.368, bf16[6144,1024]{1,0:T(8,128)(2,1)} %bitcast.347, bf16[128,6144]{1,0:T(8,128)(2,1)} %collective-permute-done.28), kind=kOutput, calls=%fused_computation.60 | convolution fusion | flops 1612972032 | bytes 15990784 | tf_op jit(solution)/shard_map/dot_general | solution.py:76
  712.4 11.2 %all_to_all.95 = bf16[8,128,128]{1,2,0:T(8,128)(2,1)S(1)} all-to-all(bf16[8,128,128]{1,2,0:T(8,128)(2,1)S(1)} %broadcast_in_dim.168), channel_id=1, replica_groups=mesh['section'=16,'tensor'=8] {'tensor'}, dimensions={0} | all-to-all | bytes 524288 | tf_op jit(solution)/shard_map/all_to_all | solution.py:27
  723.6 10.4 %fusion.45 = bf16[128,6144]{1,0:T(8,128)(2,1)} fusion(bf16[128,1024]{0,1:T(8,128)(2,1)S(1)} %bitcast.369, bf16[6144,1024]{1,0:T(8,128)(2,1)} %bitcast.348, bf16[128,6144]{1,0:T(8,128)(2,1)} %collective-permute-done.30), kind=kOutput, calls=%fused_computation.61 | convolution fusion | flops 1612972032 | bytes 15990784 | tf_op jit(solution)/shard_map/dot_general | solution.py:76
  757.5 11.4 %all_to_all.96 = bf16[8,128,128]{1,2,0:T(8,128)(2,1)S(1)} all-to-all(bf16[8,128,128]{1,2,0:T(8,128)(2,1)S(1)} %broadcast_in_dim.169), channel_id=1, replica_groups=mesh['section'=16,'tensor'=8] {'tensor'}, dimensions={0} | all-to-all | bytes 524288 | tf_op jit(solution)/shard_map/all_to_all | solution.py:27
  768.9 10.5 %fusion.46 = bf16[128,6144]{1,0:T(8,128)(2,1)} fusion(bf16[128,1024]{0,1:T(8,128)(2,1)S(1)} %bitcast.370, bf16[6144,1024]{1,0:T(8,128)(2,1)} %bitcast.349, bf16[128,6144]{1,0:T(8,128)(2,1)} %collective-permute-done.32), kind=kOutput, calls=%fused_computation.62 | convolution fusion | flops 1612972032 | bytes 15990784 | tf_op jit(solution)/shard_map/dot_general | solution.py:76
  803.5 11.2 %all_to_all.97 = bf16[8,128,128]{1,2,0:T(8,128)(2,1)S(1)} all-to-all(bf16[8,128,128]{1,2,0:T(8,128)(2,1)S(1)} %broadcast_in_dim.170), channel_id=1, replica_groups=mesh['section'=16,'tensor'=8] {'tensor'}, dimensions={0} | all-to-all | bytes 524288 | tf_op jit(solution)/shard_map/all_to_all | solution.py:27
  814.7 10.4 %fusion.47 = bf16[128,6144]{1,0:T(8,128)(2,1)} fusion(bf16[128,1024]{0,1:T(8,128)(2,1)S(1)} %bitcast.371, bf16[6144,1024]{1,0:T(8,128)(2,1)} %bitcast.350, bf16[128,6144]{1,0:T(8,128)(2,1)} %collective-permute-done.34), kind=kOutput, calls=%fused_computation.63 | convolution fusion | flops 1612972032 | bytes 15990784 | tf_op jit(solution)/shard_map/dot_general | solution.py:76
  884.3 12.0 %collective-permute-done.39 = bf16[128,128]{1,0:T(8,128)(2,1)S(1)} collective-permute-done((bf16[128,128]{1,0:T(8,128)(2,1)S(1)}, bf16[128,128]{1,0:T(8,128)(2,1)S(1)}, u32[]{:S(2)}, u32[]{:S(2)}) %collective-permute-start.39) | collective-permute-done | bytes 32800 | tf_op jit(solution)/shard_map/ppermute | solution.py:22
  (203 shorter events, 484.0 us)
Async XLA Ops:
  0.7 24.0 %collective-permute-start.2 = (bf16[768,1024]{1,0:T(8,128)(2,1)}, bf16[768,1024]{1,0:T(8,128)(2,1)}, u32[]{:S(2)}, u32[]{:S(2)}) collective-permute-start(bf16[768,1024]{1,0:T(8,128)(2,1)} %bitcast.375), channel_id=1, source_target_pairs={{0,120},{8,0},{16,8},{24,16},{32,24},{40,32},{48,40},{56,48},{64,5... | collective-permute-start | bytes 4718600 | tf_op jit(solution)/shard_map/ppermute | solution.py:22
  4.9 30.9 %all-to-all-start = ((bf16[8,128,768]{2,1,0:T(8,128)(2,1)}), bf16[8,128,768]{2,1,0:T(8,128)(2,1)S(1)}, u32[]{:S(2)}, u32[]{:S(2)}) async-start(bf16[8,128,768]{2,1,0:T(8,128)(2,1)} %broadcast_in_dim.74), calls=%async_computation | async-start | bytes 3145728 | tf_op jit(solution)/shard_map/all_to_all | solution.py:27
  24.7 107.0 %collective-permute-start.3 = (bf16[768,1024]{1,0:T(8,128)(2,1)}, bf16[768,1024]{1,0:T(8,128)(2,1)}, u32[]{:S(2)}, u32[]{:S(2)}) collective-permute-start(bf16[768,1024]{1,0:T(8,128)(2,1)} %collective-permute-done.2), channel_id=1, source_target_pairs={{0,1},{1,2},{2,3},{3,4},{4,5},{5,6},{6,7},{7,0},{8,9},{9,10},{10,1... | collective-permute-start | bytes 4718600 | tf_op jit(solution)/shard_map/ppermute | solution.py:22
  24.9 121.6 %collective-permute-start.4 = (bf16[768,1024]{1,0:T(8,128)(2,1)}, bf16[768,1024]{1,0:T(8,128)(2,1)}, u32[]{:S(2)}, u32[]{:S(2)}) collective-permute-start(bf16[768,1024]{1,0:T(8,128)(2,1)} %collective-permute-done.2), channel_id=1, source_target_pairs={{0,2},{1,3},{2,4},{3,5},{4,6},{5,7},{6,0},{7,1},{8,10},{9,11},{10,... | collective-permute-start | bytes 4718600 | tf_op jit(solution)/shard_map/ppermute | solution.py:22
  36.0 114.6 %collective-permute-start.5 = (bf16[768,1024]{1,0:T(8,128)(2,1)}, bf16[768,1024]{1,0:T(8,128)(2,1)}, u32[]{:S(2)}, u32[]{:S(2)}) collective-permute-start(bf16[768,1024]{1,0:T(8,128)(2,1)} %collective-permute-done.2), channel_id=1, source_target_pairs={{0,3},{1,4},{2,5},{3,6},{4,7},{5,0},{6,1},{7,2},{8,11},{9,12},{10,... | collective-permute-start | bytes 4718600 | tf_op jit(solution)/shard_map/ppermute | solution.py:22
  41.5 128.3 %collective-permute-start.6 = (bf16[768,1024]{1,0:T(8,128)(2,1)}, bf16[768,1024]{1,0:T(8,128)(2,1)}, u32[]{:S(2)}, u32[]{:S(2)}) collective-permute-start(bf16[768,1024]{1,0:T(8,128)(2,1)} %collective-permute-done.2), channel_id=1, source_target_pairs={{0,4},{1,5},{2,6},{3,7},{4,0},{5,1},{6,2},{7,3},{8,12},{9,13},{10,... | collective-permute-start | bytes 4718600 | tf_op jit(solution)/shard_map/ppermute | solution.py:22
  49.1 73.6 %collective-permute-start.1 = (bf16[128,128]{1,0:T(8,128)(2,1)S(1)}, bf16[128,128]{1,0:T(8,128)(2,1)S(1)}, u32[]{:S(2)}, u32[]{:S(2)}) collective-permute-start(bf16[128,128]{1,0:T(8,128)(2,1)S(1)} %bitcast.377), channel_id=1, source_target_pairs={{0,120},{8,0},{16,8},{24,16},{32,24},{40,32},{48,40},{56,48},{64,5... | collective-permute-start | bytes 98312 | tf_op jit(solution)/shard_map/ppermute | solution.py:22
  122.7 49.9 %collective-permute-start.7 = (bf16[768,1024]{1,0:T(8,128)(2,1)}, bf16[768,1024]{1,0:T(8,128)(2,1)}, u32[]{:S(2)}, u32[]{:S(2)}) collective-permute-start(bf16[768,1024]{1,0:T(8,128)(2,1)} %collective-permute-done.2), channel_id=1, source_target_pairs={{0,5},{1,6},{2,7},{3,0},{4,1},{5,2},{6,3},{7,4},{8,13},{9,14},{10,... | collective-permute-start | bytes 4718600 | tf_op jit(solution)/shard_map/ppermute | solution.py:22
  126.6 86.8 %all-to-all-start.1 = ((bf16[8,128,128]{1,2,0:T(8,128)(2,1)}), bf16[8,128,128]{1,2,0:T(8,128)(2,1)S(1)}, u32[]{:S(2)}, u32[]{:S(2)}) async-start(bf16[8,128,128]{1,2,0:T(8,128)(2,1)} %broadcast_in_dim.148), calls=%async_computation.1 | async-start | bytes 524288 | tf_op jit(solution)/shard_map/all_to_all | solution.py:27
  131.7 67.2 %collective-permute-start.8 = (bf16[768,1024]{1,0:T(8,128)(2,1)}, bf16[768,1024]{1,0:T(8,128)(2,1)S(1)}, u32[]{:S(2)}, u32[]{:S(2)}) collective-permute-start(bf16[768,1024]{1,0:T(8,128)(2,1)} %collective-permute-done.2), channel_id=1, source_target_pairs={{0,6},{1,7},{2,0},{3,1},{4,2},{5,3},{6,4},{7,5},{8,14},{9,15},{10,... | collective-permute-start | bytes 4718600 | tf_op jit(solution)/shard_map/ppermute | solution.py:22
  146.5 65.6 %collective-permute-start.9 = (bf16[768,1024]{1,0:T(8,128)(2,1)}, bf16[768,1024]{1,0:T(8,128)(2,1)S(1)}, u32[]{:S(2)}, u32[]{:S(2)}) collective-permute-start(bf16[768,1024]{1,0:T(8,128)(2,1)} %collective-permute-done.2), channel_id=1, source_target_pairs={{0,7},{1,0},{2,1},{3,2},{4,3},{5,4},{6,5},{7,6},{8,15},{9,8},{10,9... | collective-permute-start | bytes 4718600 | tf_op jit(solution)/shard_map/ppermute | solution.py:22
  150.6 62.8 %collective-permute-start = (bf16[128,6144]{1,0:T(8,128)(2,1)S(1)}, bf16[128,6144]{1,0:T(8,128)(2,1)S(1)}, u32[]{:S(2)}, u32[]{:S(2)}) collective-permute-start(bf16[128,6144]{1,0:T(8,128)(2,1)S(1)} %bitcast.355), channel_id=1, source_target_pairs={{0,120},{8,0},{16,8},{24,16},{32,24},{40,32},{48,40},{56,48},{64,5... | collective-permute-start | bytes 4718600 | tf_op jit(solution)/shard_map/ppermute | solution.py:22
  222.2 56.2 %collective-permute-start.10 = (bf16[128,6144]{1,0:T(8,128)(2,1)S(1)}, bf16[128,6144]{1,0:T(8,128)(2,1)S(1)}, u32[]{:S(2)}, u32[]{:S(2)}) collective-permute-start(bf16[128,6144]{1,0:T(8,128)(2,1)S(1)} %fusion.34), channel_id=1, source_target_pairs={{0,120},{8,0},{16,8},{24,16},{32,24},{40,32},{48,40},{56,48},{64,5... | collective-permute-start | bytes 4718600 | tf_op jit(solution)/shard_map/ppermute | solution.py:22
  288.9 33.1 %collective-permute-start.12 = (bf16[128,6144]{1,0:T(8,128)(2,1)S(1)}, bf16[128,6144]{1,0:T(8,128)(2,1)}, u32[]{:S(2)}, u32[]{:S(2)}) collective-permute-start(bf16[128,6144]{1,0:T(8,128)(2,1)S(1)} %fusion.35), channel_id=1, source_target_pairs={{0,120},{8,0},{16,8},{24,16},{32,24},{40,32},{48,40},{56,48},{64,5... | collective-permute-start | bytes 4718600 | tf_op jit(solution)/shard_map/ppermute | solution.py:22
  332.4 33.1 %collective-permute-start.14 = (bf16[128,6144]{1,0:T(8,128)(2,1)}, bf16[128,6144]{1,0:T(8,128)(2,1)}, u32[]{:S(2)}, u32[]{:S(2)}) collective-permute-start(bf16[128,6144]{1,0:T(8,128)(2,1)} %fusion.36), channel_id=1, source_target_pairs={{0,120},{8,0},{16,8},{24,16},{32,24},{40,32},{48,40},{56,48},{64,5... | collective-permute-start | bytes 4718600 | tf_op jit(solution)/shard_map/ppermute | solution.py:22
  375.9 33.1 %collective-permute-start.16 = (bf16[128,6144]{1,0:T(8,128)(2,1)}, bf16[128,6144]{1,0:T(8,128)(2,1)}, u32[]{:S(2)}, u32[]{:S(2)}) collective-permute-start(bf16[128,6144]{1,0:T(8,128)(2,1)} %fusion.37), channel_id=1, source_target_pairs={{0,120},{8,0},{16,8},{24,16},{32,24},{40,32},{48,40},{56,48},{64,5... | collective-permute-start | bytes 4718600 | tf_op jit(solution)/shard_map/ppermute | solution.py:22
  419.4 35.2 %collective-permute-start.18 = (bf16[128,6144]{1,0:T(8,128)(2,1)}, bf16[128,6144]{1,0:T(8,128)(2,1)}, u32[]{:S(2)}, u32[]{:S(2)}) collective-permute-start(bf16[128,6144]{1,0:T(8,128)(2,1)} %fusion.38), channel_id=1, source_target_pairs={{0,120},{8,0},{16,8},{24,16},{32,24},{40,32},{48,40},{56,48},{64,5... | collective-permute-start | bytes 4718600 | tf_op jit(solution)/shard_map/ppermute | solution.py:22
  465.0 34.1 %collective-permute-start.20 = (bf16[128,6144]{1,0:T(8,128)(2,1)}, bf16[128,6144]{1,0:T(8,128)(2,1)}, u32[]{:S(2)}, u32[]{:S(2)}) collective-permute-start(bf16[128,6144]{1,0:T(8,128)(2,1)} %fusion.39), channel_id=1, source_target_pairs={{0,120},{8,0},{16,8},{24,16},{32,24},{40,32},{48,40},{56,48},{64,5... | collective-permute-start | bytes 4718600 | tf_op jit(solution)/shard_map/ppermute | solution.py:22
  509.5 33.9 %collective-permute-start.22 = (bf16[128,6144]{1,0:T(8,128)(2,1)}, bf16[128,6144]{1,0:T(8,128)(2,1)}, u32[]{:S(2)}, u32[]{:S(2)}) collective-permute-start(bf16[128,6144]{1,0:T(8,128)(2,1)} %fusion.40), channel_id=1, source_target_pairs={{0,120},{8,0},{16,8},{24,16},{32,24},{40,32},{48,40},{56,48},{64,5... | collective-permute-start | bytes 4718600 | tf_op jit(solution)/shard_map/ppermute | solution.py:22
  553.9 34.1 %collective-permute-start.24 = (bf16[128,6144]{1,0:T(8,128)(2,1)}, bf16[128,6144]{1,0:T(8,128)(2,1)}, u32[]{:S(2)}, u32[]{:S(2)}) collective-permute-start(bf16[128,6144]{1,0:T(8,128)(2,1)} %fusion.41), channel_id=1, source_target_pairs={{0,120},{8,0},{16,8},{24,16},{32,24},{40,32},{48,40},{56,48},{64,5... | collective-permute-start | bytes 4718600 | tf_op jit(solution)/shard_map/ppermute | solution.py:22
  598.5 34.5 %collective-permute-start.26 = (bf16[128,6144]{1,0:T(8,128)(2,1)}, bf16[128,6144]{1,0:T(8,128)(2,1)}, u32[]{:S(2)}, u32[]{:S(2)}) collective-permute-start(bf16[128,6144]{1,0:T(8,128)(2,1)} %fusion.42), channel_id=1, source_target_pairs={{0,120},{8,0},{16,8},{24,16},{32,24},{40,32},{48,40},{56,48},{64,5... | collective-permute-start | bytes 4718600 | tf_op jit(solution)/shard_map/ppermute | solution.py:22
  643.5 34.3 %collective-permute-start.28 = (bf16[128,6144]{1,0:T(8,128)(2,1)}, bf16[128,6144]{1,0:T(8,128)(2,1)}, u32[]{:S(2)}, u32[]{:S(2)}) collective-permute-start(bf16[128,6144]{1,0:T(8,128)(2,1)} %fusion.43), channel_id=1, source_target_pairs={{0,120},{8,0},{16,8},{24,16},{32,24},{40,32},{48,40},{56,48},{64,5... | collective-permute-start | bytes 4718600 | tf_op jit(solution)/shard_map/ppermute | solution.py:22
  688.2 35.3 %collective-permute-start.30 = (bf16[128,6144]{1,0:T(8,128)(2,1)}, bf16[128,6144]{1,0:T(8,128)(2,1)}, u32[]{:S(2)}, u32[]{:S(2)}) collective-permute-start(bf16[128,6144]{1,0:T(8,128)(2,1)} %fusion.44), channel_id=1, source_target_pairs={{0,120},{8,0},{16,8},{24,16},{32,24},{40,32},{48,40},{56,48},{64,5... | collective-permute-start | bytes 4718600 | tf_op jit(solution)/shard_map/ppermute | solution.py:22
  703.5 8.7 collective-permute-start.31
  734.0 34.9 %collective-permute-start.32 = (bf16[128,6144]{1,0:T(8,128)(2,1)}, bf16[128,6144]{1,0:T(8,128)(2,1)}, u32[]{:S(2)}, u32[]{:S(2)}) collective-permute-start(bf16[128,6144]{1,0:T(8,128)(2,1)} %fusion.45), channel_id=1, source_target_pairs={{0,120},{8,0},{16,8},{24,16},{32,24},{40,32},{48,40},{56,48},{64,5... | collective-permute-start | bytes 4718600 | tf_op jit(solution)/shard_map/ppermute | solution.py:22
  779.4 35.3 %collective-permute-start.34 = (bf16[128,6144]{1,0:T(8,128)(2,1)}, bf16[128,6144]{1,0:T(8,128)(2,1)}, u32[]{:S(2)}, u32[]{:S(2)}) collective-permute-start(bf16[128,6144]{1,0:T(8,128)(2,1)} %fusion.46), channel_id=1, source_target_pairs={{0,120},{8,0},{16,8},{24,16},{32,24},{40,32},{48,40},{56,48},{64,5... | collective-permute-start | bytes 4718600 | tf_op jit(solution)/shard_map/ppermute | solution.py:22
  794.6 8.8 collective-permute-start.35
  825.1 36.8 %collective-permute-start.36 = (bf16[128,6144]{1,0:T(8,128)(2,1)}, bf16[128,6144]{1,0:T(8,128)(2,1)}, u32[]{:S(2)}, u32[]{:S(2)}) collective-permute-start(bf16[128,6144]{1,0:T(8,128)(2,1)} %fusion.47), channel_id=1, source_target_pairs={{0,120},{8,0},{16,8},{24,16},{32,24},{40,32},{48,40},{56,48},{64,5... | collective-permute-start | bytes 4718600 | tf_op jit(solution)/shard_map/ppermute | solution.py:22
  849.1 12.9 %all-to-all-start.15 = ((bf16[8,128,128]{1,2,0:T(8,128)(2,1)}), bf16[8,128,128]{1,2,0:T(8,128)(2,1)}, u32[]{:S(2)}, u32[]{:S(2)}) async-start(bf16[8,128,128]{1,2,0:T(8,128)(2,1)} %broadcast_in_dim.171), calls=%async_computation.15 | async-start | bytes 524288 | tf_op jit(solution)/shard_map/all_to_all | solution.py:27
  872.2 46.4 %collective-permute-start.38 = (bf16[128,6144]{1,0:T(8,128)(2,1)}, bf16[128,6144]{1,0:T(8,128)(2,1)S(1)}, u32[]{:S(2)}, u32[]{:S(2)}) collective-permute-start(bf16[128,6144]{1,0:T(8,128)(2,1)} %get-tuple-element.5), channel_id=1, source_target_pairs={{0,120},{8,0},{16,8},{24,16},{32,24},{40,32},{48,40},{56,48},{64,5... | collective-permute-start | bytes 4718600 | tf_op jit(solution)/shard_map/ppermute | solution.py:22
  884.2 12.1 %collective-permute-start.39 = (bf16[128,128]{1,0:T(8,128)(2,1)S(1)}, bf16[128,128]{1,0:T(8,128)(2,1)S(1)}, u32[]{:S(2)}, u32[]{:S(2)}) collective-permute-start(bf16[128,128]{1,0:T(8,128)(2,1)S(1)} %bitcast.376), channel_id=1, source_target_pairs={{0,120},{8,0},{16,8},{24,16},{32,24},{40,32},{48,40},{56,48},{64,5... | collective-permute-start | bytes 98312 | tf_op jit(solution)/shard_map/ppermute | solution.py:22
  897.1 12.4 %all-to-all-start.16 = ((bf16[8,128,128]{1,2,0:T(8,128)(2,1)}), bf16[8,128,128]{1,2,0:T(8,128)(2,1)S(1)}, u32[]{:S(2)}, u32[]{:S(2)}) async-start(bf16[8,128,128]{1,2,0:T(8,128)(2,1)} %broadcast_in_dim.172), calls=%async_computation.16 | async-start | bytes 524288 | tf_op jit(solution)/shard_map/all_to_all | solution.py:27
  (21 other events, 1234.5 us)

commit v2 on v1

v2 whole, which is shorter than its diff:
```python
import functools
import math

import jax
import jax.numpy as jnp
from jax import lax
from jax.experimental import pallas as pl
from jax.experimental.pallas import tpu as pltpu
from jax.sharding import PartitionSpec as P

F32 = jnp.float32
BF16 = jnp.bfloat16
NN = (((1,), (0,)), ((), ()))
TN = (((0,), (0,)), ((), ()))


def causal_probs(query_heads, key_rows):
    head_size = key_rows.shape[-1]
    length = key_rows.shape[0]
    logits = jnp.einsum("qgd,pd->gqp", query_heads, key_rows, preferred_element_type=F32)
    logits = logits * (1.0 / math.sqrt(head_size))
    row_pos = lax.broadcasted_iota(jnp.int32, (length, length), 0)
    col_pos = lax.broadcasted_iota(jnp.int32, (length, length), 1)
    logits = jnp.where(col_pos <= row_pos, logits, -jnp.inf)
    return jax.nn.softmax(logits, axis=-1).astype(BF16)


def shift(value, axis, by):
    length = lax.axis_size(axis)
    return lax.ppermute(value, axis, [(i, (i + by) % length) for i in range(length)])


def blocks_of_all(value):
    copies = jnp.broadcast_to(value[None], (lax.axis_size("tensor"),) + value.shape)
    return lax.all_to_all(copies, "tensor", 0, 0)


def value_grad_of(total, probs_t_ref, value_ref):
    attn = total.astype(BF16)
    micro_batch, length, depth = probs_t_ref.shape
    head_size = value_ref.shape[1]
    for m in range(micro_batch):
        rows = slice(m * length, (m + 1) * length)
        heads = [
            attn[rows, g * head_size : (g + 1) * head_size] for g in range(depth // length)
        ]
        value_ref[rows, :] = lax.dot_general(
            probs_t_ref[m], jnp.concatenate(heads, 0), NN, preferred_element_type=F32
        ).astype(BF16)


def first_kernel(steps, rows_ref, weight_ref, probs_t_ref, value_ref, total):
    step = pl.program_id(0)

    @pl.when(step == 0)
    def _():
        total[...] = jnp.zeros_like(total)

    total[...] += lax.dot_general(rows_ref[...], weight_ref[...], NN, preferred_element_type=F32)

    @pl.when(step == steps - 1)
    def _():
        value_grad_of(total[...], probs_t_ref, value_ref)


def turn_kernel(
    steps, flag_ref, blocks_ref, rows_ref, back_ref, weight_ref, probs_t_ref, kept_ref,
    new_ref, value_ref, saved_ref, heads, total, sem,
):
    step = pl.program_id(0)
    head_size = blocks_ref.shape[2]

    @pl.when(step == 0)
    def _():
        for c in range(blocks_ref.shape[0]):
            heads[:, c * head_size : (c + 1) * head_size] = blocks_ref[c]
        total[...] = jnp.zeros_like(total)

    branch = lax.dot_general(heads[...], back_ref[0], NN, preferred_element_type=F32)
    new_rows = (rows_ref[...].astype(F32) + branch).astype(BF16)
    new_ref[...] = new_rows
    total[...] += lax.dot_general(new_rows, weight_ref[...], NN, preferred_element_type=F32)

    @pl.when(flag_ref[0] == 1)
    def _():
        width = new_ref.shape[1]
        spot = pl.ds(pl.multiple_of(step * width, width), width)
        copy = pltpu.make_async_copy(new_ref, saved_ref.at[:, spot], sem)
        copy.start()
        copy.wait()

    @pl.when(step == steps - 1)
    def _():
        value_grad_of(total[...], probs_t_ref, value_ref)


def first_value_grad(rows, weight_t, probs_t):
    count, width = rows.shape
    own = weight_t.shape[1]
    steps = 4
    tile = width // steps
    head_size = 128
    return pl.pallas_call(
        functools.partial(first_kernel, steps),
        grid=(steps,),
        in_specs=[
            pl.BlockSpec((count, tile), lambda i: (0, i)),
            pl.BlockSpec((tile, own), lambda i: (i, 0)),
            pl.BlockSpec(probs_t.shape, lambda i: (0, 0, 0)),
        ],
        out_specs=pl.BlockSpec((count, head_size), lambda i: (0, 0)),
        out_shape=jax.ShapeDtypeStruct((count, head_size), BF16),
        scratch_shapes=[pltpu.VMEM((count, own), F32)],
        compiler_params=pltpu.CompilerParams(vmem_limit_bytes=24 << 20),
        cost_estimate=pl.CostEstimate(
            flops=2 * count * width * own, bytes_accessed=2 * width * own, transcendentals=0
        ),
        name="first_turn",
    )(rows, weight_t, probs_t)


def turn(flag, blocks, rows, back, weight_t, probs_t, saved):
    count, width = rows.shape
    own = weight_t.shape[1]
    steps, depth, tile = back.shape
    head_size = blocks.shape[2]
    return pl.pallas_call(
        functools.partial(turn_kernel, steps),
        grid=(steps,),
        in_specs=[
            pl.BlockSpec(memory_space=pltpu.SMEM),
            pl.BlockSpec(blocks.shape, lambda i: (0, 0, 0)),
            pl.BlockSpec((count, tile), lambda i: (0, i)),
            pl.BlockSpec((1, depth, tile), lambda i: (i, 0, 0)),
            pl.BlockSpec((tile, own), lambda i: (i, 0)),
            pl.BlockSpec(probs_t.shape, lambda i: (0, 0, 0)),
            pl.BlockSpec(memory_space=pl.ANY),
        ],
        out_specs=[
            pl.BlockSpec((count, tile), lambda i: (0, i)),
            pl.BlockSpec((count, head_size), lambda i: (0, 0)),
            pl.BlockSpec(memory_space=pl.ANY),
        ],
        out_shape=[
            jax.ShapeDtypeStruct(rows.shape, BF16),
            jax.ShapeDtypeStruct((count, head_size), BF16),
            jax.ShapeDtypeStruct(rows.shape, BF16),
        ],
        scratch_shapes=[
            pltpu.VMEM((count, depth), BF16),
            pltpu.VMEM((count, own), F32),
            pltpu.SemaphoreType.DMA,
        ],
        input_output_aliases={6: 2},
        compiler_params=pltpu.CompilerParams(vmem_limit_bytes=24 << 20),
        cost_estimate=pl.CostEstimate(
            flops=2 * count * width * (own + depth),
            bytes_accessed=2 * width * (own + depth),
            transcendentals=0,
        ),
        name="turn",
    )(flag, blocks, rows, back, weight_t, probs_t, saved)


def on_device(grad_top, query, keys, values, out_weight, value_weight):
    sections = lax.axis_size("section")
    place = lax.axis_index("section")
    me = lax.axis_index("tensor")
    micro_batch, length = query.shape[1], query.shape[2]
    rows = micro_batch * length
    head_size = keys.shape[3]
    group = query.shape[3] // head_size
    feat_local = grad_top.shape[2]
    back = lax.all_gather(shift(value_weight[0].T, "section", -1), "tensor", axis=0)
    top = blocks_of_all(grad_top.reshape(rows, feat_local))
    incoming = top.transpose(1, 0, 2).reshape(rows, top.shape[0] * feat_local)
    query_heads = query[0].reshape(micro_batch, length, group, head_size)
    probs = jax.vmap(causal_probs)(query_heads, keys[0])
    mixed = jnp.einsum("mgqp,mpd->mqgd", probs, values[0], preferred_element_type=F32)
    mixed = mixed.astype(BF16).reshape(rows, group * head_size)
    probs_t = probs.transpose(0, 3, 1, 2).reshape(micro_batch, length, group * length)
    weight_t = out_weight[0].T
    saved = incoming
    value_grad = first_value_grad(incoming, weight_t, probs_t)
    for number in range(1, sections + 1):
        moved = shift(value_grad, "section", -1)
        incoming, moved = lax.optimization_barrier((incoming, moved))
        incoming = shift(incoming, "section", -1)
        blocks = blocks_of_all(moved)
        if number < sections:
            flag = (place == sections - 1 - number).astype(jnp.int32).reshape(1)
            incoming, value_grad, saved = turn(
                flag, blocks, incoming, back, weight_t, probs_t, saved
            )
    heads = blocks.transpose(1, 0, 2).reshape(rows, blocks.shape[0] * head_size)
    own = lax.dynamic_slice_in_dim(incoming, me * feat_local, feat_local, 1)
    branch = jnp.dot(
        heads, lax.dynamic_index_in_dim(back, me, 0, keepdims=False), preferred_element_type=F32
    )
    last = (own.astype(F32) + branch).astype(BF16)
    weight_grad = lax.dot_general(mixed, saved, TN, preferred_element_type=F32).astype(BF16)
    own = lax.dynamic_slice_in_dim(saved, me * feat_local, feat_local, 1)
    grads = shift(jnp.where(place == sections - 1, last, own), "section", 1)
    return (grads.reshape(1, micro_batch, length, feat_local), weight_grad[None])


def solution(mesh):
    placed = (
        P(None, None, "tensor"),
        P("section", None, None, "tensor"),
        P("section", None, None, "tensor"),
        P("section", None, None, "tensor"),
        P("section", "tensor", None),
        P("section", "tensor", None),
    )
    return jax.shard_map(
        on_device,
        mesh=mesh,
        in_specs=placed,
        out_specs=(P("section", None, None, "tensor"), P("section", "tensor", None)),
        check_vma=False,
    )
```

time: 935 us -> 942 us (level)
  the two profiles are of different devices: /device:TPU:32 before, /device:TPU:0 now
where the time goes in v2:
time: 942 us; the launch traced here: 935 us
  waiting for transfers between devices  348 us (37%)
  starting transfers between devices  285 us (30%)
  local copies, waits for them, and re-layouts  173 us (18%)
  Pallas kernels  106 us (11%)
  between operations  14.4 us (2%)
    ppermute x34, starting transfers between devices, shift(): lax.ppermute(value, axis, [(i, (i + by) % length) for i in range(length)])  161 us
    all_to_all x17, waiting for transfers between devices, blocks_of_all(): return lax.all_to_all(copies, 'tensor', 0, 0)  145 us
    unnamed x78, local copies, waits for them, and re-layouts  143 us
    all_to_all x17, starting transfers between devices, blocks_of_all(): return lax.all_to_all(copies, 'tensor', 0, 0)  124 us
    pallas_call x15, Pallas kernels, turn(): pl.pallas_call(functools.partial(turn_kernel, steps), grid=(steps,), in_s...  104 us
    ppermute x34, waiting for transfers between devices, shift(): lax.ppermute(value, axis, [(i, (i + by) % length) for i in range(length)])  103 us
    all_gather x1, waiting for transfers between devices, on_device(): lax.all_gather(shift(value_weight[0].T, 'section', -1), 'tensor', axis=0)  99.6 us
  transfers between devices with their start and end apart: 52, of which 50 were waited for; matrix products, arithmetic and copies ran while one was open for 5% of the time, Pallas kernels for 0%

profile of v2, /device:TPU:0, one launch (start us, length us, event | category | flops | bytes accessed | tf_op | source)
XLA Modules:
  0.0 935.2 jit_solution(3058577094818628341)
XLA Ops:
  11.2 18.3 %collective-permute-done.2 = bf16[1024,768]{0,1:T(8,128)(2,1)S(1)} collective-permute-done((bf16[1024,768]{0,1:T(8,128)(2,1)}, bf16[1024,768]{0,1:T(8,128)(2,1)S(1)}, u32[]{:S(2)}, u32[]{:S(2)}) %collective-permute-start.2) | collective-permute-done | bytes 1572896 | tf_op jit(solution)/shard_map/ppermute | solution.py:30
  31.9 7.5 all-to-all-start
  41.1 12.9 %copy.36 = bf16[1,768,6144]{1,2,0:T(8,128)(2,1)} copy(bf16[1,768,6144]{2,1,0:T(8,128)(2,1)} %param.10) | data formatting | bytes 18874368 | tf_op args[4]
  54.0 14.8 %all-to-all-done = bf16[8,128,768]{2,1,0:T(8,128)(2,1)S(1)} async-done(((bf16[8,128,768]{2,1,0:T(8,128)(2,1)}), bf16[8,128,768]{2,1,0:T(8,128)(2,1)S(1)}, u32[]{:S(2)}, u32[]{:S(2)}) %all-to-all-start) | async-done | bytes 1572896 | tf_op jit(solution)/shard_map/all_to_all | solution.py:35
  84.0 8.5 all-to-all-start.1
  92.5 99.6 %all-gather.3.cloned.1.call-done = bf16[8192,768]{0,1:T(8,128)(2,1)} async-done(((bf16[1024,768]{0,1:T(8,128)(2,1)}), bf16[8192,768]{0,1:T(8,128)(2,1)}) %all-gather.3.cloned.1.call-update) | async-done | bytes 12582928 | tf_op jit(solution)/shard_map/all_gather | solution.py:174
  192.1 16.6 %copy.39 = bf16[8192,768]{1,0:T(8,128)(2,1)} copy(bf16[8192,768]{0,1:T(8,128)(2,1)} %all-gather.3.cloned.1.call-done) | data formatting | bytes 25165824 | tf_op jit(solution)/shard_map/all_gather | solution.py:174
  223.9 10.9 %collective-permute-start.3 = (bf16[128,128]{1,0:T(8,128)(2,1)S(1)}, bf16[128,128]{1,0:T(8,128)(2,1)S(1)}, u32[]{:S(2)}, u32[]{:S(2)}) collective-permute-start(bf16[128,128]{1,0:T(8,128)(2,1)S(1)} %get-tuple-element.82), channel_id=1, source_target_pairs={{0,120},{8,0},{16,8},{24,16},{32,24},{40,32},{48,40},{56,48},{64,5... | collective-permute-start | bytes 98312 | tf_op jit(solution)/shard_map/ppermute | solution.py:30
  246.8 8.8 all-to-all-done.2.blocks_ref
  294.3 8.8 all-to-all-done.3.blocks_ref
  340.7 8.8 all-to-all-done.4.blocks_ref
  380.8 7.3 all-to-all-start.5
  388.1 8.8 all-to-all-done.5.blocks_ref
  434.7 8.8 all-to-all-done.6.blocks_ref
  474.6 7.6 all-to-all-start.7
  482.2 8.8 all-to-all-done.7.blocks_ref
  528.6 8.8 all-to-all-done.8.blocks_ref
  568.5 7.6 all-to-all-start.9
  576.1 8.8 all-to-all-done.9.blocks_ref
  622.7 8.8 all-to-all-done.10.blocks_ref
  662.3 7.6 all-to-all-start.11
  669.9 8.8 all-to-all-done.11.blocks_ref
  709.4 7.2 all-to-all-start.12
  716.6 8.8 all-to-all-done.12.blocks_ref
  756.2 7.6 all-to-all-start.13
  763.8 8.8 all-to-all-done.13.blocks_ref
  803.3 7.2 all-to-all-start.14
  810.5 8.8 all-to-all-done.14.blocks_ref
  850.0 7.7 all-to-all-start.15
  857.7 8.8 all-to-all-done.15.blocks_ref
  897.3 7.3 all-to-all-start.16
  906.0 7.4 all-to-all-done.16
  (199 shorter events, 534.2 us)
Async XLA Ops:
  7.2 184.9 %all-gather.3.cloned.1.call-start = ((), (), s32[]{:S(2)}) async-start(), calls=%async_computation.17 | async-start | bytes 14155776 | tf_op jit(solution)/shard_map/all_gather | solution.py:174
  7.2 22.2 %collective-permute-start.2 = (bf16[1024,768]{0,1:T(8,128)(2,1)}, bf16[1024,768]{0,1:T(8,128)(2,1)S(1)}, u32[]{:S(2)}, u32[]{:S(2)}) collective-permute-start(bf16[1024,768]{0,1:T(8,128)(2,1)} %bitcast.121), channel_id=1, source_target_pairs={{0,120},{8,0},{16,8},{24,16},{32,24},{40,32},{48,40},{56,48},{64,5... | collective-permute-start | bytes 4718600 | tf_op jit(solution)/shard_map/ppermute | solution.py:30
  31.9 37.0 %all-to-all-start = ((bf16[8,128,768]{2,1,0:T(8,128)(2,1)}), bf16[8,128,768]{2,1,0:T(8,128)(2,1)S(1)}, u32[]{:S(2)}, u32[]{:S(2)}) async-start(bf16[8,128,768]{2,1,0:T(8,128)(2,1)} %broadcast_in_dim.51), calls=%async_computation | async-start | bytes 3145728 | tf_op jit(solution)/shard_map/all_to_all | solution.py:35
  79.4 129.3 %collective-permute-start.1 = (bf16[128,6144]{1,0:T(8,128)(2,1)S(1)}, bf16[128,6144]{1,0:T(8,128)(2,1)S(1)}, u32[]{:S(2)}, u32[]{:S(2)}) collective-permute-start(bf16[128,6144]{1,0:T(8,128)(2,1)S(1)} %bitcast.114), channel_id=1, source_target_pairs={{0,120},{8,0},{16,8},{24,16},{32,24},{40,32},{48,40},{56,48},{64,5... | collective-permute-start | bytes 4718600 | tf_op jit(solution)/shard_map/ppermute | solution.py:30
  84.0 124.7 %all-to-all-start.1 = ((bf16[8,128,128]{2,1,0:T(8,128)(2,1)}), bf16[8,128,128]{2,1,0:T(8,128)(2,1)S(1)}, u32[]{:S(2)}, u32[]{:S(2)}) async-start(bf16[8,128,128]{2,1,0:T(8,128)(2,1)} %broadcast_in_dim.56), calls=%async_computation.1 | async-start | bytes 524288 | tf_op jit(solution)/shard_map/all_to_all | solution.py:35
  236.4 24.2 %collective-permute-start.4 = (bf16[128,6144]{1,0:T(8,128)(2,1)}, bf16[128,6144]{1,0:T(8,128)(2,1)S(1)}, u32[]{:S(2)}, u32[]{:S(2)}) collective-permute-start(bf16[128,6144]{1,0:T(8,128)(2,1)} %get-tuple-element.84), channel_id=1, source_target_pairs={{0,120},{8,0},{16,8},{24,16},{32,24},{40,32},{48,40},{56,48},{64,5... | collective-permute-start | bytes 4718600 | tf_op jit(solution)/shard_map/ppermute | solution.py:30
  283.1 24.2 %collective-permute-start.6 = (bf16[128,6144]{1,0:T(8,128)(2,1)}, bf16[128,6144]{1,0:T(8,128)(2,1)S(1)}, u32[]{:S(2)}, u32[]{:S(2)}) collective-permute-start(bf16[128,6144]{1,0:T(8,128)(2,1)} %get-tuple-element.89), channel_id=1, source_target_pairs={{0,120},{8,0},{16,8},{24,16},{32,24},{40,32},{48,40},{56,48},{64,5... | collective-permute-start | bytes 4718600 | tf_op jit(solution)/shard_map/ppermute | solution.py:30
  329.1 24.2 %collective-permute-start.8 = (bf16[128,6144]{1,0:T(8,128)(2,1)}, bf16[128,6144]{1,0:T(8,128)(2,1)S(1)}, u32[]{:S(2)}, u32[]{:S(2)}) collective-permute-start(bf16[128,6144]{1,0:T(8,128)(2,1)} %get-tuple-element.94), channel_id=1, source_target_pairs={{0,120},{8,0},{16,8},{24,16},{32,24},{40,32},{48,40},{56,48},{64,5... | collective-permute-start | bytes 4718600 | tf_op jit(solution)/shard_map/ppermute | solution.py:30
  376.2 24.2 %collective-permute-start.10 = (bf16[128,6144]{1,0:T(8,128)(2,1)}, bf16[128,6144]{1,0:T(8,128)(2,1)S(1)}, u32[]{:S(2)}, u32[]{:S(2)}) collective-permute-start(bf16[128,6144]{1,0:T(8,128)(2,1)} %get-tuple-element.99), channel_id=1, source_target_pairs={{0,120},{8,0},{16,8},{24,16},{32,24},{40,32},{48,40},{56,48},{64,5... | collective-permute-start | bytes 4718600 | tf_op jit(solution)/shard_map/ppermute | solution.py:30
  380.8 16.1 %all-to-all-start.5 = ((bf16[8,128,128]{2,1,0:T(8,128)(2,1)}), bf16[8,128,128]{2,1,0:T(8,128)(2,1)S(1)}, u32[]{:S(2)}, u32[]{:S(2)}) async-start(bf16[8,128,128]{2,1,0:T(8,128)(2,1)} %broadcast_in_dim.60), calls=%async_computation.5 | async-start | bytes 524288 | tf_op jit(solution)/shard_map/all_to_all | solution.py:35
  423.0 24.2 %collective-permute-start.12 = (bf16[128,6144]{1,0:T(8,128)(2,1)}, bf16[128,6144]{1,0:T(8,128)(2,1)S(1)}, u32[]{:S(2)}, u32[]{:S(2)}) collective-permute-start(bf16[128,6144]{1,0:T(8,128)(2,1)} %get-tuple-element.104), channel_id=1, source_target_pairs={{0,120},{8,0},{16,8},{24,16},{32,24},{40,32},{48,40},{56,48},{64,5... | collective-permute-start | bytes 4718600 | tf_op jit(solution)/shard_map/ppermute | solution.py:30
  427.6 15.9 %all-to-all-start.6 = ((bf16[8,128,128]{2,1,0:T(8,128)(2,1)}), bf16[8,128,128]{2,1,0:T(8,128)(2,1)S(1)}, u32[]{:S(2)}, u32[]{:S(2)}) async-start(bf16[8,128,128]{2,1,0:T(8,128)(2,1)} %broadcast_in_dim.61), calls=%async_computation.6 | async-start | bytes 524288 | tf_op jit(solution)/shard_map/all_to_all | solution.py:35
  470.0 24.2 %collective-permute-start.14 = (bf16[128,6144]{1,0:T(8,128)(2,1)}, bf16[128,6144]{1,0:T(8,128)(2,1)S(1)}, u32[]{:S(2)}, u32[]{:S(2)}) collective-permute-start(bf16[128,6144]{1,0:T(8,128)(2,1)} %get-tuple-element.109), channel_id=1, source_target_pairs={{0,120},{8,0},{16,8},{24,16},{32,24},{40,32},{48,40},{56,48},{64,5... | collective-permute-start | bytes 4718600 | tf_op jit(solution)/shard_map/ppermute | solution.py:30
  474.6 16.3 %all-to-all-start.7 = ((bf16[8,128,128]{2,1,0:T(8,128)(2,1)}), bf16[8,128,128]{2,1,0:T(8,128)(2,1)S(1)}, u32[]{:S(2)}, u32[]{:S(2)}) async-start(bf16[8,128,128]{2,1,0:T(8,128)(2,1)} %broadcast_in_dim.62), calls=%async_computation.7 | async-start | bytes 524288 | tf_op jit(solution)/shard_map/all_to_all | solution.py:35
  516.9 24.2 %collective-permute-start.16 = (bf16[128,6144]{1,0:T(8,128)(2,1)}, bf16[128,6144]{1,0:T(8,128)(2,1)S(1)}, u32[]{:S(2)}, u32[]{:S(2)}) collective-permute-start(bf16[128,6144]{1,0:T(8,128)(2,1)} %get-tuple-element.114), channel_id=1, source_target_pairs={{0,120},{8,0},{16,8},{24,16},{32,24},{40,32},{48,40},{56,48},{64,5... | collective-permute-start | bytes 4718600 | tf_op jit(solution)/shard_map/ppermute | solution.py:30
  521.5 16.0 %all-to-all-start.8 = ((bf16[8,128,128]{2,1,0:T(8,128)(2,1)}), bf16[8,128,128]{2,1,0:T(8,128)(2,1)S(1)}, u32[]{:S(2)}, u32[]{:S(2)}) async-start(bf16[8,128,128]{2,1,0:T(8,128)(2,1)} %broadcast_in_dim.63), calls=%async_computation.8 | async-start | bytes 524288 | tf_op jit(solution)/shard_map/all_to_all | solution.py:35
  563.9 24.2 %collective-permute-start.18 = (bf16[128,6144]{1,0:T(8,128)(2,1)}, bf16[128,6144]{1,0:T(8,128)(2,1)S(1)}, u32[]{:S(2)}, u32[]{:S(2)}) collective-permute-start(bf16[128,6144]{1,0:T(8,128)(2,1)} %get-tuple-element.119), channel_id=1, source_target_pairs={{0,120},{8,0},{16,8},{24,16},{32,24},{40,32},{48,40},{56,48},{64,5... | collective-permute-start | bytes 4718600 | tf_op jit(solution)/shard_map/ppermute | solution.py:30
  568.5 16.4 %all-to-all-start.9 = ((bf16[8,128,128]{2,1,0:T(8,128)(2,1)}), bf16[8,128,128]{2,1,0:T(8,128)(2,1)S(1)}, u32[]{:S(2)}, u32[]{:S(2)}) async-start(bf16[8,128,128]{2,1,0:T(8,128)(2,1)} %broadcast_in_dim.64), calls=%async_computation.9 | async-start | bytes 524288 | tf_op jit(solution)/shard_map/all_to_all | solution.py:35
  610.9 24.2 %collective-permute-start.20 = (bf16[128,6144]{1,0:T(8,128)(2,1)}, bf16[128,6144]{1,0:T(8,128)(2,1)S(1)}, u32[]{:S(2)}, u32[]{:S(2)}) collective-permute-start(bf16[128,6144]{1,0:T(8,128)(2,1)} %get-tuple-element.124), channel_id=1, source_target_pairs={{0,120},{8,0},{16,8},{24,16},{32,24},{40,32},{48,40},{56,48},{64,5... | collective-permute-start | bytes 4718600 | tf_op jit(solution)/shard_map/ppermute | solution.py:30
  615.5 16.0 %all-to-all-start.10 = ((bf16[8,128,128]{2,1,0:T(8,128)(2,1)}), bf16[8,128,128]{2,1,0:T(8,128)(2,1)S(1)}, u32[]{:S(2)}, u32[]{:S(2)}) async-start(bf16[8,128,128]{2,1,0:T(8,128)(2,1)} %broadcast_in_dim.65), calls=%async_computation.10 | async-start | bytes 524288 | tf_op jit(solution)/shard_map/all_to_all | solution.py:35
  657.7 24.2 %collective-permute-start.22 = (bf16[128,6144]{1,0:T(8,128)(2,1)}, bf16[128,6144]{1,0:T(8,128)(2,1)S(1)}, u32[]{:S(2)}, u32[]{:S(2)}) collective-permute-start(bf16[128,6144]{1,0:T(8,128)(2,1)} %get-tuple-element.129), channel_id=1, source_target_pairs={{0,120},{8,0},{16,8},{24,16},{32,24},{40,32},{48,40},{56,48},{64,5... | collective-permute-start | bytes 4718600 | tf_op jit(solution)/shard_map/ppermute | solution.py:30
  662.3 16.4 %all-to-all-start.11 = ((bf16[8,128,128]{2,1,0:T(8,128)(2,1)}), bf16[8,128,128]{2,1,0:T(8,128)(2,1)S(1)}, u32[]{:S(2)}, u32[]{:S(2)}) async-start(bf16[8,128,128]{2,1,0:T(8,128)(2,1)} %broadcast_in_dim.66), calls=%async_computation.11 | async-start | bytes 524288 | tf_op jit(solution)/shard_map/all_to_all | solution.py:35
  704.8 24.2 %collective-permute-start.24 = (bf16[128,6144]{1,0:T(8,128)(2,1)}, bf16[128,6144]{1,0:T(8,128)(2,1)S(1)}, u32[]{:S(2)}, u32[]{:S(2)}) collective-permute-start(bf16[128,6144]{1,0:T(8,128)(2,1)} %get-tuple-element.134), channel_id=1, source_target_pairs={{0,120},{8,0},{16,8},{24,16},{32,24},{40,32},{48,40},{56,48},{64,5... | collective-permute-start | bytes 4718600 | tf_op jit(solution)/shard_map/ppermute | solution.py:30
  709.4 16.0 %all-to-all-start.12 = ((bf16[8,128,128]{2,1,0:T(8,128)(2,1)}), bf16[8,128,128]{2,1,0:T(8,128)(2,1)S(1)}, u32[]{:S(2)}, u32[]{:S(2)}) async-start(bf16[8,128,128]{2,1,0:T(8,128)(2,1)} %broadcast_in_dim.67), calls=%async_computation.12 | async-start | bytes 524288 | tf_op jit(solution)/shard_map/all_to_all | solution.py:35
  751.6 24.3 %collective-permute-start.26 = (bf16[128,6144]{1,0:T(8,128)(2,1)}, bf16[128,6144]{1,0:T(8,128)(2,1)S(1)}, u32[]{:S(2)}, u32[]{:S(2)}) collective-permute-start(bf16[128,6144]{1,0:T(8,128)(2,1)} %get-tuple-element.139), channel_id=1, source_target_pairs={{0,120},{8,0},{16,8},{24,16},{32,24},{40,32},{48,40},{56,48},{64,5... | collective-permute-start | bytes 4718600 | tf_op jit(solution)/shard_map/ppermute | solution.py:30
  756.2 16.4 %all-to-all-start.13 = ((bf16[8,128,128]{2,1,0:T(8,128)(2,1)}), bf16[8,128,128]{2,1,0:T(8,128)(2,1)S(1)}, u32[]{:S(2)}, u32[]{:S(2)}) async-start(bf16[8,128,128]{2,1,0:T(8,128)(2,1)} %broadcast_in_dim.68), calls=%async_computation.13 | async-start | bytes 524288 | tf_op jit(solution)/shard_map/all_to_all | solution.py:35
  798.7 24.2 %collective-permute-start.28 = (bf16[128,6144]{1,0:T(8,128)(2,1)}, bf16[128,6144]{1,0:T(8,128)(2,1)S(1)}, u32[]{:S(2)}, u32[]{:S(2)}) collective-permute-start(bf16[128,6144]{1,0:T(8,128)(2,1)} %get-tuple-element.144), channel_id=1, source_target_pairs={{0,120},{8,0},{16,8},{24,16},{32,24},{40,32},{48,40},{56,48},{64,5... | collective-permute-start | bytes 4718600 | tf_op jit(solution)/shard_map/ppermute | solution.py:30
  803.3 16.0 %all-to-all-start.14 = ((bf16[8,128,128]{2,1,0:T(8,128)(2,1)}), bf16[8,128,128]{2,1,0:T(8,128)(2,1)S(1)}, u32[]{:S(2)}, u32[]{:S(2)}) async-start(bf16[8,128,128]{2,1,0:T(8,128)(2,1)} %broadcast_in_dim.69), calls=%async_computation.14 | async-start | bytes 524288 | tf_op jit(solution)/shard_map/all_to_all | solution.py:35
  845.5 24.2 %collective-permute-start.30 = (bf16[128,6144]{1,0:T(8,128)(2,1)}, bf16[128,6144]{1,0:T(8,128)(2,1)S(1)}, u32[]{:S(2)}, u32[]{:S(2)}) collective-permute-start(bf16[128,6144]{1,0:T(8,128)(2,1)} %get-tuple-element.149), channel_id=1, source_target_pairs={{0,120},{8,0},{16,8},{24,16},{32,24},{40,32},{48,40},{56,48},{64,5... | collective-permute-start | bytes 4718600 | tf_op jit(solution)/shard_map/ppermute | solution.py:30
  850.0 16.5 %all-to-all-start.15 = ((bf16[8,128,128]{2,1,0:T(8,128)(2,1)}), bf16[8,128,128]{2,1,0:T(8,128)(2,1)S(1)}, u32[]{:S(2)}, u32[]{:S(2)}) async-start(bf16[8,128,128]{2,1,0:T(8,128)(2,1)} %broadcast_in_dim.70), calls=%async_computation.15 | async-start | bytes 524288 | tf_op jit(solution)/shard_map/all_to_all | solution.py:35
  892.6 24.2 %collective-permute-start.32 = (bf16[128,6144]{1,0:T(8,128)(2,1)}, bf16[128,6144]{1,0:T(8,128)(2,1)}, u32[]{:S(2)}, u32[]{:S(2)}) collective-permute-start(bf16[128,6144]{1,0:T(8,128)(2,1)} %get-tuple-element.153), channel_id=1, source_target_pairs={{0,120},{8,0},{16,8},{24,16},{32,24},{40,32},{48,40},{56,48},{64,5... | collective-permute-start | bytes 4718600 | tf_op jit(solution)/shard_map/ppermute | solution.py:30
  897.3 16.1 %all-to-all-start.16 = ((bf16[8,128,128]{1,2,0:T(8,128)(2,1)}), bf16[8,128,128]{1,2,0:T(8,128)(2,1)S(1)}, u32[]{:S(2)}, u32[]{:S(2)}) async-start(bf16[8,128,128]{1,2,0:T(8,128)(2,1)} %broadcast_in_dim.71), calls=%async_computation.16 | async-start | bytes 524288 | tf_op jit(solution)/shard_map/all_to_all | solution.py:35
  (58 other events, 1255.0 us)
Sparse Core Ops, SparseCore 0:
  30.7 161.3 all-gather.2

commit v3 on v2

--- a/solution.py
+++ b/solution.py
@@ -11,6 +11,7 @@
 F32 = jnp.float32
 BF16 = jnp.bfloat16
 NN = (((1,), (0,)), ((), ()))
+NT = (((1,), (1,)), ((), ()))
 TN = (((0,), (0,)), ((), ()))
 
 
@@ -30,9 +31,61 @@
     return lax.ppermute(value, axis, [(i, (i + by) % length) for i in range(length)])
 
 
+def hand_down(value, section):
+    length = lax.axis_size("section")
+    half = length // 2
+    if section % 2:
+        pairs = [(i, i ^ 1) for i in range(length)]
+    else:
+        lows = [section - 1] if section == half else [
+            i for i in range(1, length - 1, 2) if i != half - 1
+        ]
+        other = {i: i for i in range(length)}
+        for low in lows:
+            other[low], other[low + 1] = low + 1, low
+        pairs = sorted(other.items())
+    return lax.ppermute(value, "section", pairs)
+
+
+def copies_kernel(value_ref, out_ref):
+    for c in range(out_ref.shape[0]):
+        out_ref[c] = value_ref[...]
+
+
 def blocks_of_all(value):
-    copies = jnp.broadcast_to(value[None], (lax.axis_size("tensor"),) + value.shape)
+    shape = (lax.axis_size("tensor"),) + value.shape
+    copies = pl.pallas_call(
+        copies_kernel,
+        in_specs=[pl.BlockSpec(memory_space=pltpu.VMEM)],
+        out_specs=pl.BlockSpec(memory_space=pltpu.VMEM),
+        out_shape=jax.ShapeDtypeStruct(shape, value.dtype),
+        compiler_params=pltpu.CompilerParams(vmem_limit_bytes=6 << 20),
+        cost_estimate=pl.CostEstimate(
+            flops=0, bytes_accessed=2 * math.prod(shape), transcendentals=0
+        ),
+        name="copies",
+    )(value)
     return lax.all_to_all(copies, "tensor", 0, 0)
+
+
+def transpose_kernel(value_ref, out_ref):
+    out_ref[...] = value_ref[...].T
+
+
+def transposed(value, tile=512):
+    rows, columns = value.shape
+    return pl.pallas_call(
+        transpose_kernel,
+        grid=(columns // tile,),
+        in_specs=[pl.BlockSpec((rows, tile), lambda i: (0, i))],
+        out_specs=pl.BlockSpec((tile, rows), lambda i: (i, 0)),
+        out_shape=jax.ShapeDtypeStruct((columns, rows), value.dtype),
+        compiler_params=pltpu.CompilerParams(vmem_limit_bytes=12 << 20),
+        cost_estimate=pl.CostEstimate(
+            flops=0, bytes_accessed=4 * rows * columns, transcendentals=0
+        ),
+        name="transposed",
+    )(value)
 
 
 def value_grad_of(total, probs_t_ref, value_ref):
@@ -64,7 +117,7 @@
 
 
 def turn_kernel(
-    steps, flag_ref, blocks_ref, rows_ref, back_ref, weight_ref, probs_t_ref, kept_ref,
+    steps, section, place_ref, blocks_ref, rows_ref, back_ref, weight_ref, probs_t_ref, kept_ref,
     new_ref, value_ref, saved_ref, heads, total, sem,
 ):
     step = pl.program_id(0)
@@ -81,7 +134,7 @@
     new_ref[...] = new_rows
     total[...] += lax.dot_general(new_rows, weight_ref[...], NN, preferred_element_type=F32)
 
-    @pl.when(flag_ref[0] == 1)
+    @pl.when(place_ref[0] == section)
     def _():
         width = new_ref.shape[1]
         spot = pl.ds(pl.multiple_of(step * width, width), width)
@@ -111,7 +164,7 @@
         out_specs=pl.BlockSpec((count, head_size), lambda i: (0, 0)),
         out_shape=jax.ShapeDtypeStruct((count, head_size), BF16),
         scratch_shapes=[pltpu.VMEM((count, own), F32)],
-        compiler_params=pltpu.CompilerParams(vmem_limit_bytes=24 << 20),
+        compiler_params=pltpu.CompilerParams(vmem_limit_bytes=16 << 20),
         cost_estimate=pl.CostEstimate(
             flops=2 * count * width * own, bytes_accessed=2 * width * own, transcendentals=0
         ),
@@ -119,13 +172,13 @@
     )(rows, weight_t, probs_t)
 
 
-def turn(flag, blocks, rows, back, weight_t, probs_t, saved):
+def turn(section, place, blocks, rows, back, weight_t, probs_t, saved):
     count, width = rows.shape
     own = weight_t.shape[1]
     steps, depth, tile = back.shape
     head_size = blocks.shape[2]
     return pl.pallas_call(
-        functools.partial(turn_kernel, steps),
+        functools.partial(turn_kernel, steps, section),
         grid=(steps,),
         in_specs=[
             pl.BlockSpec(memory_space=pltpu.SMEM),
@@ -152,14 +205,14 @@
             pltpu.SemaphoreType.DMA,
         ],
         input_output_aliases={6: 2},
-        compiler_params=pltpu.CompilerParams(vmem_limit_bytes=24 << 20),
+        compiler_params=pltpu.CompilerParams(vmem_limit_bytes=16 << 20),
         cost_estimate=pl.CostEstimate(
             flops=2 * count * width * (own + depth),
             bytes_accessed=2 * width * (own + depth),
             transcendentals=0,
         ),
         name="turn",
-    )(flag, blocks, rows, back, weight_t, probs_t, saved)
+    )(place, blocks, rows, back, weight_t, probs_t, saved)
 
 
 def on_device(grad_top, query, keys, values, out_weight, value_weight):
@@ -171,7 +224,7 @@
     head_size = keys.shape[3]
     group = query.shape[3] // head_size
     feat_local = grad_top.shape[2]
-    back = lax.all_gather(shift(value_weight[0].T, "section", -1), "tensor", axis=0)
+    back = lax.all_gather(shift(transposed(value_weight[0]), "section", -1), "tensor", axis=0)
     top = blocks_of_all(grad_top.reshape(rows, feat_local))
     incoming = top.transpose(1, 0, 2).reshape(rows, top.shape[0] * feat_local)
     query_heads = query[0].reshape(micro_batch, length, group, head_size)
@@ -179,28 +232,26 @@
     mixed = jnp.einsum("mgqp,mpd->mqgd", probs, values[0], preferred_element_type=F32)
     mixed = mixed.astype(BF16).reshape(rows, group * head_size)
     probs_t = probs.transpose(0, 3, 1, 2).reshape(micro_batch, length, group * length)
-    weight_t = out_weight[0].T
+    weight_t = transposed(out_weight[0])
+    spot = place.astype(jnp.int32).reshape(1)
     saved = incoming
     value_grad = first_value_grad(incoming, weight_t, probs_t)
-    for number in range(1, sections + 1):
-        moved = shift(value_grad, "section", -1)
+    for section in range(sections - 1, 0, -1):
+        moved = hand_down(value_grad, section)
         incoming, moved = lax.optimization_barrier((incoming, moved))
-        incoming = shift(incoming, "section", -1)
+        incoming = hand_down(incoming, section)
         blocks = blocks_of_all(moved)
-        if number < sections:
-            flag = (place == sections - 1 - number).astype(jnp.int32).reshape(1)
-            incoming, value_grad, saved = turn(
-                flag, blocks, incoming, back, weight_t, probs_t, saved
-            )
+        incoming, value_grad, saved = turn(
+            section - 1, spot, blocks, incoming, back, weight_t, probs_t, saved
+        )
+    own = lax.dynamic_slice_in_dim(saved, me * feat_local, feat_local, 1)
+    above = shift(own, "section", 1)
+    blocks = blocks_of_all(value_grad)
+    weight_grad = lax.dot_general(mixed, saved, TN, preferred_element_type=F32).astype(BF16)
     heads = blocks.transpose(1, 0, 2).reshape(rows, blocks.shape[0] * head_size)
-    own = lax.dynamic_slice_in_dim(incoming, me * feat_local, feat_local, 1)
-    branch = jnp.dot(
-        heads, lax.dynamic_index_in_dim(back, me, 0, keepdims=False), preferred_element_type=F32
-    )
+    branch = lax.dot_general(heads, value_weight[0], NT, preferred_element_type=F32)
     last = (own.astype(F32) + branch).astype(BF16)
-    weight_grad = lax.dot_general(mixed, saved, TN, preferred_element_type=F32).astype(BF16)
-    own = lax.dynamic_slice_in_dim(saved, me * feat_local, feat_local, 1)
-    grads = shift(jnp.where(place == sections - 1, last, own), "section", 1)
+    grads = jnp.where(place == 0, last, above)
     return (grads.reshape(1, micro_batch, length, feat_local), weight_grad[None])
 
 

time: 942 us -> 626 us (0.66)
  waiting for transfers between devices: 348 us -> 159 us
  blocking collectives: 0 us -> 156 us
  starting transfers between devices: 285 us -> 141 us
  local copies, waits for them, and re-layouts: 173 us -> 37.5 us
    ppermute x34 -> x2, starting transfers between devices: 161 us -> 3.96 us  [shift(): lax.ppermute(value, axis, [(i, (i + by) % length) for i in range(length)])]
    all_to_all x0 -> x13, blocking collectives: none -> 156 us  [blocks_of_all(): return lax.all_to_all(copies, 'tensor', 0, 0)]
    ppermute x0 -> x30, starting transfers between devices: none -> 115 us  [hand_down(): return lax.ppermute(value, 'section', pairs)]
    all_to_all x17 -> x4, waiting for transfers between devices: 145 us -> 35.2 us  [blocks_of_all(): return lax.all_to_all(copies, 'tensor', 0, 0)]
    unnamed x78 -> x40, local copies, waits for them, and re-layouts: 143 us -> 34.1 us
    all_to_all x17 -> x4, starting transfers between devices: 124 us -> 22.3 us  [blocks_of_all(): return lax.all_to_all(copies, 'tensor', 0, 0)]
    ppermute x34 -> x2, waiting for transfers between devices: 103 us -> 17.9 us  [shift(): lax.ppermute(value, axis, [(i, (i + by) % length) for i in range(length)])]
    all_gather x1 -> x0, local copies, waits for them, and re-layouts: 16.6 us -> none  [on_device(): lax.all_gather(shift(value_weight[0].T, 'section', -1), 'tensor', axis=0)]
  transfers between devices with their start and end apart: 52 -> 37, of which waited for: 50 -> 14; matrix products, arithmetic and copies ran while one was open for 5% -> 2% of each run, Pallas kernels for 0% -> 1%
where the time goes in v3:
time: 626 us; the launch traced here: 623 us
  waiting for transfers between devices  159 us (25%)
  blocking collectives  156 us (25%)
  starting transfers between devices  141 us (23%)
  Pallas kernels  105 us (17%)
  local copies, waits for them, and re-layouts  37.5 us (6%)
  between operations  14.7 us (2%)
  matrix products  8.49 us (1%)
    all_to_all x13, blocking collectives, blocks_of_all(): return lax.all_to_all(copies, 'tensor', 0, 0)  156 us
    ppermute x30, starting transfers between devices, hand_down(): return lax.ppermute(value, 'section', pairs)  115 us
    all_gather x1, waiting for transfers between devices, on_device(): lax.all_gather(shift(transposed(value_weight[0]), 'section', -1), 'tensor...  98.6 us
    pallas_call x15, Pallas kernels, turn(): pl.pallas_call(functools.partial(turn_kernel, steps, section), grid=(step...  95.8 us
    all_to_all x4, waiting for transfers between devices, blocks_of_all(): return lax.all_to_all(copies, 'tensor', 0, 0)  35.2 us
    unnamed x40, local copies, waits for them, and re-layouts  34.1 us
    all_to_all x4, starting transfers between devices, blocks_of_all(): return lax.all_to_all(copies, 'tensor', 0, 0)  22.3 us
    ppermute x2, waiting for transfers between devices, shift(): lax.ppermute(value, axis, [(i, (i + by) % length) for i in range(length)])  17.9 us
  transfers between devices with their start and end apart: 37, of which 14 were waited for; matrix products, arithmetic and copies ran while one was open for 2% of the time, Pallas kernels for 1%

profile of v3, /device:TPU:0, one launch (start us, length us, event | category | flops | bytes accessed | tf_op | source)
XLA Modules:
  0.0 622.6 jit_solution(1811353221104130120)
XLA Ops:
  13.3 17.9 %collective-permute-done.2 = bf16[1024,768]{1,0:T(8,128)(2,1)S(1)} collective-permute-done((bf16[1024,768]{1,0:T(8,128)(2,1)S(1)}, bf16[1024,768]{1,0:T(8,128)(2,1)S(1)}, u32[]{:S(2)}, u32[]{:S(2)}) %collective-permute-start.2) | collective-permute-done | bytes 1572896 | tf_op jit(solution)/shard_map/ppermute | solution.py:31
  33.6 7.5 %all-to-all-start = ((bf16[8,128,768]{2,1,0:T(8,128)(2,1)}), bf16[8,128,768]{2,1,0:T(8,128)(2,1)S(1)}, u32[]{:S(2)}, u32[]{:S(2)}) async-start(bf16[8,128,768]{2,1,0:T(8,128)(2,1)} %copies.17), calls=%async_computation | async-start | bytes 3145728 | tf_op jit(solution)/shard_map/all_to_all | solution.py:68
  55.4 15.4 %all-to-all-done = bf16[8,128,768]{2,1,0:T(8,128)(2,1)S(1)} async-done(((bf16[8,128,768]{2,1,0:T(8,128)(2,1)}), bf16[8,128,768]{2,1,0:T(8,128)(2,1)S(1)}, u32[]{:S(2)}, u32[]{:S(2)}) %all-to-all-start) | async-done | bytes 1572896 | tf_op jit(solution)/shard_map/all_to_all | solution.py:68
  79.1 7.8 %all-to-all-start.1 = ((bf16[8,128,128]{2,1,0:T(8,128)(2,1)}), bf16[8,128,128]{2,1,0:T(8,128)(2,1)S(1)}, u32[]{:S(2)}, u32[]{:S(2)}) async-start(bf16[8,128,128]{2,1,0:T(8,128)(2,1)} %copy-done.12), calls=%async_computation.1 | async-start | bytes 524288 | tf_op jit(solution)/shard_map/all_to_all | solution.py:68
  86.9 9.3 %all-to-all-done.1.blocks_ref = bf16[8,128,128]{2,1,0:T(8,128)(2,1)S(1)} async-done(((bf16[8,128,128]{2,1,0:T(8,128)(2,1)}), bf16[8,128,128]{2,1,0:T(8,128)(2,1)S(1)}, u32[]{:S(2)}, u32[]{:S(2)}) %all-to-all-start.1) | async-done | bytes 262176 | tf_op jit(solution)/shard_map/all_to_all | solution.py:68
  96.2 98.6 %all-gather.3.cloned.1.call-done = bf16[8192,768]{1,0:T(8,128)(2,1)} async-done(((bf16[1024,768]{1,0:T(8,128)(2,1)}), bf16[8192,768]{1,0:T(8,128)(2,1)}) %all-gather.3.cloned.1.call-update) | async-done | bytes 12582928 | tf_op jit(solution)/shard_map/all_gather | solution.py:227
  203.0 6.3 %turn.15 = (bf16[128,6144]{1,0:T(8,128)(2,1)S(1)}, bf16[128,128]{1,0:T(8,128)(2,1)S(1)}, bf16[128,6144]{1,0:T(8,128)(2,1)S(1)}) custom-call(s32[1]{0:T(128)} %bitcast.place_ref, bf16[8,128,128]{2,1,0:T(8,128)(2,1)S(1)} %all-to-all-done.1.blocks_ref, bf16[128,6144]{1,0:T(8,128)(2,1)S(1)} %collective-permute-done.1.rows_ref, ...), custom_call_target="tpu_custom_call", output_to_operand_aliasing={{2}: (6, {})} | custom-call | flops 2818572288 | bytes 22020096 | tf_op jit(solution)/shard_map/turn/pallas_call | solution.py:180
  210.8 11.4 %all_to_all.85.blocks_ref = bf16[8,128,128]{2,1,0:T(8,128)(2,1)S(1)} all-to-all(bf16[8,128,128]{2,1,0:T(8,128)(2,1)S(1)} %copies.19), channel_id=1, replica_groups=mesh['section'=16,'tensor'=8] {'tensor'}, dimensions={0} | all-to-all | bytes 524288 | tf_op jit(solution)/shard_map/all_to_all | solution.py:68
  228.5 14.0 %collective-permute-start.5 = (bf16[128,128]{1,0:T(8,128)(2,1)S(1)}, bf16[128,128]{1,0:T(8,128)(2,1)S(1)}, u32[]{:S(2)}, u32[]{:S(2)}) collective-permute-start(bf16[128,128]{1,0:T(8,128)(2,1)S(1)} %get-tuple-element.84), channel_id=1, source_target_pairs={{0,8},{8,0},{16,24},{24,16},{32,40},{40,32},{48,56},{56,48},{64,72... | collective-permute-start | bytes 98312 | tf_op jit(solution)/shard_map/ppermute | solution.py:47
  243.8 11.8 %all_to_all.86.blocks_ref = bf16[8,128,128]{2,1,0:T(8,128)(2,1)S(1)} all-to-all(bf16[8,128,128]{2,1,0:T(8,128)(2,1)S(1)} %copies.20), channel_id=1, replica_groups=mesh['section'=16,'tensor'=8] {'tensor'}, dimensions={0} | all-to-all | bytes 524288 | tf_op jit(solution)/shard_map/all_to_all | solution.py:68
  255.6 6.3 %turn.17 = (bf16[128,6144]{1,0:T(8,128)(2,1)S(1)}, bf16[128,128]{1,0:T(8,128)(2,1)S(1)}, bf16[128,6144]{1,0:T(8,128)(2,1)S(1)}) custom-call(s32[1]{0:T(128)} %bitcast.place_ref, bf16[8,128,128]{2,1,0:T(8,128)(2,1)S(1)} %all_to_all.86.blocks_ref, bf16[128,6144]{1,0:T(8,128)(2,1)S(1)} %collective-permute-done.6.rows_ref, ...), custom_call_target="tpu_custom_call", output_to_operand_aliasing={{2}: (6, {})} | custom-call | flops 2818572288 | bytes 22020096 | tf_op jit(solution)/shard_map/turn/pallas_call | solution.py:180
  263.4 11.3 %all_to_all.87.blocks_ref = bf16[8,128,128]{2,1,0:T(8,128)(2,1)S(1)} all-to-all(bf16[8,128,128]{2,1,0:T(8,128)(2,1)S(1)} %copies.21), channel_id=1, replica_groups=mesh['section'=16,'tensor'=8] {'tensor'}, dimensions={0} | all-to-all | bytes 524288 | tf_op jit(solution)/shard_map/all_to_all | solution.py:68
  274.7 6.3 %turn.18 = (bf16[128,6144]{1,0:T(8,128)(2,1)S(1)}, bf16[128,128]{1,0:T(8,128)(2,1)S(1)}, bf16[128,6144]{1,0:T(8,128)(2,1)S(1)}) custom-call(s32[1]{0:T(128)} %bitcast.place_ref, bf16[8,128,128]{2,1,0:T(8,128)(2,1)S(1)} %all_to_all.87.blocks_ref, bf16[128,6144]{1,0:T(8,128)(2,1)S(1)} %collective-permute-done.8.rows_ref, ...), custom_call_target="tpu_custom_call", output_to_operand_aliasing={{2}: (6, {})} | custom-call | flops 2818572288 | bytes 22020096 | tf_op jit(solution)/shard_map/turn/pallas_call | solution.py:180
  281.0 14.6 %collective-permute-start.9 = (bf16[128,128]{1,0:T(8,128)(2,1)S(1)}, bf16[128,128]{1,0:T(8,128)(2,1)S(1)}, u32[]{:S(2)}, u32[]{:S(2)}) collective-permute-start(bf16[128,128]{1,0:T(8,128)(2,1)S(1)} %get-tuple-element.94), channel_id=1, source_target_pairs={{0,8},{8,0},{16,24},{24,16},{32,40},{40,32},{48,56},{56,48},{64,72... | collective-permute-start | bytes 98312 | tf_op jit(solution)/shard_map/ppermute | solution.py:47
  296.8 11.8 %all_to_all.88.blocks_ref = bf16[8,128,128]{2,1,0:T(8,128)(2,1)S(1)} all-to-all(bf16[8,128,128]{2,1,0:T(8,128)(2,1)S(1)} %copies.22), channel_id=1, replica_groups=mesh['section'=16,'tensor'=8] {'tensor'}, dimensions={0} | all-to-all | bytes 524288 | tf_op jit(solution)/shard_map/all_to_all | solution.py:68
  308.6 6.3 %turn.19 = (bf16[128,6144]{1,0:T(8,128)(2,1)S(1)}, bf16[128,128]{1,0:T(8,128)(2,1)S(1)}, bf16[128,6144]{1,0:T(8,128)(2,1)S(1)}) custom-call(s32[1]{0:T(128)} %bitcast.place_ref, bf16[8,128,128]{2,1,0:T(8,128)(2,1)S(1)} %all_to_all.88.blocks_ref, bf16[128,6144]{1,0:T(8,128)(2,1)S(1)} %collective-permute-done.10.rows_ref, ...), custom_call_target="tpu_custom_call", output_to_operand_aliasing={{2}: (6, {})} | custom-call | flops 2818572288 | bytes 22020096 | tf_op jit(solution)/shard_map/turn/pallas_call | solution.py:180
  316.4 11.3 %all_to_all.89.blocks_ref = bf16[8,128,128]{2,1,0:T(8,128)(2,1)S(1)} all-to-all(bf16[8,128,128]{2,1,0:T(8,128)(2,1)S(1)} %copies.23), channel_id=1, replica_groups=mesh['section'=16,'tensor'=8] {'tensor'}, dimensions={0} | all-to-all | bytes 524288 | tf_op jit(solution)/shard_map/all_to_all | solution.py:68
  334.0 14.6 %collective-permute-start.13 = (bf16[128,128]{1,0:T(8,128)(2,1)S(1)}, bf16[128,128]{1,0:T(8,128)(2,1)S(1)}, u32[]{:S(2)}, u32[]{:S(2)}) collective-permute-start(bf16[128,128]{1,0:T(8,128)(2,1)S(1)} %get-tuple-element.104), channel_id=1, source_target_pairs={{0,8},{8,0},{16,24},{24,16},{32,40},{40,32},{48,56},{56,48},{64,72... | collective-permute-start | bytes 98312 | tf_op jit(solution)/shard_map/ppermute | solution.py:47
  349.9 12.0 %all_to_all.90.blocks_ref = bf16[8,128,128]{2,1,0:T(8,128)(2,1)S(1)} all-to-all(bf16[8,128,128]{2,1,0:T(8,128)(2,1)S(1)} %copies.24), channel_id=1, replica_groups=mesh['section'=16,'tensor'=8] {'tensor'}, dimensions={0} | all-to-all | bytes 524288 | tf_op jit(solution)/shard_map/all_to_all | solution.py:68
  369.6 11.3 %all_to_all.91.blocks_ref = bf16[8,128,128]{2,1,0:T(8,128)(2,1)S(1)} all-to-all(bf16[8,128,128]{2,1,0:T(8,128)(2,1)S(1)} %copies.25), channel_id=1, replica_groups=mesh['section'=16,'tensor'=8] {'tensor'}, dimensions={0} | all-to-all | bytes 524288 | tf_op jit(solution)/shard_map/all_to_all | solution.py:68
  388.8 14.3 %all_to_all.92.blocks_ref = bf16[8,128,128]{2,1,0:T(8,128)(2,1)S(1)} all-to-all(bf16[8,128,128]{2,1,0:T(8,128)(2,1)S(1)} %copies.26), channel_id=1, replica_groups=mesh['section'=16,'tensor'=8] {'tensor'}, dimensions={0} | all-to-all | bytes 524288 | tf_op jit(solution)/shard_map/all_to_all | solution.py:68
  410.9 12.8 %all_to_all.93.blocks_ref = bf16[8,128,128]{2,1,0:T(8,128)(2,1)S(1)} all-to-all(bf16[8,128,128]{2,1,0:T(8,128)(2,1)S(1)} %copies.27), channel_id=1, replica_groups=mesh['section'=16,'tensor'=8] {'tensor'}, dimensions={0} | all-to-all | bytes 524288 | tf_op jit(solution)/shard_map/all_to_all | solution.py:68
  430.0 12.7 %collective-permute-start.21 = (bf16[128,128]{1,0:T(8,128)(2,1)S(1)}, bf16[128,128]{1,0:T(8,128)(2,1)S(1)}, u32[]{:S(2)}, u32[]{:S(2)}) collective-permute-start(bf16[128,128]{1,0:T(8,128)(2,1)S(1)} %get-tuple-element.124), channel_id=1, source_target_pairs={{0,8},{8,0},{16,24},{24,16},{32,40},{40,32},{48,56},{56,48},{64,72... | collective-permute-start | bytes 98312 | tf_op jit(solution)/shard_map/ppermute | solution.py:47
  444.0 13.2 %all_to_all.94.blocks_ref = bf16[8,128,128]{2,1,0:T(8,128)(2,1)S(1)} all-to-all(bf16[8,128,128]{2,1,0:T(8,128)(2,1)S(1)} %copies.28), channel_id=1, replica_groups=mesh['section'=16,'tensor'=8] {'tensor'}, dimensions={0} | all-to-all | bytes 524288 | tf_op jit(solution)/shard_map/all_to_all | solution.py:68
  465.0 11.3 %all_to_all.95.blocks_ref = bf16[8,128,128]{2,1,0:T(8,128)(2,1)S(1)} all-to-all(bf16[8,128,128]{2,1,0:T(8,128)(2,1)S(1)} %copies.29), channel_id=1, replica_groups=mesh['section'=16,'tensor'=8] {'tensor'}, dimensions={0} | all-to-all | bytes 524288 | tf_op jit(solution)/shard_map/all_to_all | solution.py:68
  482.6 13.5 %collective-permute-start.25 = (bf16[128,128]{1,0:T(8,128)(2,1)S(1)}, bf16[128,128]{1,0:T(8,128)(2,1)S(1)}, u32[]{:S(2)}, u32[]{:S(2)}) collective-permute-start(bf16[128,128]{1,0:T(8,128)(2,1)S(1)} %get-tuple-element.134), channel_id=1, source_target_pairs={{0,8},{8,0},{16,24},{24,16},{32,40},{40,32},{48,56},{56,48},{64,72... | collective-permute-start | bytes 98312 | tf_op jit(solution)/shard_map/ppermute | solution.py:47
  497.4 11.8 %all_to_all.96.blocks_ref = bf16[8,128,128]{2,1,0:T(8,128)(2,1)S(1)} all-to-all(bf16[8,128,128]{2,1,0:T(8,128)(2,1)S(1)} %copies.30), channel_id=1, replica_groups=mesh['section'=16,'tensor'=8] {'tensor'}, dimensions={0} | all-to-all | bytes 524288 | tf_op jit(solution)/shard_map/all_to_all | solution.py:68
  517.0 11.3 %all_to_all.97.blocks_ref = bf16[8,128,128]{2,1,0:T(8,128)(2,1)S(1)} all-to-all(bf16[8,128,128]{2,1,0:T(8,128)(2,1)S(1)} %copies.31), channel_id=1, replica_groups=mesh['section'=16,'tensor'=8] {'tensor'}, dimensions={0} | all-to-all | bytes 524288 | tf_op jit(solution)/shard_map/all_to_all | solution.py:68
  528.3 6.9 %turn.28 = (bf16[128,6144]{1,0:T(8,128)(2,1)}, bf16[128,128]{1,0:T(8,128)(2,1)S(1)}, bf16[128,6144]{1,0:T(8,128)(2,1)S(1)}) custom-call(s32[1]{0:T(128)} %bitcast.place_ref, bf16[8,128,128]{2,1,0:T(8,128)(2,1)S(1)} %all_to_all.97.blocks_ref, bf16[128,6144]{1,0:T(8,128)(2,1)S(1)} %collective-permute-done.28.rows_ref, ...), custom_call_target="tpu_custom_call", output_to_operand_aliasing={{2}: (6, {})} | custom-call | flops 2818572288 | bytes 22020096 | tf_op jit(solution)/shard_map/turn/pallas_call | solution.py:180
  535.2 32.7 %collective-permute-start.29 = (bf16[128,128]{1,0:T(8,128)(2,1)S(1)}, bf16[128,128]{1,0:T(8,128)(2,1)S(1)}, u32[]{:S(2)}, u32[]{:S(2)}) collective-permute-start(bf16[128,128]{1,0:T(8,128)(2,1)S(1)} %get-tuple-element.144), channel_id=1, source_target_pairs={{0,8},{8,0},{16,24},{24,16},{32,40},{40,32},{48,56},{56,48},{64,72... | collective-permute-start | bytes 98312 | tf_op jit(solution)/shard_map/ppermute | solution.py:47
  575.6 7.0 %all-to-all-done.15.blocks_ref = bf16[8,128,128]{2,1,0:T(8,128)(2,1)S(1)} async-done(((bf16[8,128,128]{2,1,0:T(8,128)(2,1)}), bf16[8,128,128]{2,1,0:T(8,128)(2,1)S(1)}, u32[]{:S(2)}, u32[]{:S(2)}) %all-to-all-start.15) | async-done | bytes 262176 | tf_op jit(solution)/shard_map/all_to_all | solution.py:68
  590.8 7.0 %turn.29 = (bf16[128,6144]{1,0:T(8,128)(2,1)}, bf16[128,128]{1,0:T(8,128)(2,1)S(1)}, bf16[128,6144]{1,0:T(8,128)(2,1)S(1)}) custom-call(s32[1]{0:T(128)} %bitcast.place_ref, bf16[8,128,128]{2,1,0:T(8,128)(2,1)S(1)} %all-to-all-done.15.blocks_ref, bf16[128,6144]{1,0:T(8,128)(2,1)S(1)} %collective-permute-done.30.rows_ref, ...), custom_call_target="tpu_custom_call", output_to_operand_aliasing={{2}: (6, {})} | custom-call | flops 2818572288 | bytes 22020096 | tf_op jit(solution)/shard_map/turn/pallas_call | solution.py:180
  (147 shorter events, 147.7 us)
Async XLA Ops:
  7.2 187.6 %all-gather.3.cloned.1.call-start = ((), (), s32[]{:S(2)}) async-start(), calls=%async_computation.17 | async-start | bytes 14155776 | tf_op jit(solution)/shard_map/all_gather | solution.py:227
  9.3 21.9 %collective-permute-start.2 = (bf16[1024,768]{1,0:T(8,128)(2,1)S(1)}, bf16[1024,768]{1,0:T(8,128)(2,1)S(1)}, u32[]{:S(2)}, u32[]{:S(2)}) collective-permute-start(bf16[1024,768]{1,0:T(8,128)(2,1)S(1)} %transposed.3), channel_id=1, source_target_pairs={{0,120},{8,0},{16,8},{24,16},{32,24},{40,32},{48,40},{56,48},{64,5... | collective-permute-start | bytes 4718600 | tf_op jit(solution)/shard_map/ppermute | solution.py:31
  33.6 37.1 %all-to-all-start = ((bf16[8,128,768]{2,1,0:T(8,128)(2,1)}), bf16[8,128,768]{2,1,0:T(8,128)(2,1)S(1)}, u32[]{:S(2)}, u32[]{:S(2)}) async-start(bf16[8,128,768]{2,1,0:T(8,128)(2,1)} %copies.17), calls=%async_computation | async-start | bytes 3145728 | tf_op jit(solution)/shard_map/all_to_all | solution.py:68
  76.9 1.3 collective-permute-start
  78.2 18.0 %collective-permute-start.1 = (bf16[128,6144]{1,0:T(8,128)(2,1)S(1)}, bf16[128,6144]{1,0:T(8,128)(2,1)S(1)}, u32[]{:S(2)}, u32[]{:S(2)}) collective-permute-start(bf16[128,6144]{1,0:T(8,128)(2,1)S(1)} %bitcast.75), channel_id=1, source_target_pairs={{0,8},{8,0},{16,24},{24,16},{32,40},{40,32},{48,56},{56,48},{64,72... | collective-permute-start | bytes 4718600 | tf_op jit(solution)/shard_map/ppermute | solution.py:47
  79.1 17.1 %all-to-all-start.1 = ((bf16[8,128,128]{2,1,0:T(8,128)(2,1)}), bf16[8,128,128]{2,1,0:T(8,128)(2,1)S(1)}, u32[]{:S(2)}, u32[]{:S(2)}) async-start(bf16[8,128,128]{2,1,0:T(8,128)(2,1)} %copy-done.12), calls=%async_computation.1 | async-start | bytes 524288 | tf_op jit(solution)/shard_map/all_to_all | solution.py:68
  209.3 0.7 collective-permute-start.3
  210.0 12.2 %collective-permute-start.4 = (bf16[128,6144]{1,0:T(8,128)(2,1)S(1)}, bf16[128,6144]{1,0:T(8,128)(2,1)S(1)}, u32[]{:S(2)}, u32[]{:S(2)}) collective-permute-start(bf16[128,6144]{1,0:T(8,128)(2,1)S(1)} %get-tuple-element.81), channel_id=1, source_target_pairs={{0,0},{8,16},{16,8},{24,32},{32,24},{40,48},{48,40},{56,56},{64,64... | collective-permute-start | bytes 4718600 | tf_op jit(solution)/shard_map/ppermute | solution.py:47
  228.5 14.9 %collective-permute-start.5 = (bf16[128,128]{1,0:T(8,128)(2,1)S(1)}, bf16[128,128]{1,0:T(8,128)(2,1)S(1)}, u32[]{:S(2)}, u32[]{:S(2)}) collective-permute-start(bf16[128,128]{1,0:T(8,128)(2,1)S(1)} %get-tuple-element.84), channel_id=1, source_target_pairs={{0,8},{8,0},{16,24},{24,16},{32,40},{40,32},{48,56},{56,48},{64,72... | collective-permute-start | bytes 98312 | tf_op jit(solution)/shard_map/ppermute | solution.py:47
  243.4 12.2 %collective-permute-start.6 = (bf16[128,6144]{1,0:T(8,128)(2,1)S(1)}, bf16[128,6144]{1,0:T(8,128)(2,1)S(1)}, u32[]{:S(2)}, u32[]{:S(2)}) collective-permute-start(bf16[128,6144]{1,0:T(8,128)(2,1)S(1)} %get-tuple-element.86), channel_id=1, source_target_pairs={{0,8},{8,0},{16,24},{24,16},{32,40},{40,32},{48,56},{56,48},{64,72... | collective-permute-start | bytes 4718600 | tf_op jit(solution)/shard_map/ppermute | solution.py:47
  262.6 12.1 %collective-permute-start.8 = (bf16[128,6144]{1,0:T(8,128)(2,1)S(1)}, bf16[128,6144]{1,0:T(8,128)(2,1)S(1)}, u32[]{:S(2)}, u32[]{:S(2)}) collective-permute-start(bf16[128,6144]{1,0:T(8,128)(2,1)S(1)} %get-tuple-element.91), channel_id=1, source_target_pairs={{0,0},{8,16},{16,8},{24,32},{32,24},{40,48},{48,40},{56,56},{64,64... | collective-permute-start | bytes 4718600 | tf_op jit(solution)/shard_map/ppermute | solution.py:47
  281.0 15.4 %collective-permute-start.9 = (bf16[128,128]{1,0:T(8,128)(2,1)S(1)}, bf16[128,128]{1,0:T(8,128)(2,1)S(1)}, u32[]{:S(2)}, u32[]{:S(2)}) collective-permute-start(bf16[128,128]{1,0:T(8,128)(2,1)S(1)} %get-tuple-element.94), channel_id=1, source_target_pairs={{0,8},{8,0},{16,24},{24,16},{32,40},{40,32},{48,56},{56,48},{64,72... | collective-permute-start | bytes 98312 | tf_op jit(solution)/shard_map/ppermute | solution.py:47
  296.4 12.2 %collective-permute-start.10 = (bf16[128,6144]{1,0:T(8,128)(2,1)S(1)}, bf16[128,6144]{1,0:T(8,128)(2,1)S(1)}, u32[]{:S(2)}, u32[]{:S(2)}) collective-permute-start(bf16[128,6144]{1,0:T(8,128)(2,1)S(1)} %get-tuple-element.96), channel_id=1, source_target_pairs={{0,8},{8,0},{16,24},{24,16},{32,40},{40,32},{48,56},{56,48},{64,72... | collective-permute-start | bytes 4718600 | tf_op jit(solution)/shard_map/ppermute | solution.py:47
  315.6 12.1 %collective-permute-start.12 = (bf16[128,6144]{1,0:T(8,128)(2,1)S(1)}, bf16[128,6144]{1,0:T(8,128)(2,1)S(1)}, u32[]{:S(2)}, u32[]{:S(2)}) collective-permute-start(bf16[128,6144]{1,0:T(8,128)(2,1)S(1)} %get-tuple-element.101), channel_id=1, source_target_pairs={{0,0},{8,16},{16,8},{24,32},{32,24},{40,48},{48,40},{56,56},{64,64... | collective-permute-start | bytes 4718600 | tf_op jit(solution)/shard_map/ppermute | solution.py:47
  334.0 15.4 %collective-permute-start.13 = (bf16[128,128]{1,0:T(8,128)(2,1)S(1)}, bf16[128,128]{1,0:T(8,128)(2,1)S(1)}, u32[]{:S(2)}, u32[]{:S(2)}) collective-permute-start(bf16[128,128]{1,0:T(8,128)(2,1)S(1)} %get-tuple-element.104), channel_id=1, source_target_pairs={{0,8},{8,0},{16,24},{24,16},{32,40},{40,32},{48,56},{56,48},{64,72... | collective-permute-start | bytes 98312 | tf_op jit(solution)/shard_map/ppermute | solution.py:47
  349.5 12.4 %collective-permute-start.14 = (bf16[128,6144]{1,0:T(8,128)(2,1)S(1)}, bf16[128,6144]{1,0:T(8,128)(2,1)S(1)}, u32[]{:S(2)}, u32[]{:S(2)}) collective-permute-start(bf16[128,6144]{1,0:T(8,128)(2,1)S(1)} %get-tuple-element.106), channel_id=1, source_target_pairs={{0,8},{8,0},{16,24},{24,16},{32,40},{40,32},{48,56},{56,48},{64,72... | collective-permute-start | bytes 4718600 | tf_op jit(solution)/shard_map/ppermute | solution.py:47
  368.8 12.2 %collective-permute-start.16 = (bf16[128,6144]{1,0:T(8,128)(2,1)S(1)}, bf16[128,6144]{1,0:T(8,128)(2,1)S(1)}, u32[]{:S(2)}, u32[]{:S(2)}) collective-permute-start(bf16[128,6144]{1,0:T(8,128)(2,1)S(1)} %get-tuple-element.111), channel_id=1, source_target_pairs={{0,0},{8,8},{16,16},{24,24},{32,32},{40,40},{48,48},{56,64},{64,56... | collective-permute-start | bytes 4718600 | tf_op jit(solution)/shard_map/ppermute | solution.py:47
  387.3 1.3 collective-permute-start.17
  388.6 14.5 %collective-permute-start.18 = (bf16[128,6144]{1,0:T(8,128)(2,1)S(1)}, bf16[128,6144]{1,0:T(8,128)(2,1)S(1)}, u32[]{:S(2)}, u32[]{:S(2)}) collective-permute-start(bf16[128,6144]{1,0:T(8,128)(2,1)S(1)} %get-tuple-element.116), channel_id=1, source_target_pairs={{0,8},{8,0},{16,24},{24,16},{32,40},{40,32},{48,56},{56,48},{64,72... | collective-permute-start | bytes 4718600 | tf_op jit(solution)/shard_map/ppermute | solution.py:47
  410.0 13.7 %collective-permute-start.20 = (bf16[128,6144]{1,0:T(8,128)(2,1)S(1)}, bf16[128,6144]{1,0:T(8,128)(2,1)S(1)}, u32[]{:S(2)}, u32[]{:S(2)}) collective-permute-start(bf16[128,6144]{1,0:T(8,128)(2,1)S(1)} %get-tuple-element.121), channel_id=1, source_target_pairs={{0,0},{8,16},{16,8},{24,32},{32,24},{40,48},{48,40},{56,56},{64,64... | collective-permute-start | bytes 4718600 | tf_op jit(solution)/shard_map/ppermute | solution.py:47
  430.0 13.6 %collective-permute-start.21 = (bf16[128,128]{1,0:T(8,128)(2,1)S(1)}, bf16[128,128]{1,0:T(8,128)(2,1)S(1)}, u32[]{:S(2)}, u32[]{:S(2)}) collective-permute-start(bf16[128,128]{1,0:T(8,128)(2,1)S(1)} %get-tuple-element.124), channel_id=1, source_target_pairs={{0,8},{8,0},{16,24},{24,16},{32,40},{40,32},{48,56},{56,48},{64,72... | collective-permute-start | bytes 98312 | tf_op jit(solution)/shard_map/ppermute | solution.py:47
  443.6 13.5 %collective-permute-start.22 = (bf16[128,6144]{1,0:T(8,128)(2,1)S(1)}, bf16[128,6144]{1,0:T(8,128)(2,1)S(1)}, u32[]{:S(2)}, u32[]{:S(2)}) collective-permute-start(bf16[128,6144]{1,0:T(8,128)(2,1)S(1)} %get-tuple-element.126), channel_id=1, source_target_pairs={{0,8},{8,0},{16,24},{24,16},{32,40},{40,32},{48,56},{56,48},{64,72... | collective-permute-start | bytes 4718600 | tf_op jit(solution)/shard_map/ppermute | solution.py:47
  463.5 0.7 collective-permute-start.23
  464.1 12.1 %collective-permute-start.24 = (bf16[128,6144]{1,0:T(8,128)(2,1)S(1)}, bf16[128,6144]{1,0:T(8,128)(2,1)S(1)}, u32[]{:S(2)}, u32[]{:S(2)}) collective-permute-start(bf16[128,6144]{1,0:T(8,128)(2,1)S(1)} %get-tuple-element.131), channel_id=1, source_target_pairs={{0,0},{8,16},{16,8},{24,32},{32,24},{40,48},{48,40},{56,56},{64,64... | collective-permute-start | bytes 4718600 | tf_op jit(solution)/shard_map/ppermute | solution.py:47
  482.6 14.4 %collective-permute-start.25 = (bf16[128,128]{1,0:T(8,128)(2,1)S(1)}, bf16[128,128]{1,0:T(8,128)(2,1)S(1)}, u32[]{:S(2)}, u32[]{:S(2)}) collective-permute-start(bf16[128,128]{1,0:T(8,128)(2,1)S(1)} %get-tuple-element.134), channel_id=1, source_target_pairs={{0,8},{8,0},{16,24},{24,16},{32,40},{40,32},{48,56},{56,48},{64,72... | collective-permute-start | bytes 98312 | tf_op jit(solution)/shard_map/ppermute | solution.py:47
  497.0 12.2 %collective-permute-start.26 = (bf16[128,6144]{1,0:T(8,128)(2,1)S(1)}, bf16[128,6144]{1,0:T(8,128)(2,1)S(1)}, u32[]{:S(2)}, u32[]{:S(2)}) collective-permute-start(bf16[128,6144]{1,0:T(8,128)(2,1)S(1)} %get-tuple-element.136), channel_id=1, source_target_pairs={{0,8},{8,0},{16,24},{24,16},{32,40},{40,32},{48,56},{56,48},{64,72... | collective-permute-start | bytes 4718600 | tf_op jit(solution)/shard_map/ppermute | solution.py:47
  516.2 12.1 %collective-permute-start.28 = (bf16[128,6144]{1,0:T(8,128)(2,1)S(1)}, bf16[128,6144]{1,0:T(8,128)(2,1)S(1)}, u32[]{:S(2)}, u32[]{:S(2)}) collective-permute-start(bf16[128,6144]{1,0:T(8,128)(2,1)S(1)} %get-tuple-element.141), channel_id=1, source_target_pairs={{0,0},{8,16},{16,8},{24,32},{32,24},{40,48},{48,40},{56,56},{64,64... | collective-permute-start | bytes 4718600 | tf_op jit(solution)/shard_map/ppermute | solution.py:47
  535.2 33.5 %collective-permute-start.29 = (bf16[128,128]{1,0:T(8,128)(2,1)S(1)}, bf16[128,128]{1,0:T(8,128)(2,1)S(1)}, u32[]{:S(2)}, u32[]{:S(2)}) collective-permute-start(bf16[128,128]{1,0:T(8,128)(2,1)S(1)} %get-tuple-element.144), channel_id=1, source_target_pairs={{0,8},{8,0},{16,24},{24,16},{32,40},{40,32},{48,56},{56,48},{64,72... | collective-permute-start | bytes 98312 | tf_op jit(solution)/shard_map/ppermute | solution.py:47
  568.7 13.8 %collective-permute-start.30 = (bf16[128,6144]{1,0:T(8,128)(2,1)}, bf16[128,6144]{1,0:T(8,128)(2,1)S(1)}, u32[]{:S(2)}, u32[]{:S(2)}) collective-permute-start(bf16[128,6144]{1,0:T(8,128)(2,1)} %get-tuple-element.146), channel_id=1, source_target_pairs={{0,8},{8,0},{16,24},{24,16},{32,40},{40,32},{48,56},{56,48},{64,72... | collective-permute-start | bytes 4718600 | tf_op jit(solution)/shard_map/ppermute | solution.py:47
  569.8 12.7 %all-to-all-start.15 = ((bf16[8,128,128]{2,1,0:T(8,128)(2,1)}), bf16[8,128,128]{2,1,0:T(8,128)(2,1)S(1)}, u32[]{:S(2)}, u32[]{:S(2)}) async-start(bf16[8,128,128]{2,1,0:T(8,128)(2,1)} %copy-done.11), calls=%async_computation.15 | async-start | bytes 524288 | tf_op jit(solution)/shard_map/all_to_all | solution.py:68
  598.6 16.4 %collective-permute-start.31 = (bf16[128,768]{1,0:T(8,128)(2,1)}, bf16[128,768]{1,0:T(8,128)(2,1)}, u32[]{:S(2)}, u32[]{:S(2)}) collective-permute-start(bf16[128,768]{1,0:T(8,128)(2,1)} %constant_dynamic-slice_fusion), channel_id=1, source_target_pairs={{0,8},{8,16},{16,24},{24,32},{32,40},{40,48},{48,56},{56,64},{64,7... | collective-permute-start | bytes 589832 | tf_op jit(solution)/shard_map/ppermute | solution.py:31
  599.3 13.2 %all-to-all-start.16 = ((bf16[8,128,128]{2,1,0:T(8,128)(2,1)}), bf16[8,128,128]{2,1,0:T(8,128)(2,1)S(1)}, u32[]{:S(2)}, u32[]{:S(2)}) async-start(bf16[8,128,128]{2,1,0:T(8,128)(2,1)} %copies.33), calls=%async_computation.16 | async-start | bytes 524288 | tf_op jit(solution)/shard_map/all_to_all | solution.py:68
  (25 other events, 682.7 us)
Sparse Core Ops, SparseCore 0:
  32.5 162.2 all-gather.2

commit v4 on v3

--- a/solution.py
+++ b/solution.py
@@ -11,8 +11,6 @@
 F32 = jnp.float32
 BF16 = jnp.bfloat16
 NN = (((1,), (0,)), ((), ()))
-NT = (((1,), (1,)), ((), ()))
-TN = (((0,), (0,)), ((), ()))
 
 
 def causal_probs(query_heads, key_rows):
@@ -72,20 +70,93 @@
     out_ref[...] = value_ref[...].T
 
 
-def transposed(value, tile=512):
+def transposed(value, tile=512, first=0, count=None):
     rows, columns = value.shape
+    count = columns // tile if count is None else count
     return pl.pallas_call(
         transpose_kernel,
-        grid=(columns // tile,),
-        in_specs=[pl.BlockSpec((rows, tile), lambda i: (0, i))],
+        grid=(count,),
+        in_specs=[pl.BlockSpec((rows, tile), lambda i: (0, i + first))],
         out_specs=pl.BlockSpec((tile, rows), lambda i: (i, 0)),
-        out_shape=jax.ShapeDtypeStruct((columns, rows), value.dtype),
+        out_shape=jax.ShapeDtypeStruct((count * tile, rows), value.dtype),
         compiler_params=pltpu.CompilerParams(vmem_limit_bytes=12 << 20),
         cost_estimate=pl.CostEstimate(
-            flops=0, bytes_accessed=4 * rows * columns, transcendentals=0
+            flops=0, bytes_accessed=4 * rows * count * tile, transcendentals=0
         ),
         name="transposed",
     )(value)
+
+
+def place_kernel(spots, given, index_ref, *refs):
+    pieces, out_ref, sems = refs[:given], refs[-2], refs[-1]
+    copies = []
+    for i, (piece, (slot, row)) in enumerate(zip(pieces, spots)):
+        goal = out_ref.at[index_ref[slot], pl.ds(row, piece.shape[0])]
+        copies.append(pltpu.make_async_copy(piece, goal, sems.at[i]))
+    for copy in copies:
+        copy.start()
+    for copy in copies:
+        copy.wait()
+
+
+def put(index, pieces, shape, whole=None):
+    arrays = [piece[0] for piece in pieces]
+    spots = [piece[1:] for piece in pieces]
+    more = [] if whole is None else [whole]
+    return pl.pallas_call(
+        functools.partial(place_kernel, spots, len(arrays)),
+        in_specs=[pl.BlockSpec(memory_space=pltpu.SMEM)]
+        + [pl.BlockSpec(memory_space=pl.ANY)] * (len(arrays) + len(more)),
+        out_specs=pl.BlockSpec(memory_space=pl.ANY),
+        out_shape=jax.ShapeDtypeStruct(shape, arrays[0].dtype),
+        scratch_shapes=[pltpu.SemaphoreType.DMA((len(arrays),))],
+        input_output_aliases={1 + len(arrays): 0} if more else {},
+        compiler_params=pltpu.CompilerParams(vmem_limit_bytes=1 << 20),
+        cost_estimate=pl.CostEstimate(
+            flops=0,
+            bytes_accessed=4 * sum(math.prod(array.shape) for array in arrays),
+            transcendentals=0,
+        ),
+        name="put",
+    )(index, *arrays, *more)
+
+
+def across(value, x_by=0, z_by=0):
+    length = lax.axis_size("tensor")
+    xs = length // 2
+    pairs = []
+    for i in range(length):
+        z, x = divmod(i, xs)
+        pairs.append((i, (z + z_by) % 2 * xs + (x + x_by) % xs))
+    return lax.ppermute(value, "tensor", pairs)
+
+
+def gather_back(index, whole, halves, beside):
+    n, k = whole.shape
+    half = n // 2
+    low, high = halves
+    other = across(whole, 0, 1)
+    left_low, right_low = across(low, 1), across(low, -1)
+    left_high, right_high = across(high, 1), across(high, -1)
+    first = (other, left_low, right_low, left_high, right_high)
+    first, beside = lax.optimization_barrier((first, beside))
+    other, left_low, right_low, left_high, right_high = first
+    cross_left, cross_right = across(left_high, 0, 1), across(right_high, 0, 1)
+    far_high, far_low = across(right_high, -1), across(left_low, 1)
+    next_left, next_right = across(other[:half], 1), across(other[:half], -1)
+    early = [
+        (whole, 0, 0), (left_low, 1, 0), (left_high, 1, half),
+        (right_low, 2, 0), (right_high, 2, half), (other, 4, 0),
+    ]
+    late = [
+        (far_low, 3, 0), (far_high, 3, half),
+        (next_left, 5, 0), (cross_left, 5, half), (next_right, 6, 0), (cross_right, 6, half),
+        (across(next_left, 1), 7, 0), (across(far_high, 0, 1), 7, half),
+    ]
+    shape = (lax.axis_size("tensor"), n, k)
+    whole, far_high = lax.optimization_barrier((whole, far_high))
+    early[0], late[1] = (whole, 0, 0), (far_high, 3, half)
+    return put(index, late, shape, put(index, early, shape)), beside
 
 
 def value_grad_of(total, probs_t_ref, value_ref):
@@ -102,14 +173,27 @@
         ).astype(BF16)
 
 
-def first_kernel(steps, rows_ref, weight_ref, probs_t_ref, value_ref, total):
+def keep(step, block, saved_ref, sem):
+    copy = pltpu.make_async_copy(block, saved_ref.at[step], sem)
+    copy.start()
+    copy.wait()
+
+
+def plain_kernel(
+    steps, section, place_ref, rows_ref, weight_ref, probs_t_ref, kept_ref,
+    value_ref, saved_ref, total, sem,
+):
     step = pl.program_id(0)
 
     @pl.when(step == 0)
     def _():
         total[...] = jnp.zeros_like(total)
 
-    total[...] += lax.dot_general(rows_ref[...], weight_ref[...], NN, preferred_element_type=F32)
+    total[...] += lax.dot_general(rows_ref[0], weight_ref[...], NN, preferred_element_type=F32)
+
+    @pl.when(place_ref[0] == section)
+    def _():
+        keep(step, rows_ref.at[0], saved_ref, sem)
 
     @pl.when(step == steps - 1)
     def _():
@@ -130,50 +214,59 @@
         total[...] = jnp.zeros_like(total)
 
     branch = lax.dot_general(heads[...], back_ref[0], NN, preferred_element_type=F32)
-    new_rows = (rows_ref[...].astype(F32) + branch).astype(BF16)
-    new_ref[...] = new_rows
+    new_rows = (rows_ref[0].astype(F32) + branch).astype(BF16)
+    new_ref[0] = new_rows
     total[...] += lax.dot_general(new_rows, weight_ref[...], NN, preferred_element_type=F32)
 
     @pl.when(place_ref[0] == section)
     def _():
-        width = new_ref.shape[1]
-        spot = pl.ds(pl.multiple_of(step * width, width), width)
-        copy = pltpu.make_async_copy(new_ref, saved_ref.at[:, spot], sem)
-        copy.start()
-        copy.wait()
+        keep(step, new_ref.at[0], saved_ref, sem)
 
     @pl.when(step == steps - 1)
     def _():
         value_grad_of(total[...], probs_t_ref, value_ref)
 
 
-def first_value_grad(rows, weight_t, probs_t):
-    count, width = rows.shape
+def params():
+    return pltpu.CompilerParams(vmem_limit_bytes=16 << 20)
+
+
+def plain_turn(section, place, rows, weight_t, probs_t, saved):
+    steps, count, tile = rows.shape
     own = weight_t.shape[1]
-    steps = 4
-    tile = width // steps
     head_size = 128
     return pl.pallas_call(
-        functools.partial(first_kernel, steps),
+        functools.partial(plain_kernel, steps, section),
         grid=(steps,),
         in_specs=[
-            pl.BlockSpec((count, tile), lambda i: (0, i)),
+            pl.BlockSpec(memory_space=pltpu.SMEM),
+            pl.BlockSpec((1, count, tile), lambda i: (i, 0, 0)),
             pl.BlockSpec((tile, own), lambda i: (i, 0)),
             pl.BlockSpec(probs_t.shape, lambda i: (0, 0, 0)),
-        ],
-        out_specs=pl.BlockSpec((count, head_size), lambda i: (0, 0)),
-        out_shape=jax.ShapeDtypeStruct((count, head_size), BF16),
-        scratch_shapes=[pltpu.VMEM((count, own), F32)],
-        compiler_params=pltpu.CompilerParams(vmem_limit_bytes=16 << 20),
-        cost_estimate=pl.CostEstimate(
-            flops=2 * count * width * own, bytes_accessed=2 * width * own, transcendentals=0
-        ),
-        name="first_turn",
-    )(rows, weight_t, probs_t)
+            pl.BlockSpec(memory_space=pl.ANY),
+        ],
+        out_specs=[
+            pl.BlockSpec((count, head_size), lambda i: (0, 0)),
+            pl.BlockSpec(memory_space=pl.ANY),
+        ],
+        out_shape=[
+            jax.ShapeDtypeStruct((count, head_size), BF16),
+            jax.ShapeDtypeStruct(saved.shape, BF16),
+        ],
+        scratch_shapes=[pltpu.VMEM((count, own), F32), pltpu.SemaphoreType.DMA],
+        input_output_aliases={4: 1},
+        compiler_params=params(),
+        cost_estimate=pl.CostEstimate(
+            flops=2 * steps * count * tile * own,
+            bytes_accessed=2 * steps * tile * own,
+            transcendentals=0,
+        ),
+        name="plain_turn",
+    )(place, rows, weight_t, probs_t, saved)
 
 
 def turn(section, place, blocks, rows, back, weight_t, probs_t, saved):
-    count, width = rows.shape
+    count = rows.shape[1]
     own = weight_t.shape[1]
     steps, depth, tile = back.shape
     head_size = blocks.shape[2]
@@ -183,21 +276,21 @@
         in_specs=[
             pl.BlockSpec(memory_space=pltpu.SMEM),
             pl.BlockSpec(blocks.shape, lambda i: (0, 0, 0)),
-            pl.BlockSpec((count, tile), lambda i: (0, i)),
+            pl.BlockSpec((1, count, tile), lambda i: (i, 0, 0)),
             pl.BlockSpec((1, depth, tile), lambda i: (i, 0, 0)),
             pl.BlockSpec((tile, own), lambda i: (i, 0)),
             pl.BlockSpec(probs_t.shape, lambda i: (0, 0, 0)),
             pl.BlockSpec(memory_space=pl.ANY),
         ],
         out_specs=[
-            pl.BlockSpec((count, tile), lambda i: (0, i)),
+            pl.BlockSpec((1, count, tile), lambda i: (i, 0, 0)),
             pl.BlockSpec((count, head_size), lambda i: (0, 0)),
             pl.BlockSpec(memory_space=pl.ANY),
         ],
         out_shape=[
             jax.ShapeDtypeStruct(rows.shape, BF16),
             jax.ShapeDtypeStruct((count, head_size), BF16),
-            jax.ShapeDtypeStruct(rows.shape, BF16),
+            jax.ShapeDtypeStruct(saved.shape, BF16),
         ],
         scratch_shapes=[
             pltpu.VMEM((count, depth), BF16),
@@ -205,14 +298,103 @@
             pltpu.SemaphoreType.DMA,
         ],
         input_output_aliases={6: 2},
-        compiler_params=pltpu.CompilerParams(vmem_limit_bytes=16 << 20),
-        cost_estimate=pl.CostEstimate(
-            flops=2 * count * width * (own + depth),
-            bytes_accessed=2 * width * (own + depth),
+        compiler_params=params(),
+        cost_estimate=pl.CostEstimate(
+            flops=2 * steps * count * tile * (own + depth),
+            bytes_accessed=2 * steps * tile * (own + depth),
             transcendentals=0,
         ),
         name="turn",
     )(place, blocks, rows, back, weight_t, probs_t, saved)
+
+
+def pick_kernel(me_ref, rows_ref, out_ref):
+    out_ref[...] = rows_ref[0]
+
+
+def pick(me, rows):
+    _, count, tile = rows.shape
+    return pl.pallas_call(
+        pick_kernel,
+        grid_spec=pltpu.PrefetchScalarGridSpec(
+            num_scalar_prefetch=1,
+            grid=(1,),
+            in_specs=[pl.BlockSpec((1, count, tile), lambda i, me: (me[0], 0, 0))],
+            out_specs=pl.BlockSpec((count, tile), lambda i, me: (0, 0)),
+        ),
+        out_shape=jax.ShapeDtypeStruct((count, tile), rows.dtype),
+        compiler_params=pltpu.CompilerParams(vmem_limit_bytes=4 << 20),
+        name="pick",
+    )(me, rows)
+
+
+def last_kernel(place_ref, me_ref, blocks_ref, rows_ref, value_t_ref, above_ref, out_ref, heads):
+    head_size = blocks_ref.shape[2]
+
+    @pl.when(place_ref[0] == 0)
+    def _():
+        for c in range(blocks_ref.shape[0]):
+            heads[:, c * head_size : (c + 1) * head_size] = blocks_ref[c]
+        branch = lax.dot_general(heads[...], value_t_ref[...], NN, preferred_element_type=F32)
+        out_ref[...] = (rows_ref[0].astype(F32) + branch).astype(BF16)
+
+    @pl.when(place_ref[0] != 0)
+    def _():
+        out_ref[...] = above_ref[...]
+
+
+def last_features(place, me, blocks, rows, value_t, above):
+    _, count, tile = rows.shape
+    depth = value_t.shape[0]
+    return pl.pallas_call(
+        last_kernel,
+        grid_spec=pltpu.PrefetchScalarGridSpec(
+            num_scalar_prefetch=2,
+            grid=(1,),
+            in_specs=[
+                pl.BlockSpec(blocks.shape, lambda i, place, me: (0, 0, 0)),
+                pl.BlockSpec((1, count, tile), lambda i, place, me: (me[0], 0, 0)),
+                pl.BlockSpec(value_t.shape, lambda i, place, me: (0, 0)),
+                pl.BlockSpec((count, tile), lambda i, place, me: (0, 0)),
+            ],
+            out_specs=pl.BlockSpec((count, tile), lambda i, place, me: (0, 0)),
+            scratch_shapes=[pltpu.VMEM((count, depth), BF16)],
+        ),
+        out_shape=jax.ShapeDtypeStruct((count, tile), BF16),
+        compiler_params=params(),
+        cost_estimate=pl.CostEstimate(
+            flops=2 * count * tile * depth, bytes_accessed=2 * tile * depth, transcendentals=0
+        ),
+        name="last_features",
+    )(place, me, blocks, rows, value_t, above)
+
+
+def weight_kernel(mixed_t_ref, rows_ref, out_ref):
+    out_ref[...] = lax.dot_general(
+        mixed_t_ref[...], rows_ref[0], NN, preferred_element_type=F32
+    ).astype(BF16)
+
+
+def weight_grads(mixed_t, rows):
+    steps, count, tile = rows.shape
+    own = mixed_t.shape[0]
+    return pl.pallas_call(
+        weight_kernel,
+        grid=(steps,),
+        in_specs=[
+            pl.BlockSpec((own, count), lambda i: (0, 0)),
+            pl.BlockSpec((1, count, tile), lambda i: (i, 0, 0)),
+        ],
+        out_specs=pl.BlockSpec((own, tile), lambda i: (0, i)),
+        out_shape=jax.ShapeDtypeStruct((own, steps * tile), BF16),
+        compiler_params=params(),
+        cost_estimate=pl.CostEstimate(
+            flops=2 * steps * count * tile * own,
+            bytes_accessed=2 * steps * tile * own,
+            transcendentals=0,
+        ),
+        name="weight_grads",
+    )(mixed_t, rows)
 
 
 def on_device(grad_top, query, keys, values, out_weight, value_weight):
@@ -224,18 +406,39 @@
     head_size = keys.shape[3]
     group = query.shape[3] // head_size
     feat_local = grad_top.shape[2]
-    back = lax.all_gather(shift(transposed(value_weight[0]), "section", -1), "tensor", axis=0)
-    top = blocks_of_all(grad_top.reshape(rows, feat_local))
-    incoming = top.transpose(1, 0, 2).reshape(rows, top.shape[0] * feat_local)
+    spot = place.astype(jnp.int32).reshape(1)
+    mine = me.astype(jnp.int32).reshape(1)
+    xs = lax.axis_size("tensor") // 2
+    z, x = me // xs, me % xs
+    index = jnp.stack(
+        [
+            (z + dz) % 2 * xs + (x + dx) % xs
+            for dz in (0, 1)
+            for dx in (0, -1, 1, 2)
+        ]
+    ).astype(jnp.int32)
+    value_t = transposed(value_weight[0])
+    top, value_t = lax.optimization_barrier((grad_top.reshape(rows, feat_local), value_t))
+    whole = lax.ppermute(value_t, "section", [(i, i - 1) for i in range(1, sections)])
+    incoming = blocks_of_all(top)
     query_heads = query[0].reshape(micro_batch, length, group, head_size)
     probs = jax.vmap(causal_probs)(query_heads, keys[0])
     mixed = jnp.einsum("mgqp,mpd->mqgd", probs, values[0], preferred_element_type=F32)
-    mixed = mixed.astype(BF16).reshape(rows, group * head_size)
+    mixed_t = transposed(mixed.astype(BF16).reshape(rows, group * head_size), group * head_size)
     probs_t = probs.transpose(0, 3, 1, 2).reshape(micro_batch, length, group * length)
     weight_t = transposed(out_weight[0])
-    spot = place.astype(jnp.int32).reshape(1)
-    saved = incoming
-    value_grad = first_value_grad(incoming, weight_t, probs_t)
+    half = whole.shape[0] // 2
+    whole, incoming, index, spot, mine = lax.optimization_barrier(
+        (whole, incoming, index, spot, mine)
+    )
+    halves = lax.optimization_barrier((whole[:half], whole[half:]))
+    value_grad, saved = plain_turn(
+        sections - 1, spot, incoming, weight_t, probs_t, jnp.zeros_like(incoming)
+    )
+    beside = (incoming, value_grad, saved, mixed_t, probs_t, weight_t, value_t)
+    back, beside = gather_back(index, whole, halves, beside)
+    incoming, value_grad, saved, mixed_t, probs_t, weight_t, value_t = beside
+    back, value_grad = lax.optimization_barrier((back, value_grad))
     for section in range(sections - 1, 0, -1):
         moved = hand_down(value_grad, section)
         incoming, moved = lax.optimization_barrier((incoming, moved))
@@ -244,15 +447,12 @@
         incoming, value_grad, saved = turn(
             section - 1, spot, blocks, incoming, back, weight_t, probs_t, saved
         )
-    own = lax.dynamic_slice_in_dim(saved, me * feat_local, feat_local, 1)
-    above = shift(own, "section", 1)
-    blocks = blocks_of_all(value_grad)
-    weight_grad = lax.dot_general(mixed, saved, TN, preferred_element_type=F32).astype(BF16)
-    heads = blocks.transpose(1, 0, 2).reshape(rows, blocks.shape[0] * head_size)
-    branch = lax.dot_general(heads, value_weight[0], NT, preferred_element_type=F32)
-    last = (own.astype(F32) + branch).astype(BF16)
-    grads = jnp.where(place == 0, last, above)
-    return (grads.reshape(1, micro_batch, length, feat_local), weight_grad[None])
+    above = shift(pick(mine, saved), "section", 1)
+    grads = last_features(spot, mine, blocks_of_all(value_grad), saved, value_t, above)
+    return (
+        grads.reshape(1, micro_batch, length, feat_local),
+        weight_grads(mixed_t, saved)[None],
+    )
 
 
 def solution(mesh):

time: 626 us -> 588 us (0.939)
  waiting for transfers between devices: 159 us -> 97.2 us
  starting transfers between devices: 141 us -> 176 us
  blocking collectives: 156 us -> 179 us
  local copies, waits for them, and re-layouts: 37.5 us -> 17.3 us
  between operations: 14.7 us -> 1.35 us
  Pallas kernels: 105 us -> 114 us
  matrix products: 8.49 us -> 1.6 us
    all_gather x1 -> x0, waiting for transfers between devices: 98.6 us -> none  [on_device(): lax.all_gather(shift(transposed(value_weight[0]), 'section', -1), 'tensor...]
    ppermute x0 -> x14, waiting for transfers between devices: none -> 64.8 us  [the longest x13 64.8 us: across(): return lax.ppermute(value, 'tensor', pairs)]
    ppermute x30, starting transfers between devices: 115 us -> 148 us  [hand_down(): return lax.ppermute(value, 'section', pairs)]
    all_to_all x13 -> x15, blocking collectives: 156 us -> 179 us  [blocks_of_all(): return lax.all_to_all(copies, 'tensor', 0, 0)]
    unnamed x40 -> x33, local copies, waits for them, and re-layouts: 34.1 us -> 11.4 us
    ppermute x2 -> x1, waiting for transfers between devices: 17.9 us -> 0.06 us  [shift(): lax.ppermute(value, axis, [(i, (i + by) % length) for i in range(length)])]
    ppermute x0 -> x14, starting transfers between devices: none -> 17.4 us  [the longest x13 16.1 us: across(): return lax.ppermute(value, 'tensor', pairs)]
    pallas_call x3 -> x9, Pallas kernels: 6.83 us -> 19.5 us  [the longest x1 6.32 us: weight_grads(): pl.pallas_call(weight_kernel, grid=(steps,), in_specs=[pl.BlockSpec((own,...]
  transfers between devices with their start and end apart: 37 -> 47, of which waited for: 14 -> 21; matrix products, arithmetic and copies ran while one was open for 2% -> 1% of each run, Pallas kernels for 1% -> 3%
where the time goes in v4:
time: 588 us; the launch traced here: 587 us
  blocking collectives  179 us (30%)
  starting transfers between devices  176 us (30%)
  Pallas kernels  114 us (19%)
  waiting for transfers between devices  97.2 us (17%)
  local copies, waits for them, and re-layouts  17.3 us (3%)
    all_to_all x15, blocking collectives, blocks_of_all(): return lax.all_to_all(copies, 'tensor', 0, 0)  179 us
    ppermute x30, starting transfers between devices, hand_down(): return lax.ppermute(value, 'section', pairs)  148 us
    pallas_call x15, Pallas kernels, turn(): pl.pallas_call(functools.partial(turn_kernel, steps, section), grid=(step...  93.5 us
    ppermute x13, waiting for transfers between devices, across(): return lax.ppermute(value, 'tensor', pairs)  64.8 us
    all_to_all x2, waiting for transfers between devices, blocks_of_all(): return lax.all_to_all(copies, 'tensor', 0, 0)  24.8 us
    ppermute x13, starting transfers between devices, across(): return lax.ppermute(value, 'tensor', pairs)  16.1 us
  transfers between devices with their start and end apart: 47, of which 21 were waited for; matrix products, arithmetic and copies ran while one was open for 1% of the time, Pallas kernels for 3%

profile of v4, /device:TPU:0, one launch (start us, length us, event | category | flops | bytes accessed | tf_op | source)
XLA Modules:
  0.0 586.8 jit_solution(11037316219006817895)
XLA Ops:
  5.3 7.8 %all-to-all-start = ((bf16[8,128,768]{2,1,0:T(8,128)(2,1)}), bf16[8,128,768]{2,1,0:T(8,128)(2,1)S(1)}, u32[]{:S(2)}, u32[]{:S(2)}) async-start(bf16[8,128,768]{2,1,0:T(8,128)(2,1)} %copy-done.5), calls=%async_computation | async-start | bytes 3145728 | tf_op jit(solution)/shard_map/all_to_all | solution.py:66
  13.2 24.0 %all-to-all-done.rows_ref = bf16[8,128,768]{2,1,0:T(8,128)(2,1)S(1)} async-done(((bf16[8,128,768]{2,1,0:T(8,128)(2,1)}), bf16[8,128,768]{2,1,0:T(8,128)(2,1)S(1)}, u32[]{:S(2)}, u32[]{:S(2)}) %all-to-all-start) | async-done | bytes 1572896 | tf_op jit(solution)/shard_map/all_to_all | solution.py:66
  69.2 11.8 %collective-permute-done.5.refs_4_ = bf16[512,768]{1,0:T(8,128)(2,1)} collective-permute-done((bf16[512,768]{1,0:T(8,128)(2,1)}, bf16[512,768]{1,0:T(8,128)(2,1)}, u32[]{:S(2)}, u32[]{:S(2)}) %collective-permute-start.5) | collective-permute-done | bytes 786464 | tf_op jit(solution)/shard_map/ppermute | solution.py:131
  90.5 15.6 %collective-permute-done.10.refs_4_ = bf16[512,768]{1,0:T(8,128)(2,1)S(1)} collective-permute-done((bf16[512,768]{1,0:T(8,128)(2,1)S(1)}, bf16[512,768]{1,0:T(8,128)(2,1)S(1)}, u32[]{:S(2)}, u32[]{:S(2)}) %collective-permute-start.10) | collective-permute-done | bytes 786464 | tf_op jit(solution)/shard_map/ppermute | solution.py:131
  108.2 12.2 %collective-permute-done.7.refs_1_ = bf16[512,768]{1,0:T(8,128)(2,1)S(1)} collective-permute-done((bf16[512,768]{1,0:T(8,128)(2,1)}, bf16[512,768]{1,0:T(8,128)(2,1)S(1)}, u32[]{:S(2)}, u32[]{:S(2)}) %collective-permute-start.7) | collective-permute-done | bytes 786464 | tf_op jit(solution)/shard_map/ppermute | solution.py:131
  128.1 10.7 %collective-permute-done.12.refs_6_ = bf16[512,768]{1,0:T(8,128)(2,1)S(1)} collective-permute-done((bf16[512,768]{1,0:T(8,128)(2,1)S(1)}, bf16[512,768]{1,0:T(8,128)(2,1)S(1)}, u32[]{:S(2)}, u32[]{:S(2)}) %collective-permute-start.12) | collective-permute-done | bytes 786464 | tf_op jit(solution)/shard_map/ppermute | solution.py:131
  144.5 12.0 %all_to_all.85.blocks_ref = bf16[8,128,128]{2,1,0:T(8,128)(2,1)S(1)} all-to-all(bf16[8,128,128]{2,1,0:T(8,128)(2,1)S(1)} %copies.18), channel_id=1, replica_groups=mesh['section'=16,'tensor'=8] {'tensor'}, dimensions={0} | all-to-all | bytes 524288 | tf_op jit(solution)/shard_map/all_to_all | solution.py:66
  156.5 6.1 %turn.15 = (bf16[8,128,768]{2,1,0:T(8,128)(2,1)S(1)}, bf16[128,128]{1,0:T(8,128)(2,1)S(1)}, bf16[8,128,768]{2,1,0:T(8,128)(2,1)S(1)}) custom-call(s32[1]{0:T(128)} %bitcast.10.place_ref, bf16[8,128,128]{2,1,0:T(8,128)(2,1)S(1)} %all_to_all.85.blocks_ref, bf16[8,128,768]{2,1,0:T(8,128)(2,1)S(1)} %collective-permute-done.15.rows_ref, ...), custom_call_target="tpu_custom_call", output_to_operand_aliasing={{2}: (6, {})} | custom-call | flops 2818572288 | bytes 22020096 | tf_op jit(solution)/shard_map/turn/pallas_call | solution.py:273
  164.1 11.3 %all_to_all.86.blocks_ref = bf16[8,128,128]{2,1,0:T(8,128)(2,1)S(1)} all-to-all(bf16[8,128,128]{2,1,0:T(8,128)(2,1)S(1)} %copies.19), channel_id=1, replica_groups=mesh['section'=16,'tensor'=8] {'tensor'}, dimensions={0} | all-to-all | bytes 524288 | tf_op jit(solution)/shard_map/all_to_all | solution.py:66
  181.5 14.0 %collective-permute-start.18 = (bf16[128,128]{1,0:T(8,128)(2,1)S(1)}, bf16[128,128]{1,0:T(8,128)(2,1)S(1)}, u32[]{:S(2)}, u32[]{:S(2)}) collective-permute-start(bf16[128,128]{1,0:T(8,128)(2,1)S(1)} %get-tuple-element.136), channel_id=1, source_target_pairs={{0,8},{8,0},{16,24},{24,16},{32,40},{40,32},{48,56},{56,48},{64,72... | collective-permute-start | bytes 98312 | tf_op jit(solution)/shard_map/ppermute | solution.py:45
  196.7 11.8 %all_to_all.87.blocks_ref = bf16[8,128,128]{2,1,0:T(8,128)(2,1)S(1)} all-to-all(bf16[8,128,128]{2,1,0:T(8,128)(2,1)S(1)} %copies.20), channel_id=1, replica_groups=mesh['section'=16,'tensor'=8] {'tensor'}, dimensions={0} | all-to-all | bytes 524288 | tf_op jit(solution)/shard_map/all_to_all | solution.py:66
  216.1 11.3 %all_to_all.88.blocks_ref = bf16[8,128,128]{2,1,0:T(8,128)(2,1)S(1)} all-to-all(bf16[8,128,128]{2,1,0:T(8,128)(2,1)S(1)} %copies.21), channel_id=1, replica_groups=mesh['section'=16,'tensor'=8] {'tensor'}, dimensions={0} | all-to-all | bytes 524288 | tf_op jit(solution)/shard_map/all_to_all | solution.py:66
  233.4 13.9 %collective-permute-start.22 = (bf16[128,128]{1,0:T(8,128)(2,1)S(1)}, bf16[128,128]{1,0:T(8,128)(2,1)S(1)}, u32[]{:S(2)}, u32[]{:S(2)}) collective-permute-start(bf16[128,128]{1,0:T(8,128)(2,1)S(1)} %get-tuple-element.146), channel_id=1, source_target_pairs={{0,8},{8,0},{16,24},{24,16},{32,40},{40,32},{48,56},{56,48},{64,72... | collective-permute-start | bytes 98312 | tf_op jit(solution)/shard_map/ppermute | solution.py:45
  248.6 11.8 %all_to_all.89.blocks_ref = bf16[8,128,128]{2,1,0:T(8,128)(2,1)S(1)} all-to-all(bf16[8,128,128]{2,1,0:T(8,128)(2,1)S(1)} %copies.22), channel_id=1, replica_groups=mesh['section'=16,'tensor'=8] {'tensor'}, dimensions={0} | all-to-all | bytes 524288 | tf_op jit(solution)/shard_map/all_to_all | solution.py:66
  268.0 11.3 %all_to_all.90.blocks_ref = bf16[8,128,128]{2,1,0:T(8,128)(2,1)S(1)} all-to-all(bf16[8,128,128]{2,1,0:T(8,128)(2,1)S(1)} %copies.23), channel_id=1, replica_groups=mesh['section'=16,'tensor'=8] {'tensor'}, dimensions={0} | all-to-all | bytes 524288 | tf_op jit(solution)/shard_map/all_to_all | solution.py:66
  279.3 6.1 %turn.20 = (bf16[8,128,768]{2,1,0:T(8,128)(2,1)S(1)}, bf16[128,128]{1,0:T(8,128)(2,1)S(1)}, bf16[8,128,768]{2,1,0:T(8,128)(2,1)S(1)}) custom-call(s32[1]{0:T(128)} %bitcast.10.place_ref, bf16[8,128,128]{2,1,0:T(8,128)(2,1)S(1)} %all_to_all.90.blocks_ref, bf16[8,128,768]{2,1,0:T(8,128)(2,1)S(1)} %collective-permute-done.25.rows_ref, ...), custom_call_target="tpu_custom_call", output_to_operand_aliasing={{2}: (6, {})} | custom-call | flops 2818572288 | bytes 22020096 | tf_op jit(solution)/shard_map/turn/pallas_call | solution.py:273
  285.3 15.4 %collective-permute-start.26 = (bf16[128,128]{1,0:T(8,128)(2,1)S(1)}, bf16[128,128]{1,0:T(8,128)(2,1)S(1)}, u32[]{:S(2)}, u32[]{:S(2)}) collective-permute-start(bf16[128,128]{1,0:T(8,128)(2,1)S(1)} %get-tuple-element.156), channel_id=1, source_target_pairs={{0,8},{8,0},{16,24},{24,16},{32,40},{40,32},{48,56},{56,48},{64,72... | collective-permute-start | bytes 98312 | tf_op jit(solution)/shard_map/ppermute | solution.py:45
  302.0 11.8 %all_to_all.91.blocks_ref = bf16[8,128,128]{2,1,0:T(8,128)(2,1)S(1)} all-to-all(bf16[8,128,128]{2,1,0:T(8,128)(2,1)S(1)} %copies.24), channel_id=1, replica_groups=mesh['section'=16,'tensor'=8] {'tensor'}, dimensions={0} | all-to-all | bytes 524288 | tf_op jit(solution)/shard_map/all_to_all | solution.py:66
  321.4 11.3 %all_to_all.92.blocks_ref = bf16[8,128,128]{2,1,0:T(8,128)(2,1)S(1)} all-to-all(bf16[8,128,128]{2,1,0:T(8,128)(2,1)S(1)} %copies.25), channel_id=1, replica_groups=mesh['section'=16,'tensor'=8] {'tensor'}, dimensions={0} | all-to-all | bytes 524288 | tf_op jit(solution)/shard_map/all_to_all | solution.py:66
  340.3 12.0 %all_to_all.93.blocks_ref = bf16[8,128,128]{2,1,0:T(8,128)(2,1)S(1)} all-to-all(bf16[8,128,128]{2,1,0:T(8,128)(2,1)S(1)} %copies.26), channel_id=1, replica_groups=mesh['section'=16,'tensor'=8] {'tensor'}, dimensions={0} | all-to-all | bytes 524288 | tf_op jit(solution)/shard_map/all_to_all | solution.py:66
  359.8 16.4 %all_to_all.94.blocks_ref = bf16[8,128,128]{2,1,0:T(8,128)(2,1)S(1)} all-to-all(bf16[8,128,128]{2,1,0:T(8,128)(2,1)S(1)} %copies.27), channel_id=1, replica_groups=mesh['section'=16,'tensor'=8] {'tensor'}, dimensions={0} | all-to-all | bytes 524288 | tf_op jit(solution)/shard_map/all_to_all | solution.py:66
  382.2 9.5 %collective-permute-start.34 = (bf16[128,128]{1,0:T(8,128)(2,1)S(1)}, bf16[128,128]{1,0:T(8,128)(2,1)S(1)}, u32[]{:S(2)}, u32[]{:S(2)}) collective-permute-start(bf16[128,128]{1,0:T(8,128)(2,1)S(1)} %get-tuple-element.176), channel_id=1, source_target_pairs={{0,8},{8,0},{16,24},{24,16},{32,40},{40,32},{48,56},{56,48},{64,72... | collective-permute-start | bytes 98312 | tf_op jit(solution)/shard_map/ppermute | solution.py:45
  393.0 11.8 %all_to_all.95.blocks_ref = bf16[8,128,128]{2,1,0:T(8,128)(2,1)S(1)} all-to-all(bf16[8,128,128]{2,1,0:T(8,128)(2,1)S(1)} %copies.28), channel_id=1, replica_groups=mesh['section'=16,'tensor'=8] {'tensor'}, dimensions={0} | all-to-all | bytes 524288 | tf_op jit(solution)/shard_map/all_to_all | solution.py:66
  412.4 11.3 %all_to_all.96.blocks_ref = bf16[8,128,128]{2,1,0:T(8,128)(2,1)S(1)} all-to-all(bf16[8,128,128]{2,1,0:T(8,128)(2,1)S(1)} %copies.29), channel_id=1, replica_groups=mesh['section'=16,'tensor'=8] {'tensor'}, dimensions={0} | all-to-all | bytes 524288 | tf_op jit(solution)/shard_map/all_to_all | solution.py:66
  429.8 14.6 %collective-permute-start.38 = (bf16[128,128]{1,0:T(8,128)(2,1)S(1)}, bf16[128,128]{1,0:T(8,128)(2,1)S(1)}, u32[]{:S(2)}, u32[]{:S(2)}) collective-permute-start(bf16[128,128]{1,0:T(8,128)(2,1)S(1)} %get-tuple-element.186), channel_id=1, source_target_pairs={{0,8},{8,0},{16,24},{24,16},{32,40},{40,32},{48,56},{56,48},{64,72... | collective-permute-start | bytes 98312 | tf_op jit(solution)/shard_map/ppermute | solution.py:45
  445.6 11.8 %all_to_all.97.blocks_ref = bf16[8,128,128]{2,1,0:T(8,128)(2,1)S(1)} all-to-all(bf16[8,128,128]{2,1,0:T(8,128)(2,1)S(1)} %copies.30), channel_id=1, replica_groups=mesh['section'=16,'tensor'=8] {'tensor'}, dimensions={0} | all-to-all | bytes 524288 | tf_op jit(solution)/shard_map/all_to_all | solution.py:66
  464.9 11.3 %all_to_all.98.blocks_ref = bf16[8,128,128]{2,1,0:T(8,128)(2,1)S(1)} all-to-all(bf16[8,128,128]{2,1,0:T(8,128)(2,1)S(1)} %copies.31), channel_id=1, replica_groups=mesh['section'=16,'tensor'=8] {'tensor'}, dimensions={0} | all-to-all | bytes 524288 | tf_op jit(solution)/shard_map/all_to_all | solution.py:66
  476.3 6.1 %turn.28 = (bf16[8,128,768]{2,1,0:T(8,128)(2,1)S(1)}, bf16[128,128]{1,0:T(8,128)(2,1)S(1)}, bf16[8,128,768]{2,1,0:T(8,128)(2,1)S(1)}) custom-call(s32[1]{0:T(128)} %bitcast.10.place_ref, bf16[8,128,128]{2,1,0:T(8,128)(2,1)S(1)} %all_to_all.98.blocks_ref, bf16[8,128,768]{2,1,0:T(8,128)(2,1)S(1)} %collective-permute-done.41.rows_ref, ...), custom_call_target="tpu_custom_call", output_to_operand_aliasing={{2}: (6, {})} | custom-call | flops 2818572288 | bytes 22020096 | tf_op jit(solution)/shard_map/turn/pallas_call | solution.py:273
  482.3 67.7 %collective-permute-start.42 = (bf16[128,128]{1,0:T(8,128)(2,1)S(1)}, bf16[128,128]{1,0:T(8,128)(2,1)S(1)}, u32[]{:S(2)}, u32[]{:S(2)}) collective-permute-start(bf16[128,128]{1,0:T(8,128)(2,1)S(1)} %get-tuple-element.196), channel_id=1, source_target_pairs={{0,8},{8,0},{16,24},{24,16},{32,40},{40,32},{48,56},{56,48},{64,72... | collective-permute-start | bytes 98312 | tf_op jit(solution)/shard_map/ppermute | solution.py:45
  551.3 11.8 %all_to_all.99.blocks_ref = bf16[8,128,128]{2,1,0:T(8,128)(2,1)S(1)} all-to-all(bf16[8,128,128]{2,1,0:T(8,128)(2,1)S(1)} %copies.32), channel_id=1, replica_groups=mesh['section'=16,'tensor'=8] {'tensor'}, dimensions={0} | all-to-all | bytes 524288 | tf_op jit(solution)/shard_map/all_to_all | solution.py:66
  563.1 8.8 %turn.29 = (bf16[8,128,768]{2,1,0:T(8,128)(2,1)}, bf16[128,128]{1,0:T(8,128)(2,1)S(1)}, bf16[8,128,768]{2,1,0:T(8,128)(2,1)S(1)}) custom-call(s32[1]{0:T(128)} %bitcast.10.place_ref, bf16[8,128,128]{2,1,0:T(8,128)(2,1)S(1)} %all_to_all.99.blocks_ref, bf16[8,128,768]{2,1,0:T(8,128)(2,1)S(1)} %collective-permute-done.43.rows_ref, ...), custom_call_target="tpu_custom_call", output_to_operand_aliasing={{2}: (6, {})} | custom-call | flops 2818572288 | bytes 22020096 | tf_op jit(solution)/shard_map/turn/pallas_call | solution.py:273
  577.0 6.3 %weight_grads.1 = bf16[768,6144]{1,0:T(8,128)(2,1)} custom-call(bf16[768,128]{1,0:T(8,128)(2,1)S(1)} %copy-done.9, bf16[8,128,768]{2,1,0:T(8,128)(2,1)S(1)} %get-tuple-element.201.rows_ref), custom_call_target="tpu_custom_call" | custom-call | flops 1207959552 | bytes 9437184 | tf_op jit(solution)/shard_map/weight_grads/pallas_call | solution.py:381
  (165 shorter events, 155.8 us)
Async XLA Ops:
  2.7 34.5 %collective-permute-start = (bf16[1024,768]{1,0:T(8,128)(2,1)S(1)}, bf16[1024,768]{1,0:T(8,128)(2,1)}, u32[]{:S(2)}, u32[]{:S(2)}) collective-permute-start(bf16[1024,768]{1,0:T(8,128)(2,1)S(1)} %transposed.3.value_t_ref), channel_id=1, source_target_pairs={{8,0},{16,8},{24,16},{32,24},{40,32},{48,40},{56,48},{64,56},{72,6... | collective-permute-start | bytes 4718600 | tf_op jit(solution)/shard_map/ppermute | solution.py:422
  5.3 31.9 %all-to-all-start = ((bf16[8,128,768]{2,1,0:T(8,128)(2,1)}), bf16[8,128,768]{2,1,0:T(8,128)(2,1)S(1)}, u32[]{:S(2)}, u32[]{:S(2)}) async-start(bf16[8,128,768]{2,1,0:T(8,128)(2,1)} %copy-done.5), calls=%async_computation | async-start | bytes 3145728 | tf_op jit(solution)/shard_map/all_to_all | solution.py:66
  37.2 47.2 %collective-permute-start.1 = (bf16[1024,768]{1,0:T(8,128)(2,1)}, bf16[1024,768]{1,0:T(8,128)(2,1)}, u32[]{:S(2)}, u32[]{:S(2)}) collective-permute-start(bf16[1024,768]{1,0:T(8,128)(2,1)} %collective-permute-done.refs_0_), channel_id=1, source_target_pairs={{0,4},{1,5},{2,6},{3,7},{4,0},{5,1},{6,2},{7,3},{8,12},{9,13},{10,... | collective-permute-start | bytes 4718600 | tf_op jit(solution)/shard_map/ppermute | solution.py:131
  42.2 23.3 %collective-permute-start.3 = (bf16[512,768]{1,0:T(8,128)(2,1)}, bf16[512,768]{1,0:T(8,128)(2,1)}, u32[]{:S(2)}, u32[]{:S(2)}) collective-permute-start(bf16[512,768]{1,0:T(8,128)(2,1)} %get-tuple-element.108), channel_id=1, source_target_pairs={{0,3},{1,0},{2,1},{3,2},{4,7},{5,4},{6,5},{7,6},{8,11},{9,8},{10,9... | collective-permute-start | bytes 2359304 | tf_op jit(solution)/shard_map/ppermute | solution.py:131
  47.2 22.0 %collective-permute-start.2 = (bf16[512,768]{1,0:T(8,128)(2,1)}, bf16[512,768]{1,0:T(8,128)(2,1)}, u32[]{:S(2)}, u32[]{:S(2)}) collective-permute-start(bf16[512,768]{1,0:T(8,128)(2,1)} %get-tuple-element.108), channel_id=1, source_target_pairs={{0,1},{1,2},{2,3},{3,0},{4,5},{5,6},{6,7},{7,4},{8,9},{9,10},{10,1... | collective-permute-start | bytes 2359304 | tf_op jit(solution)/shard_map/ppermute | solution.py:131
  47.2 33.8 %collective-permute-start.5 = (bf16[512,768]{1,0:T(8,128)(2,1)}, bf16[512,768]{1,0:T(8,128)(2,1)}, u32[]{:S(2)}, u32[]{:S(2)}) collective-permute-start(bf16[512,768]{1,0:T(8,128)(2,1)} %get-tuple-element.109), channel_id=1, source_target_pairs={{0,3},{1,0},{2,1},{3,2},{4,7},{5,4},{6,5},{7,6},{8,11},{9,8},{10,9... | collective-permute-start | bytes 2359304 | tf_op jit(solution)/shard_map/ppermute | solution.py:131
  50.5 34.0 %collective-permute-start.4 = (bf16[512,768]{1,0:T(8,128)(2,1)}, bf16[512,768]{1,0:T(8,128)(2,1)}, u32[]{:S(2)}, u32[]{:S(2)}) collective-permute-start(bf16[512,768]{1,0:T(8,128)(2,1)} %get-tuple-element.109), channel_id=1, source_target_pairs={{0,1},{1,2},{2,3},{3,0},{4,5},{5,6},{6,7},{7,4},{8,9},{9,10},{10,1... | collective-permute-start | bytes 2359304 | tf_op jit(solution)/shard_map/ppermute | solution.py:131
  85.6 20.5 %collective-permute-start.10 = (bf16[512,768]{1,0:T(8,128)(2,1)S(1)}, bf16[512,768]{1,0:T(8,128)(2,1)S(1)}, u32[]{:S(2)}, u32[]{:S(2)}) collective-permute-start(bf16[512,768]{1,0:T(8,128)(2,1)S(1)} %slice.12), channel_id=1, source_target_pairs={{0,3},{1,0},{2,1},{3,2},{4,7},{5,4},{6,5},{7,6},{8,11},{9,8},{10,9... | collective-permute-start | bytes 2359304 | tf_op jit(solution)/shard_map/ppermute | solution.py:131
  86.0 21.7 %collective-permute-start.8 = (bf16[512,768]{1,0:T(8,128)(2,1)S(1)}, bf16[512,768]{1,0:T(8,128)(2,1)S(1)}, u32[]{:S(2)}, u32[]{:S(2)}) collective-permute-start(bf16[512,768]{1,0:T(8,128)(2,1)S(1)} %slice.12), channel_id=1, source_target_pairs={{0,1},{1,2},{2,3},{3,0},{4,5},{5,6},{6,7},{7,4},{8,9},{9,10},{10,1... | collective-permute-start | bytes 2359304 | tf_op jit(solution)/shard_map/ppermute | solution.py:131
  87.7 32.7 %collective-permute-start.7 = (bf16[512,768]{1,0:T(8,128)(2,1)}, bf16[512,768]{1,0:T(8,128)(2,1)S(1)}, u32[]{:S(2)}, u32[]{:S(2)}) collective-permute-start(bf16[512,768]{1,0:T(8,128)(2,1)} %collective-permute-done.5.refs_4_), channel_id=1, source_target_pairs={{0,3},{1,0},{2,1},{3,2},{4,7},{5,4},{6,5},{7,6},{8,11},{9,8},{10,9... | collective-permute-start | bytes 2359304 | tf_op jit(solution)/shard_map/ppermute | solution.py:131
  89.2 38.9 %collective-permute-start.11 = (bf16[512,768]{1,0:T(8,128)(2,1)}, bf16[512,768]{1,0:T(8,128)(2,1)S(1)}, u32[]{:S(2)}, u32[]{:S(2)}) collective-permute-start(bf16[512,768]{1,0:T(8,128)(2,1)} %collective-permute-done.5.refs_4_), channel_id=1, source_target_pairs={{0,4},{1,5},{2,6},{3,7},{4,0},{5,1},{6,2},{7,3},{8,12},{9,13},{10,... | collective-permute-start | bytes 2359304 | tf_op jit(solution)/shard_map/ppermute | solution.py:131
  90.0 34.9 %collective-permute-start.6 = (bf16[512,768]{1,0:T(8,128)(2,1)}, bf16[512,768]{1,0:T(8,128)(2,1)S(1)}, u32[]{:S(2)}, u32[]{:S(2)}) collective-permute-start(bf16[512,768]{1,0:T(8,128)(2,1)} %collective-permute-done.2.refs_1_), channel_id=1, source_target_pairs={{0,1},{1,2},{2,3},{3,0},{4,5},{5,6},{6,7},{7,4},{8,9},{9,10},{10,1... | collective-permute-start | bytes 2359304 | tf_op jit(solution)/shard_map/ppermute | solution.py:131
  106.2 22.0 %collective-permute-start.9 = (bf16[512,768]{1,0:T(8,128)(2,1)}, bf16[512,768]{1,0:T(8,128)(2,1)S(1)}, u32[]{:S(2)}, u32[]{:S(2)}) collective-permute-start(bf16[512,768]{1,0:T(8,128)(2,1)} %collective-permute-done.4.refs_2_), channel_id=1, source_target_pairs={{0,4},{1,5},{2,6},{3,7},{4,0},{5,1},{6,2},{7,3},{8,12},{9,13},{10,... | collective-permute-start | bytes 2359304 | tf_op jit(solution)/shard_map/ppermute | solution.py:131
  107.7 31.1 %collective-permute-start.12 = (bf16[512,768]{1,0:T(8,128)(2,1)S(1)}, bf16[512,768]{1,0:T(8,128)(2,1)S(1)}, u32[]{:S(2)}, u32[]{:S(2)}) collective-permute-start(bf16[512,768]{1,0:T(8,128)(2,1)S(1)} %collective-permute-done.8.refs_2_), channel_id=1, source_target_pairs={{0,1},{1,2},{2,3},{3,0},{4,5},{5,6},{6,7},{7,4},{8,9},{9,10},{10,1... | collective-permute-start | bytes 2359304 | tf_op jit(solution)/shard_map/ppermute | solution.py:131
  120.4 21.6 %collective-permute-start.13 = (bf16[512,768]{1,0:T(8,128)(2,1)S(1)}, bf16[512,768]{1,0:T(8,128)(2,1)S(1)}, u32[]{:S(2)}, u32[]{:S(2)}) collective-permute-start(bf16[512,768]{1,0:T(8,128)(2,1)S(1)} %collective-permute-done.7.refs_1_), channel_id=1, source_target_pairs={{0,4},{1,5},{2,6},{3,7},{4,0},{5,1},{6,2},{7,3},{8,12},{9,13},{10,... | collective-permute-start | bytes 2359304 | tf_op jit(solution)/shard_map/ppermute | solution.py:131
  144.3 12.2 %collective-permute-start.15 = (bf16[8,128,768]{2,1,0:T(8,128)(2,1)S(1)}, bf16[8,128,768]{2,1,0:T(8,128)(2,1)S(1)}, u32[]{:S(2)}, u32[]{:S(2)}) collective-permute-start(bf16[8,128,768]{2,1,0:T(8,128)(2,1)S(1)} %copy-done.4), channel_id=1, source_target_pairs={{0,8},{8,0},{16,24},{24,16},{32,40},{40,32},{48,56},{56,48},{64,72... | collective-permute-start | bytes 4718600 | tf_op jit(solution)/shard_map/ppermute | solution.py:45
  181.5 14.9 %collective-permute-start.18 = (bf16[128,128]{1,0:T(8,128)(2,1)S(1)}, bf16[128,128]{1,0:T(8,128)(2,1)S(1)}, u32[]{:S(2)}, u32[]{:S(2)}) collective-permute-start(bf16[128,128]{1,0:T(8,128)(2,1)S(1)} %get-tuple-element.136), channel_id=1, source_target_pairs={{0,8},{8,0},{16,24},{24,16},{32,40},{40,32},{48,56},{56,48},{64,72... | collective-permute-start | bytes 98312 | tf_op jit(solution)/shard_map/ppermute | solution.py:45
  196.3 12.2 %collective-permute-start.19 = (bf16[8,128,768]{2,1,0:T(8,128)(2,1)S(1)}, bf16[8,128,768]{2,1,0:T(8,128)(2,1)S(1)}, u32[]{:S(2)}, u32[]{:S(2)}) collective-permute-start(bf16[8,128,768]{2,1,0:T(8,128)(2,1)S(1)} %get-tuple-element.138), channel_id=1, source_target_pairs={{0,8},{8,0},{16,24},{24,16},{32,40},{40,32},{48,56},{56,48},{64,72... | collective-permute-start | bytes 4718600 | tf_op jit(solution)/shard_map/ppermute | solution.py:45
  233.4 14.8 %collective-permute-start.22 = (bf16[128,128]{1,0:T(8,128)(2,1)S(1)}, bf16[128,128]{1,0:T(8,128)(2,1)S(1)}, u32[]{:S(2)}, u32[]{:S(2)}) collective-permute-start(bf16[128,128]{1,0:T(8,128)(2,1)S(1)} %get-tuple-element.146), channel_id=1, source_target_pairs={{0,8},{8,0},{16,24},{24,16},{32,40},{40,32},{48,56},{56,48},{64,72... | collective-permute-start | bytes 98312 | tf_op jit(solution)/shard_map/ppermute | solution.py:45
  248.2 12.2 %collective-permute-start.23 = (bf16[8,128,768]{2,1,0:T(8,128)(2,1)S(1)}, bf16[8,128,768]{2,1,0:T(8,128)(2,1)S(1)}, u32[]{:S(2)}, u32[]{:S(2)}) collective-permute-start(bf16[8,128,768]{2,1,0:T(8,128)(2,1)S(1)} %get-tuple-element.148), channel_id=1, source_target_pairs={{0,8},{8,0},{16,24},{24,16},{32,40},{40,32},{48,56},{56,48},{64,72... | collective-permute-start | bytes 4718600 | tf_op jit(solution)/shard_map/ppermute | solution.py:45
  285.3 16.3 %collective-permute-start.26 = (bf16[128,128]{1,0:T(8,128)(2,1)S(1)}, bf16[128,128]{1,0:T(8,128)(2,1)S(1)}, u32[]{:S(2)}, u32[]{:S(2)}) collective-permute-start(bf16[128,128]{1,0:T(8,128)(2,1)S(1)} %get-tuple-element.156), channel_id=1, source_target_pairs={{0,8},{8,0},{16,24},{24,16},{32,40},{40,32},{48,56},{56,48},{64,72... | collective-permute-start | bytes 98312 | tf_op jit(solution)/shard_map/ppermute | solution.py:45
  301.7 12.2 %collective-permute-start.27 = (bf16[8,128,768]{2,1,0:T(8,128)(2,1)S(1)}, bf16[8,128,768]{2,1,0:T(8,128)(2,1)S(1)}, u32[]{:S(2)}, u32[]{:S(2)}) collective-permute-start(bf16[8,128,768]{2,1,0:T(8,128)(2,1)S(1)} %get-tuple-element.158), channel_id=1, source_target_pairs={{0,8},{8,0},{16,24},{24,16},{32,40},{40,32},{48,56},{56,48},{64,72... | collective-permute-start | bytes 4718600 | tf_op jit(solution)/shard_map/ppermute | solution.py:45
  320.6 12.2 %collective-permute-start.29 = (bf16[8,128,768]{2,1,0:T(8,128)(2,1)S(1)}, bf16[8,128,768]{2,1,0:T(8,128)(2,1)S(1)}, u32[]{:S(2)}, u32[]{:S(2)}) collective-permute-start(bf16[8,128,768]{2,1,0:T(8,128)(2,1)S(1)} %get-tuple-element.163), channel_id=1, source_target_pairs={{0,0},{8,8},{16,16},{24,24},{32,32},{40,40},{48,48},{56,64},{64,56... | collective-permute-start | bytes 4718600 | tf_op jit(solution)/shard_map/ppermute | solution.py:45
  340.1 12.2 %collective-permute-start.31 = (bf16[8,128,768]{2,1,0:T(8,128)(2,1)S(1)}, bf16[8,128,768]{2,1,0:T(8,128)(2,1)S(1)}, u32[]{:S(2)}, u32[]{:S(2)}) collective-permute-start(bf16[8,128,768]{2,1,0:T(8,128)(2,1)S(1)} %get-tuple-element.168), channel_id=1, source_target_pairs={{0,8},{8,0},{16,24},{24,16},{32,40},{40,32},{48,56},{56,48},{64,72... | collective-permute-start | bytes 4718600 | tf_op jit(solution)/shard_map/ppermute | solution.py:45
  359.0 17.2 %collective-permute-start.33 = (bf16[8,128,768]{2,1,0:T(8,128)(2,1)S(1)}, bf16[8,128,768]{2,1,0:T(8,128)(2,1)S(1)}, u32[]{:S(2)}, u32[]{:S(2)}) collective-permute-start(bf16[8,128,768]{2,1,0:T(8,128)(2,1)S(1)} %get-tuple-element.173), channel_id=1, source_target_pairs={{0,0},{8,16},{16,8},{24,32},{32,24},{40,48},{48,40},{56,56},{64,64... | collective-permute-start | bytes 4718600 | tf_op jit(solution)/shard_map/ppermute | solution.py:45
  392.6 12.2 %collective-permute-start.35 = (bf16[8,128,768]{2,1,0:T(8,128)(2,1)S(1)}, bf16[8,128,768]{2,1,0:T(8,128)(2,1)S(1)}, u32[]{:S(2)}, u32[]{:S(2)}) collective-permute-start(bf16[8,128,768]{2,1,0:T(8,128)(2,1)S(1)} %get-tuple-element.178), channel_id=1, source_target_pairs={{0,8},{8,0},{16,24},{24,16},{32,40},{40,32},{48,56},{56,48},{64,72... | collective-permute-start | bytes 4718600 | tf_op jit(solution)/shard_map/ppermute | solution.py:45
  429.8 15.4 %collective-permute-start.38 = (bf16[128,128]{1,0:T(8,128)(2,1)S(1)}, bf16[128,128]{1,0:T(8,128)(2,1)S(1)}, u32[]{:S(2)}, u32[]{:S(2)}) collective-permute-start(bf16[128,128]{1,0:T(8,128)(2,1)S(1)} %get-tuple-element.186), channel_id=1, source_target_pairs={{0,8},{8,0},{16,24},{24,16},{32,40},{40,32},{48,56},{56,48},{64,72... | collective-permute-start | bytes 98312 | tf_op jit(solution)/shard_map/ppermute | solution.py:45
  445.2 12.2 %collective-permute-start.39 = (bf16[8,128,768]{2,1,0:T(8,128)(2,1)S(1)}, bf16[8,128,768]{2,1,0:T(8,128)(2,1)S(1)}, u32[]{:S(2)}, u32[]{:S(2)}) collective-permute-start(bf16[8,128,768]{2,1,0:T(8,128)(2,1)S(1)} %get-tuple-element.188), channel_id=1, source_target_pairs={{0,8},{8,0},{16,24},{24,16},{32,40},{40,32},{48,56},{56,48},{64,72... | collective-permute-start | bytes 4718600 | tf_op jit(solution)/shard_map/ppermute | solution.py:45
  464.1 12.1 %collective-permute-start.41 = (bf16[8,128,768]{2,1,0:T(8,128)(2,1)S(1)}, bf16[8,128,768]{2,1,0:T(8,128)(2,1)S(1)}, u32[]{:S(2)}, u32[]{:S(2)}) collective-permute-start(bf16[8,128,768]{2,1,0:T(8,128)(2,1)S(1)} %get-tuple-element.193), channel_id=1, source_target_pairs={{0,0},{8,16},{16,8},{24,32},{32,24},{40,48},{48,40},{56,56},{64,64... | collective-permute-start | bytes 4718600 | tf_op jit(solution)/shard_map/ppermute | solution.py:45
  482.3 68.6 %collective-permute-start.42 = (bf16[128,128]{1,0:T(8,128)(2,1)S(1)}, bf16[128,128]{1,0:T(8,128)(2,1)S(1)}, u32[]{:S(2)}, u32[]{:S(2)}) collective-permute-start(bf16[128,128]{1,0:T(8,128)(2,1)S(1)} %get-tuple-element.196), channel_id=1, source_target_pairs={{0,8},{8,0},{16,24},{24,16},{32,40},{40,32},{48,56},{56,48},{64,72... | collective-permute-start | bytes 98312 | tf_op jit(solution)/shard_map/ppermute | solution.py:45
  550.9 12.2 %collective-permute-start.43 = (bf16[8,128,768]{2,1,0:T(8,128)(2,1)S(1)}, bf16[8,128,768]{2,1,0:T(8,128)(2,1)S(1)}, u32[]{:S(2)}, u32[]{:S(2)}) collective-permute-start(bf16[8,128,768]{2,1,0:T(8,128)(2,1)S(1)} %get-tuple-element.198), channel_id=1, source_target_pairs={{0,8},{8,0},{16,24},{24,16},{32,40},{40,32},{48,56},{56,48},{64,72... | collective-permute-start | bytes 4718600 | tf_op jit(solution)/shard_map/ppermute | solution.py:45
  572.7 12.1 %all-to-all-start.16 = ((bf16[8,128,128]{2,1,0:T(8,128)(2,1)}), bf16[8,128,128]{2,1,0:T(8,128)(2,1)S(1)}, u32[]{:S(2)}, u32[]{:S(2)}) async-start(bf16[8,128,128]{2,1,0:T(8,128)(2,1)} %copy-done.7), calls=%async_computation.16 | async-start | bytes 524288 | tf_op jit(solution)/shard_map/all_to_all | solution.py:66
  (31 other events, 208.8 us)

commit v5 on v4

--- a/solution.py
+++ b/solution.py
@@ -11,6 +11,9 @@
 F32 = jnp.float32
 BF16 = jnp.bfloat16
 NN = (((1,), (0,)), ((), ()))
+
+
+AHEAD = 5
 
 
 def causal_probs(query_heads, key_rows):
@@ -201,9 +204,15 @@
 
 
 def turn_kernel(
-    steps, section, place_ref, blocks_ref, rows_ref, back_ref, weight_ref, probs_t_ref, kept_ref,
-    new_ref, value_ref, saved_ref, heads, total, sem,
+    first, steps, section, has_total, ends, place_ref, blocks_ref, *refs,
 ):
+    refs = list(refs)
+    count = len(steps)
+    rows_refs = [refs.pop(0) for _ in range(count)]
+    back_ref, weight_ref, probs_t_ref, kept_ref = (refs.pop(0) for _ in range(4))
+    total_ref = refs.pop(0) if has_total else None
+    new_refs = [refs.pop(0) for _ in range(count)]
+    result_ref, saved_ref, heads, total, sem = refs
     step = pl.program_id(0)
     head_size = blocks_ref.shape[2]
 
@@ -211,20 +220,33 @@
     def _():
         for c in range(blocks_ref.shape[0]):
             heads[:, c * head_size : (c + 1) * head_size] = blocks_ref[c]
-        total[...] = jnp.zeros_like(total)
+        total[...] = total_ref[...] if has_total else jnp.zeros_like(total)
 
     branch = lax.dot_general(heads[...], back_ref[0], NN, preferred_element_type=F32)
-    new_rows = (rows_ref[0].astype(F32) + branch).astype(BF16)
-    new_ref[0] = new_rows
-    total[...] += lax.dot_general(new_rows, weight_ref[...], NN, preferred_element_type=F32)
-
-    @pl.when(place_ref[0] == section)
-    def _():
-        keep(step, new_ref.at[0], saved_ref, sem)
-
-    @pl.when(step == steps - 1)
-    def _():
-        value_grad_of(total[...], probs_t_ref, value_ref)
+
+    def finish(rows_ref, new_ref):
+        new_rows = (rows_ref[0].astype(F32) + branch).astype(BF16)
+        new_ref[0] = new_rows
+        total[...] += lax.dot_general(
+            new_rows, weight_ref[...], NN, preferred_element_type=F32
+        )
+
+        @pl.when(place_ref[0] == section)
+        def _():
+            keep(first + step, new_ref.at[0], saved_ref, sem)
+
+    if count == 1:
+        finish(rows_refs[0], new_refs[0])
+    else:
+        pl.when(step < steps[0])(lambda: finish(rows_refs[0], new_refs[0]))
+        pl.when(step >= steps[0])(lambda: finish(rows_refs[1], new_refs[1]))
+
+    @pl.when(step == sum(steps) - 1)
+    def _():
+        if ends:
+            value_grad_of(total[...], probs_t_ref, result_ref)
+        else:
+            result_ref[...] = total[...]
 
 
 def params():
@@ -265,31 +287,45 @@
     )(place, rows, weight_t, probs_t, saved)
 
 
-def turn(section, place, blocks, rows, back, weight_t, probs_t, saved):
-    count = rows.shape[1]
+def turn(section, place, blocks, rows, back, weight_t, probs_t, saved, first=0, total=None, ends=True):
+    count, tile = rows[0].shape[1:]
     own = weight_t.shape[1]
-    steps, depth, tile = back.shape
+    depth = back.shape[1]
     head_size = blocks.shape[2]
-    return pl.pallas_call(
-        functools.partial(turn_kernel, steps, section),
-        grid=(steps,),
+    steps = [part.shape[0] for part in rows]
+    parts = [pl.BlockSpec((1, count, tile), lambda i: (jnp.minimum(i, steps[0] - 1), 0, 0))]
+    if len(rows) == 2:
+        parts.append(
+            pl.BlockSpec((1, count, tile), lambda i: (jnp.maximum(i - steps[0], 0), 0, 0))
+        )
+    whole = pl.BlockSpec((count, own), lambda i: (0, 0))
+    extra = [] if total is None else [total]
+    if ends:
+        result = jax.ShapeDtypeStruct((count, head_size), BF16)
+    else:
+        result = jax.ShapeDtypeStruct((count, own), F32)
+    alias = 5 + len(rows)
+    outs = pl.pallas_call(
+        functools.partial(turn_kernel, first, steps, section, total is not None, ends),
+        grid=(sum(steps),),
         in_specs=[
             pl.BlockSpec(memory_space=pltpu.SMEM),
             pl.BlockSpec(blocks.shape, lambda i: (0, 0, 0)),
-            pl.BlockSpec((1, count, tile), lambda i: (i, 0, 0)),
-            pl.BlockSpec((1, depth, tile), lambda i: (i, 0, 0)),
-            pl.BlockSpec((tile, own), lambda i: (i, 0)),
+            *parts,
+            pl.BlockSpec((1, depth, tile), lambda i: (i + first, 0, 0)),
+            pl.BlockSpec((tile, own), lambda i: (i + first, 0)),
             pl.BlockSpec(probs_t.shape, lambda i: (0, 0, 0)),
             pl.BlockSpec(memory_space=pl.ANY),
+            *[whole for _ in extra],
         ],
         out_specs=[
-            pl.BlockSpec((1, count, tile), lambda i: (i, 0, 0)),
-            pl.BlockSpec((count, head_size), lambda i: (0, 0)),
+            *parts,
+            pl.BlockSpec(result.shape, lambda i: (0, 0)),
             pl.BlockSpec(memory_space=pl.ANY),
         ],
         out_shape=[
-            jax.ShapeDtypeStruct(rows.shape, BF16),
-            jax.ShapeDtypeStruct((count, head_size), BF16),
+            *[jax.ShapeDtypeStruct(part.shape, BF16) for part in rows],
+            result,
             jax.ShapeDtypeStruct(saved.shape, BF16),
         ],
         scratch_shapes=[
@@ -297,15 +333,16 @@
             pltpu.VMEM((count, own), F32),
             pltpu.SemaphoreType.DMA,
         ],
-        input_output_aliases={6: 2},
+        input_output_aliases={alias: len(rows) + 1},
         compiler_params=params(),
         cost_estimate=pl.CostEstimate(
-            flops=2 * steps * count * tile * (own + depth),
-            bytes_accessed=2 * steps * tile * (own + depth),
+            flops=2 * sum(steps) * count * tile * (own + depth),
+            bytes_accessed=2 * sum(steps) * tile * (own + depth),
             transcendentals=0,
         ),
         name="turn",
-    )(place, blocks, rows, back, weight_t, probs_t, saved)
+    )(place, blocks, *rows, back, weight_t, probs_t, saved, *extra)
+    return outs[:-2], outs[-2], outs[-1]
 
 
 def pick_kernel(me_ref, rows_ref, out_ref):
@@ -439,14 +476,25 @@
     back, beside = gather_back(index, whole, halves, beside)
     incoming, value_grad, saved, mixed_t, probs_t, weight_t, value_t = beside
     back, value_grad = lax.optimization_barrier((back, value_grad))
+    parts = (incoming[:AHEAD], incoming[AHEAD:])
     for section in range(sections - 1, 0, -1):
         moved = hand_down(value_grad, section)
-        incoming, moved = lax.optimization_barrier((incoming, moved))
-        incoming = hand_down(incoming, section)
+        parts, moved = lax.optimization_barrier((parts, moved))
+        parts = [hand_down(part, section) for part in parts]
         blocks = blocks_of_all(moved)
-        incoming, value_grad, saved = turn(
-            section - 1, spot, blocks, incoming, back, weight_t, probs_t, saved
-        )
+        below = section - 1
+        if section % 2:
+            parts, value_grad, saved = turn(
+                below, spot, blocks, parts, back, weight_t, probs_t, saved
+            )
+        else:
+            (ahead,), total, saved = turn(
+                below, spot, blocks, parts[:1], back, weight_t, probs_t, saved, ends=False
+            )
+            (rest,), value_grad, saved = turn(
+                below, spot, blocks, parts[1:], back, weight_t, probs_t, saved, AHEAD, total
+            )
+            parts = (ahead, rest)
     above = shift(pick(mine, saved), "section", 1)
     grads = last_features(spot, mine, blocks_of_all(value_grad), saved, value_t, above)
     return (

time: 588 us -> 565 us (0.961); the launches traced: 587 us -> 556 us
  starting transfers between devices: 176 us -> 130 us
  blocking collectives: 179 us -> 192 us
    ppermute x30 -> x45, starting transfers between devices: 148 us -> 102 us  [hand_down(): return lax.ppermute(value, 'section', pairs)]
    all_to_all x15, blocking collectives: 179 us -> 192 us  [blocks_of_all(): return lax.all_to_all(copies, 'tensor', 0, 0)]
    pallas_call x15 -> x22, Pallas kernels: 93.5 us -> 96.4 us  [turn(): pl.pallas_call(functools.partial(turn_kernel, first, steps, section, tota...]
  transfers between devices with their start and end apart: 47 -> 62, of which waited for: 21 -> 21; matrix products, arithmetic and copies ran while one was open for 1% -> 1% of each run, Pallas kernels for 3% -> 8%
where the time goes in v5:
time: 565 us; the launch traced here: 556 us
  blocking collectives  192 us (34%)
  starting transfers between devices  130 us (23%)
  Pallas kernels  117 us (21%)
  waiting for transfers between devices  101 us (18%)
  local copies, waits for them, and re-layouts  14.4 us (3%)
    all_to_all x15, blocking collectives, blocks_of_all(): return lax.all_to_all(copies, 'tensor', 0, 0)  192 us
    ppermute x45, starting transfers between devices, hand_down(): return lax.ppermute(value, 'section', pairs)  102 us
    pallas_call x22, Pallas kernels, turn(): pl.pallas_call(functools.partial(turn_kernel, first, steps, section, tota...  96.4 us
    ppermute x13, waiting for transfers between devices, across(): return lax.ppermute(value, 'tensor', pairs)  68 us
    all_to_all x2, waiting for transfers between devices, blocks_of_all(): return lax.all_to_all(copies, 'tensor', 0, 0)  24.6 us
    ppermute x13, starting transfers between devices, across(): return lax.ppermute(value, 'tensor', pairs)  15.1 us
  transfers between devices with their start and end apart: 62, of which 21 were waited for; matrix products, arithmetic and copies ran while one was open for 1% of the time, Pallas kernels for 8%

profile of v5, /device:TPU:0, one launch (start us, length us, event | category | flops | bytes accessed | tf_op | source)
XLA Modules:
  0.0 556.2 jit_solution(11867514326208278412)
XLA Ops:
  5.3 7.8 %all-to-all-start = ((bf16[8,128,768]{2,1,0:T(8,128)(2,1)}), bf16[8,128,768]{2,1,0:T(8,128)(2,1)S(1)}, u32[]{:S(2)}, u32[]{:S(2)}) async-start(bf16[8,128,768]{2,1,0:T(8,128)(2,1)} %copy-done.5), calls=%async_computation | async-start | bytes 3145728 | tf_op jit(solution)/shard_map/all_to_all | solution.py:69
  13.2 24.0 %all-to-all-done.rows_ref = bf16[8,128,768]{2,1,0:T(8,128)(2,1)S(1)} async-done(((bf16[8,128,768]{2,1,0:T(8,128)(2,1)}), bf16[8,128,768]{2,1,0:T(8,128)(2,1)S(1)}, u32[]{:S(2)}, u32[]{:S(2)}) %all-to-all-start) | async-done | bytes 1572896 | tf_op jit(solution)/shard_map/all_to_all | solution.py:69
  68.1 11.8 %collective-permute-done.5.refs_4_ = bf16[512,768]{1,0:T(8,128)(2,1)} collective-permute-done((bf16[512,768]{1,0:T(8,128)(2,1)}, bf16[512,768]{1,0:T(8,128)(2,1)}, u32[]{:S(2)}, u32[]{:S(2)}) %collective-permute-start.5) | collective-permute-done | bytes 786464 | tf_op jit(solution)/shard_map/ppermute | solution.py:134
  89.1 15.9 %collective-permute-done.10.refs_4_ = bf16[512,768]{1,0:T(8,128)(2,1)S(1)} collective-permute-done((bf16[512,768]{1,0:T(8,128)(2,1)S(1)}, bf16[512,768]{1,0:T(8,128)(2,1)S(1)}, u32[]{:S(2)}, u32[]{:S(2)}) %collective-permute-start.10) | collective-permute-done | bytes 786464 | tf_op jit(solution)/shard_map/ppermute | solution.py:134
  107.0 12.2 %collective-permute-done.7.refs_1_ = bf16[512,768]{1,0:T(8,128)(2,1)S(1)} collective-permute-done((bf16[512,768]{1,0:T(8,128)(2,1)}, bf16[512,768]{1,0:T(8,128)(2,1)S(1)}, u32[]{:S(2)}, u32[]{:S(2)}) %collective-permute-start.7) | collective-permute-done | bytes 786464 | tf_op jit(solution)/shard_map/ppermute | solution.py:134
  127.0 10.7 %collective-permute-done.12.refs_6_ = bf16[512,768]{1,0:T(8,128)(2,1)S(1)} collective-permute-done((bf16[512,768]{1,0:T(8,128)(2,1)S(1)}, bf16[512,768]{1,0:T(8,128)(2,1)S(1)}, u32[]{:S(2)}, u32[]{:S(2)}) %collective-permute-start.12) | collective-permute-done | bytes 786464 | tf_op jit(solution)/shard_map/ppermute | solution.py:134
  143.7 11.8 %all_to_all.85.blocks_ref = bf16[8,128,128]{2,1,0:T(8,128)(2,1)S(1)} all-to-all(bf16[8,128,128]{2,1,0:T(8,128)(2,1)S(1)} %copies.18), channel_id=1, replica_groups=mesh['section'=16,'tensor'=8] {'tensor'}, dimensions={0} | all-to-all | bytes 524288 | tf_op jit(solution)/shard_map/all_to_all | solution.py:69
  155.5 6.2 %turn.22 = (bf16[5,128,768]{2,1,0:T(8,128)(2,1)S(1)}, bf16[3,128,768]{2,1,0:T(8,128)(2,1)S(1)}, bf16[128,128]{1,0:T(8,128)(2,1)S(1)}, bf16[8,128,768]{2,1,0:T(8,128)(2,1)S(1)}) custom-call(s32[1]{0:T(128)} %bitcast.10.place_ref, bf16[8,128,128]{2,1,0:T(8,128)(2,1)S(1)} %all_to_all.85.blocks_ref, ...), custom_call_target="tpu_custom_call", output_to_operand_aliasing={{3}: (7, {})} | custom-call | flops 2818572288 | bytes 22020096 | tf_op jit(solution)/shard_map/turn/pallas_call | solution.py:308
  163.9 11.5 %all_to_all.86.blocks_ref = bf16[8,128,128]{2,1,0:T(8,128)(2,1)S(1)} all-to-all(bf16[8,128,128]{2,1,0:T(8,128)(2,1)S(1)} %copies.19), channel_id=1, replica_groups=mesh['section'=16,'tensor'=8] {'tensor'}, dimensions={0} | all-to-all | bytes 524288 | tf_op jit(solution)/shard_map/all_to_all | solution.py:69
  181.7 9.3 %collective-permute-start.20 = (bf16[128,128]{1,0:T(8,128)(2,1)S(1)}, bf16[128,128]{1,0:T(8,128)(2,1)S(1)}, u32[]{:S(2)}, u32[]{:S(2)}) collective-permute-start(bf16[128,128]{1,0:T(8,128)(2,1)S(1)} %get-tuple-element.185), channel_id=1, source_target_pairs={{0,8},{8,0},{16,24},{24,16},{32,40},{40,32},{48,56},{56,48},{64,72... | collective-permute-start | bytes 98312 | tf_op jit(solution)/shard_map/ppermute | solution.py:48
  192.4 12.0 %all_to_all.87.blocks_ref = bf16[8,128,128]{2,1,0:T(8,128)(2,1)S(1)} all-to-all(bf16[8,128,128]{2,1,0:T(8,128)(2,1)S(1)} %copies.20), channel_id=1, replica_groups=mesh['section'=16,'tensor'=8] {'tensor'}, dimensions={0} | all-to-all | bytes 524288 | tf_op jit(solution)/shard_map/all_to_all | solution.py:69
  204.4 6.2 %turn.25 = (bf16[5,128,768]{2,1,0:T(8,128)(2,1)S(1)}, bf16[3,128,768]{2,1,0:T(8,128)(2,1)S(1)}, bf16[128,128]{1,0:T(8,128)(2,1)S(1)}, bf16[8,128,768]{2,1,0:T(8,128)(2,1)S(1)}) custom-call(s32[1]{0:T(128)} %bitcast.10.place_ref, bf16[8,128,128]{2,1,0:T(8,128)(2,1)S(1)} %all_to_all.87.blocks_ref, ...), custom_call_target="tpu_custom_call", output_to_operand_aliasing={{3}: (7, {})} | custom-call | flops 2818572288 | bytes 22020096 | tf_op jit(solution)/shard_map/turn/pallas_call | solution.py:308
  212.8 11.3 %all_to_all.88.blocks_ref = bf16[8,128,128]{2,1,0:T(8,128)(2,1)S(1)} all-to-all(bf16[8,128,128]{2,1,0:T(8,128)(2,1)S(1)} %copies.21), channel_id=1, replica_groups=mesh['section'=16,'tensor'=8] {'tensor'}, dimensions={0} | all-to-all | bytes 524288 | tf_op jit(solution)/shard_map/all_to_all | solution.py:69
  230.3 9.5 %collective-permute-start.26 = (bf16[128,128]{1,0:T(8,128)(2,1)S(1)}, bf16[128,128]{1,0:T(8,128)(2,1)S(1)}, u32[]{:S(2)}, u32[]{:S(2)}) collective-permute-start(bf16[128,128]{1,0:T(8,128)(2,1)S(1)} %get-tuple-element.201), channel_id=1, source_target_pairs={{0,8},{8,0},{16,24},{24,16},{32,40},{40,32},{48,56},{56,48},{64,72... | collective-permute-start | bytes 98312 | tf_op jit(solution)/shard_map/ppermute | solution.py:48
  241.3 12.0 %all_to_all.89.blocks_ref = bf16[8,128,128]{2,1,0:T(8,128)(2,1)S(1)} all-to-all(bf16[8,128,128]{2,1,0:T(8,128)(2,1)S(1)} %copies.22), channel_id=1, replica_groups=mesh['section'=16,'tensor'=8] {'tensor'}, dimensions={0} | all-to-all | bytes 524288 | tf_op jit(solution)/shard_map/all_to_all | solution.py:69
  253.3 6.2 %turn.28 = (bf16[5,128,768]{2,1,0:T(8,128)(2,1)S(1)}, bf16[3,128,768]{2,1,0:T(8,128)(2,1)S(1)}, bf16[128,128]{1,0:T(8,128)(2,1)S(1)}, bf16[8,128,768]{2,1,0:T(8,128)(2,1)S(1)}) custom-call(s32[1]{0:T(128)} %bitcast.10.place_ref, bf16[8,128,128]{2,1,0:T(8,128)(2,1)S(1)} %all_to_all.89.blocks_ref, ...), custom_call_target="tpu_custom_call", output_to_operand_aliasing={{3}: (7, {})} | custom-call | flops 2818572288 | bytes 22020096 | tf_op jit(solution)/shard_map/turn/pallas_call | solution.py:308
  261.7 11.3 %all_to_all.90.blocks_ref = bf16[8,128,128]{2,1,0:T(8,128)(2,1)S(1)} all-to-all(bf16[8,128,128]{2,1,0:T(8,128)(2,1)S(1)} %copies.23), channel_id=1, replica_groups=mesh['section'=16,'tensor'=8] {'tensor'}, dimensions={0} | all-to-all | bytes 524288 | tf_op jit(solution)/shard_map/all_to_all | solution.py:69
  279.2 11.0 %collective-permute-start.32 = (bf16[128,128]{1,0:T(8,128)(2,1)S(1)}, bf16[128,128]{1,0:T(8,128)(2,1)S(1)}, u32[]{:S(2)}, u32[]{:S(2)}) collective-permute-start(bf16[128,128]{1,0:T(8,128)(2,1)S(1)} %get-tuple-element.217), channel_id=1, source_target_pairs={{0,8},{8,0},{16,24},{24,16},{32,40},{40,32},{48,56},{56,48},{64,72... | collective-permute-start | bytes 98312 | tf_op jit(solution)/shard_map/ppermute | solution.py:48
  291.6 12.0 %all_to_all.91.blocks_ref = bf16[8,128,128]{2,1,0:T(8,128)(2,1)S(1)} all-to-all(bf16[8,128,128]{2,1,0:T(8,128)(2,1)S(1)} %copies.24), channel_id=1, replica_groups=mesh['section'=16,'tensor'=8] {'tensor'}, dimensions={0} | all-to-all | bytes 524288 | tf_op jit(solution)/shard_map/all_to_all | solution.py:69
  303.6 6.2 %turn.31 = (bf16[5,128,768]{2,1,0:T(8,128)(2,1)S(1)}, bf16[3,128,768]{2,1,0:T(8,128)(2,1)S(1)}, bf16[128,128]{1,0:T(8,128)(2,1)S(1)}, bf16[8,128,768]{2,1,0:T(8,128)(2,1)S(1)}) custom-call(s32[1]{0:T(128)} %bitcast.10.place_ref, bf16[8,128,128]{2,1,0:T(8,128)(2,1)S(1)} %all_to_all.91.blocks_ref, ...), custom_call_target="tpu_custom_call", output_to_operand_aliasing={{3}: (7, {})} | custom-call | flops 2818572288 | bytes 22020096 | tf_op jit(solution)/shard_map/turn/pallas_call | solution.py:308
  312.0 11.6 %all_to_all.92.blocks_ref = bf16[8,128,128]{2,1,0:T(8,128)(2,1)S(1)} all-to-all(bf16[8,128,128]{2,1,0:T(8,128)(2,1)S(1)} %copies.25), channel_id=1, replica_groups=mesh['section'=16,'tensor'=8] {'tensor'}, dimensions={0} | all-to-all | bytes 524288 | tf_op jit(solution)/shard_map/all_to_all | solution.py:69
  331.7 11.9 %all_to_all.93.blocks_ref = bf16[8,128,128]{2,1,0:T(8,128)(2,1)S(1)} all-to-all(bf16[8,128,128]{2,1,0:T(8,128)(2,1)S(1)} %copies.26), channel_id=1, replica_groups=mesh['section'=16,'tensor'=8] {'tensor'}, dimensions={0} | all-to-all | bytes 524288 | tf_op jit(solution)/shard_map/all_to_all | solution.py:69
  352.0 27.4 %all_to_all.94.blocks_ref = bf16[8,128,128]{2,1,0:T(8,128)(2,1)S(1)} all-to-all(bf16[8,128,128]{2,1,0:T(8,128)(2,1)S(1)} %copies.27), channel_id=1, replica_groups=mesh['section'=16,'tensor'=8] {'tensor'}, dimensions={0} | all-to-all | bytes 524288 | tf_op jit(solution)/shard_map/all_to_all | solution.py:69
  387.5 11.8 %all_to_all.95.blocks_ref = bf16[8,128,128]{2,1,0:T(8,128)(2,1)S(1)} all-to-all(bf16[8,128,128]{2,1,0:T(8,128)(2,1)S(1)} %copies.28), channel_id=1, replica_groups=mesh['section'=16,'tensor'=8] {'tensor'}, dimensions={0} | all-to-all | bytes 524288 | tf_op jit(solution)/shard_map/all_to_all | solution.py:69
  407.7 11.3 %all_to_all.96.blocks_ref = bf16[8,128,128]{2,1,0:T(8,128)(2,1)S(1)} all-to-all(bf16[8,128,128]{2,1,0:T(8,128)(2,1)S(1)} %copies.29), channel_id=1, replica_groups=mesh['section'=16,'tensor'=8] {'tensor'}, dimensions={0} | all-to-all | bytes 524288 | tf_op jit(solution)/shard_map/all_to_all | solution.py:69
  425.3 9.5 %collective-permute-start.50 = (bf16[128,128]{1,0:T(8,128)(2,1)S(1)}, bf16[128,128]{1,0:T(8,128)(2,1)S(1)}, u32[]{:S(2)}, u32[]{:S(2)}) collective-permute-start(bf16[128,128]{1,0:T(8,128)(2,1)S(1)} %get-tuple-element.265), channel_id=1, source_target_pairs={{0,8},{8,0},{16,24},{24,16},{32,40},{40,32},{48,56},{56,48},{64,72... | collective-permute-start | bytes 98312 | tf_op jit(solution)/shard_map/ppermute | solution.py:48
  436.2 12.0 %all_to_all.97.blocks_ref = bf16[8,128,128]{2,1,0:T(8,128)(2,1)S(1)} all-to-all(bf16[8,128,128]{2,1,0:T(8,128)(2,1)S(1)} %copies.30), channel_id=1, replica_groups=mesh['section'=16,'tensor'=8] {'tensor'}, dimensions={0} | all-to-all | bytes 524288 | tf_op jit(solution)/shard_map/all_to_all | solution.py:69
  456.6 11.6 %all_to_all.98.blocks_ref = bf16[8,128,128]{2,1,0:T(8,128)(2,1)S(1)} all-to-all(bf16[8,128,128]{2,1,0:T(8,128)(2,1)S(1)} %copies.31), channel_id=1, replica_groups=mesh['section'=16,'tensor'=8] {'tensor'}, dimensions={0} | all-to-all | bytes 524288 | tf_op jit(solution)/shard_map/all_to_all | solution.py:69
  474.4 43.8 %collective-permute-start.56 = (bf16[128,128]{1,0:T(8,128)(2,1)S(1)}, bf16[128,128]{1,0:T(8,128)(2,1)S(1)}, u32[]{:S(2)}, u32[]{:S(2)}) collective-permute-start(bf16[128,128]{1,0:T(8,128)(2,1)S(1)} %get-tuple-element.281), channel_id=1, source_target_pairs={{0,8},{8,0},{16,24},{24,16},{32,40},{40,32},{48,56},{56,48},{64,72... | collective-permute-start | bytes 98312 | tf_op jit(solution)/shard_map/ppermute | solution.py:48
  519.6 12.0 %all_to_all.99.blocks_ref = bf16[8,128,128]{2,1,0:T(8,128)(2,1)S(1)} all-to-all(bf16[8,128,128]{2,1,0:T(8,128)(2,1)S(1)} %copies.32), channel_id=1, replica_groups=mesh['section'=16,'tensor'=8] {'tensor'}, dimensions={0} | all-to-all | bytes 524288 | tf_op jit(solution)/shard_map/all_to_all | solution.py:69
  531.6 9.3 %turn.43 = (bf16[5,128,768]{2,1,0:T(8,128)(2,1)}, bf16[3,128,768]{2,1,0:T(8,128)(2,1)}, bf16[128,128]{1,0:T(8,128)(2,1)S(1)}, bf16[8,128,768]{2,1,0:T(8,128)(2,1)S(1)}) custom-call(s32[1]{0:T(128)} %bitcast.10.place_ref, bf16[8,128,128]{2,1,0:T(8,128)(2,1)S(1)} %all_to_all.99.blocks_ref, ...), custom_call_target="tpu_custom_call", output_to_operand_aliasing={{3}: (7, {})} | custom-call | flops 2818572288 | bytes 22020096 | tf_op jit(solution)/shard_map/turn/pallas_call | solution.py:308
  546.2 6.3 %weight_grads.1 = bf16[768,6144]{1,0:T(8,128)(2,1)} custom-call(bf16[768,128]{1,0:T(8,128)(2,1)S(1)} %copy-done.8, bf16[8,128,768]{2,1,0:T(8,128)(2,1)S(1)} %get-tuple-element.287.rows_ref), custom_call_target="tpu_custom_call" | custom-call | flops 1207959552 | bytes 9437184 | tf_op jit(solution)/shard_map/weight_grads/pallas_call | solution.py:418
  (200 shorter events, 156.8 us)
Async XLA Ops:
  2.7 34.5 %collective-permute-start = (bf16[1024,768]{1,0:T(8,128)(2,1)S(1)}, bf16[1024,768]{1,0:T(8,128)(2,1)}, u32[]{:S(2)}, u32[]{:S(2)}) collective-permute-start(bf16[1024,768]{1,0:T(8,128)(2,1)S(1)} %transposed.3.value_t_ref), channel_id=1, source_target_pairs={{8,0},{16,8},{24,16},{32,24},{40,32},{48,40},{56,48},{64,56},{72,6... | collective-permute-start | bytes 4718600 | tf_op jit(solution)/shard_map/ppermute | solution.py:459
  5.3 31.9 %all-to-all-start = ((bf16[8,128,768]{2,1,0:T(8,128)(2,1)}), bf16[8,128,768]{2,1,0:T(8,128)(2,1)S(1)}, u32[]{:S(2)}, u32[]{:S(2)}) async-start(bf16[8,128,768]{2,1,0:T(8,128)(2,1)} %copy-done.5), calls=%async_computation | async-start | bytes 3145728 | tf_op jit(solution)/shard_map/all_to_all | solution.py:69
  37.3 46.0 %collective-permute-start.1 = (bf16[1024,768]{1,0:T(8,128)(2,1)}, bf16[1024,768]{1,0:T(8,128)(2,1)}, u32[]{:S(2)}, u32[]{:S(2)}) collective-permute-start(bf16[1024,768]{1,0:T(8,128)(2,1)} %collective-permute-done.refs_0_), channel_id=1, source_target_pairs={{0,4},{1,5},{2,6},{3,7},{4,0},{5,1},{6,2},{7,3},{8,12},{9,13},{10,... | collective-permute-start | bytes 4718600 | tf_op jit(solution)/shard_map/ppermute | solution.py:134
  41.0 23.3 %collective-permute-start.3 = (bf16[512,768]{1,0:T(8,128)(2,1)}, bf16[512,768]{1,0:T(8,128)(2,1)}, u32[]{:S(2)}, u32[]{:S(2)}) collective-permute-start(bf16[512,768]{1,0:T(8,128)(2,1)} %get-tuple-element.151), channel_id=1, source_target_pairs={{0,3},{1,0},{2,1},{3,2},{4,7},{5,4},{6,5},{7,6},{8,11},{9,8},{10,9... | collective-permute-start | bytes 2359304 | tf_op jit(solution)/shard_map/ppermute | solution.py:134
  46.1 22.0 %collective-permute-start.2 = (bf16[512,768]{1,0:T(8,128)(2,1)}, bf16[512,768]{1,0:T(8,128)(2,1)}, u32[]{:S(2)}, u32[]{:S(2)}) collective-permute-start(bf16[512,768]{1,0:T(8,128)(2,1)} %get-tuple-element.151), channel_id=1, source_target_pairs={{0,1},{1,2},{2,3},{3,0},{4,5},{5,6},{6,7},{7,4},{8,9},{9,10},{10,1... | collective-permute-start | bytes 2359304 | tf_op jit(solution)/shard_map/ppermute | solution.py:134
  46.1 33.8 %collective-permute-start.5 = (bf16[512,768]{1,0:T(8,128)(2,1)}, bf16[512,768]{1,0:T(8,128)(2,1)}, u32[]{:S(2)}, u32[]{:S(2)}) collective-permute-start(bf16[512,768]{1,0:T(8,128)(2,1)} %get-tuple-element.152), channel_id=1, source_target_pairs={{0,3},{1,0},{2,1},{3,2},{4,7},{5,4},{6,5},{7,6},{8,11},{9,8},{10,9... | collective-permute-start | bytes 2359304 | tf_op jit(solution)/shard_map/ppermute | solution.py:134
  49.3 34.0 %collective-permute-start.4 = (bf16[512,768]{1,0:T(8,128)(2,1)}, bf16[512,768]{1,0:T(8,128)(2,1)}, u32[]{:S(2)}, u32[]{:S(2)}) collective-permute-start(bf16[512,768]{1,0:T(8,128)(2,1)} %get-tuple-element.152), channel_id=1, source_target_pairs={{0,1},{1,2},{2,3},{3,0},{4,5},{5,6},{6,7},{7,4},{8,9},{9,10},{10,1... | collective-permute-start | bytes 2359304 | tf_op jit(solution)/shard_map/ppermute | solution.py:134
  84.4 20.5 %collective-permute-start.10 = (bf16[512,768]{1,0:T(8,128)(2,1)S(1)}, bf16[512,768]{1,0:T(8,128)(2,1)S(1)}, u32[]{:S(2)}, u32[]{:S(2)}) collective-permute-start(bf16[512,768]{1,0:T(8,128)(2,1)S(1)} %slice.20), channel_id=1, source_target_pairs={{0,3},{1,0},{2,1},{3,2},{4,7},{5,4},{6,5},{7,6},{8,11},{9,8},{10,9... | collective-permute-start | bytes 2359304 | tf_op jit(solution)/shard_map/ppermute | solution.py:134
  84.8 21.7 %collective-permute-start.8 = (bf16[512,768]{1,0:T(8,128)(2,1)S(1)}, bf16[512,768]{1,0:T(8,128)(2,1)S(1)}, u32[]{:S(2)}, u32[]{:S(2)}) collective-permute-start(bf16[512,768]{1,0:T(8,128)(2,1)S(1)} %slice.20), channel_id=1, source_target_pairs={{0,1},{1,2},{2,3},{3,0},{4,5},{5,6},{6,7},{7,4},{8,9},{9,10},{10,1... | collective-permute-start | bytes 2359304 | tf_op jit(solution)/shard_map/ppermute | solution.py:134
  86.5 32.7 %collective-permute-start.7 = (bf16[512,768]{1,0:T(8,128)(2,1)}, bf16[512,768]{1,0:T(8,128)(2,1)S(1)}, u32[]{:S(2)}, u32[]{:S(2)}) collective-permute-start(bf16[512,768]{1,0:T(8,128)(2,1)} %collective-permute-done.5.refs_4_), channel_id=1, source_target_pairs={{0,3},{1,0},{2,1},{3,2},{4,7},{5,4},{6,5},{7,6},{8,11},{9,8},{10,9... | collective-permute-start | bytes 2359304 | tf_op jit(solution)/shard_map/ppermute | solution.py:134
  88.0 38.9 %collective-permute-start.11 = (bf16[512,768]{1,0:T(8,128)(2,1)}, bf16[512,768]{1,0:T(8,128)(2,1)S(1)}, u32[]{:S(2)}, u32[]{:S(2)}) collective-permute-start(bf16[512,768]{1,0:T(8,128)(2,1)} %collective-permute-done.5.refs_4_), channel_id=1, source_target_pairs={{0,4},{1,5},{2,6},{3,7},{4,0},{5,1},{6,2},{7,3},{8,12},{9,13},{10,... | collective-permute-start | bytes 2359304 | tf_op jit(solution)/shard_map/ppermute | solution.py:134
  88.6 34.7 %collective-permute-start.6 = (bf16[512,768]{1,0:T(8,128)(2,1)}, bf16[512,768]{1,0:T(8,128)(2,1)S(1)}, u32[]{:S(2)}, u32[]{:S(2)}) collective-permute-start(bf16[512,768]{1,0:T(8,128)(2,1)} %collective-permute-done.2.refs_1_), channel_id=1, source_target_pairs={{0,1},{1,2},{2,3},{3,0},{4,5},{5,6},{6,7},{7,4},{8,9},{9,10},{10,1... | collective-permute-start | bytes 2359304 | tf_op jit(solution)/shard_map/ppermute | solution.py:134
  105.0 22.0 %collective-permute-start.9 = (bf16[512,768]{1,0:T(8,128)(2,1)}, bf16[512,768]{1,0:T(8,128)(2,1)S(1)}, u32[]{:S(2)}, u32[]{:S(2)}) collective-permute-start(bf16[512,768]{1,0:T(8,128)(2,1)} %collective-permute-done.4.refs_2_), channel_id=1, source_target_pairs={{0,4},{1,5},{2,6},{3,7},{4,0},{5,1},{6,2},{7,3},{8,12},{9,13},{10,... | collective-permute-start | bytes 2359304 | tf_op jit(solution)/shard_map/ppermute | solution.py:134
  106.5 31.1 %collective-permute-start.12 = (bf16[512,768]{1,0:T(8,128)(2,1)S(1)}, bf16[512,768]{1,0:T(8,128)(2,1)S(1)}, u32[]{:S(2)}, u32[]{:S(2)}) collective-permute-start(bf16[512,768]{1,0:T(8,128)(2,1)S(1)} %collective-permute-done.8.refs_2_), channel_id=1, source_target_pairs={{0,1},{1,2},{2,3},{3,0},{4,5},{5,6},{6,7},{7,4},{8,9},{9,10},{10,1... | collective-permute-start | bytes 2359304 | tf_op jit(solution)/shard_map/ppermute | solution.py:134
  119.3 21.6 %collective-permute-start.13 = (bf16[512,768]{1,0:T(8,128)(2,1)S(1)}, bf16[512,768]{1,0:T(8,128)(2,1)S(1)}, u32[]{:S(2)}, u32[]{:S(2)}) collective-permute-start(bf16[512,768]{1,0:T(8,128)(2,1)S(1)} %collective-permute-done.7.refs_1_), channel_id=1, source_target_pairs={{0,4},{1,5},{2,6},{3,7},{4,0},{5,1},{6,2},{7,3},{8,12},{9,13},{10,... | collective-permute-start | bytes 2359304 | tf_op jit(solution)/shard_map/ppermute | solution.py:134
  162.5 13.0 %collective-permute-start.18 = (bf16[5,128,768]{2,1,0:T(8,128)(2,1)S(1)}, bf16[5,128,768]{2,1,0:T(8,128)(2,1)S(1)}, u32[]{:S(2)}, u32[]{:S(2)}) collective-permute-start(bf16[5,128,768]{2,1,0:T(8,128)(2,1)S(1)} %get-tuple-element.178), channel_id=1, source_target_pairs={{0,0},{8,16},{16,8},{24,32},{32,24},{40,48},{48,40},{56,56},{64,64... | collective-permute-start | bytes 2949128 | tf_op jit(solution)/shard_map/ppermute | solution.py:48
  163.2 16.0 %collective-permute-start.19 = (bf16[3,128,768]{2,1,0:T(8,128)(2,1)S(1)}, bf16[3,128,768]{2,1,0:T(8,128)(2,1)S(1)}, u32[]{:S(2)}, u32[]{:S(2)}) collective-permute-start(bf16[3,128,768]{2,1,0:T(8,128)(2,1)S(1)} %get-tuple-element.181), channel_id=1, source_target_pairs={{0,0},{8,16},{16,8},{24,32},{32,24},{40,48},{48,40},{56,56},{64,64... | collective-permute-start | bytes 1769480 | tf_op jit(solution)/shard_map/ppermute | solution.py:48
  191.8 12.5 %collective-permute-start.21 = (bf16[5,128,768]{2,1,0:T(8,128)(2,1)S(1)}, bf16[5,128,768]{2,1,0:T(8,128)(2,1)S(1)}, u32[]{:S(2)}, u32[]{:S(2)}) collective-permute-start(bf16[5,128,768]{2,1,0:T(8,128)(2,1)S(1)} %get-tuple-element.187), channel_id=1, source_target_pairs={{0,8},{8,0},{16,24},{24,16},{32,40},{40,32},{48,56},{56,48},{64,72... | collective-permute-start | bytes 2949128 | tf_op jit(solution)/shard_map/ppermute | solution.py:48
  211.3 12.8 %collective-permute-start.24 = (bf16[5,128,768]{2,1,0:T(8,128)(2,1)S(1)}, bf16[5,128,768]{2,1,0:T(8,128)(2,1)S(1)}, u32[]{:S(2)}, u32[]{:S(2)}) collective-permute-start(bf16[5,128,768]{2,1,0:T(8,128)(2,1)S(1)} %get-tuple-element.194), channel_id=1, source_target_pairs={{0,0},{8,16},{16,8},{24,32},{32,24},{40,48},{48,40},{56,56},{64,64... | collective-permute-start | bytes 2949128 | tf_op jit(solution)/shard_map/ppermute | solution.py:48
  212.0 15.8 %collective-permute-start.25 = (bf16[3,128,768]{2,1,0:T(8,128)(2,1)S(1)}, bf16[3,128,768]{2,1,0:T(8,128)(2,1)S(1)}, u32[]{:S(2)}, u32[]{:S(2)}) collective-permute-start(bf16[3,128,768]{2,1,0:T(8,128)(2,1)S(1)} %get-tuple-element.197), channel_id=1, source_target_pairs={{0,0},{8,16},{16,8},{24,32},{32,24},{40,48},{48,40},{56,56},{64,64... | collective-permute-start | bytes 1769480 | tf_op jit(solution)/shard_map/ppermute | solution.py:48
  240.7 12.5 %collective-permute-start.27 = (bf16[5,128,768]{2,1,0:T(8,128)(2,1)S(1)}, bf16[5,128,768]{2,1,0:T(8,128)(2,1)S(1)}, u32[]{:S(2)}, u32[]{:S(2)}) collective-permute-start(bf16[5,128,768]{2,1,0:T(8,128)(2,1)S(1)} %get-tuple-element.203), channel_id=1, source_target_pairs={{0,8},{8,0},{16,24},{24,16},{32,40},{40,32},{48,56},{56,48},{64,72... | collective-permute-start | bytes 2949128 | tf_op jit(solution)/shard_map/ppermute | solution.py:48
  260.2 12.8 %collective-permute-start.30 = (bf16[5,128,768]{2,1,0:T(8,128)(2,1)S(1)}, bf16[5,128,768]{2,1,0:T(8,128)(2,1)S(1)}, u32[]{:S(2)}, u32[]{:S(2)}) collective-permute-start(bf16[5,128,768]{2,1,0:T(8,128)(2,1)S(1)} %get-tuple-element.210), channel_id=1, source_target_pairs={{0,0},{8,16},{16,8},{24,32},{32,24},{40,48},{48,40},{56,56},{64,64... | collective-permute-start | bytes 2949128 | tf_op jit(solution)/shard_map/ppermute | solution.py:48
  260.9 15.8 %collective-permute-start.31 = (bf16[3,128,768]{2,1,0:T(8,128)(2,1)S(1)}, bf16[3,128,768]{2,1,0:T(8,128)(2,1)S(1)}, u32[]{:S(2)}, u32[]{:S(2)}) collective-permute-start(bf16[3,128,768]{2,1,0:T(8,128)(2,1)S(1)} %get-tuple-element.213), channel_id=1, source_target_pairs={{0,0},{8,16},{16,8},{24,32},{32,24},{40,48},{48,40},{56,56},{64,64... | collective-permute-start | bytes 1769480 | tf_op jit(solution)/shard_map/ppermute | solution.py:48
  310.5 13.1 %collective-permute-start.36 = (bf16[5,128,768]{2,1,0:T(8,128)(2,1)S(1)}, bf16[5,128,768]{2,1,0:T(8,128)(2,1)S(1)}, u32[]{:S(2)}, u32[]{:S(2)}) collective-permute-start(bf16[5,128,768]{2,1,0:T(8,128)(2,1)S(1)} %get-tuple-element.226), channel_id=1, source_target_pairs={{0,0},{8,8},{16,16},{24,24},{32,32},{40,40},{48,48},{56,64},{64,56... | collective-permute-start | bytes 2949128 | tf_op jit(solution)/shard_map/ppermute | solution.py:48
  311.3 16.1 %collective-permute-start.37 = (bf16[3,128,768]{2,1,0:T(8,128)(2,1)S(1)}, bf16[3,128,768]{2,1,0:T(8,128)(2,1)S(1)}, u32[]{:S(2)}, u32[]{:S(2)}) collective-permute-start(bf16[3,128,768]{2,1,0:T(8,128)(2,1)S(1)} %get-tuple-element.229), channel_id=1, source_target_pairs={{0,0},{8,8},{16,16},{24,24},{32,32},{40,40},{48,48},{56,64},{64,56... | collective-permute-start | bytes 1769480 | tf_op jit(solution)/shard_map/ppermute | solution.py:48
  350.5 28.9 %collective-permute-start.42 = (bf16[5,128,768]{2,1,0:T(8,128)(2,1)S(1)}, bf16[5,128,768]{2,1,0:T(8,128)(2,1)S(1)}, u32[]{:S(2)}, u32[]{:S(2)}) collective-permute-start(bf16[5,128,768]{2,1,0:T(8,128)(2,1)S(1)} %get-tuple-element.242), channel_id=1, source_target_pairs={{0,0},{8,16},{16,8},{24,32},{32,24},{40,48},{48,40},{56,56},{64,64... | collective-permute-start | bytes 2949128 | tf_op jit(solution)/shard_map/ppermute | solution.py:48
  351.3 31.9 %collective-permute-start.43 = (bf16[3,128,768]{2,1,0:T(8,128)(2,1)S(1)}, bf16[3,128,768]{2,1,0:T(8,128)(2,1)S(1)}, u32[]{:S(2)}, u32[]{:S(2)}) collective-permute-start(bf16[3,128,768]{2,1,0:T(8,128)(2,1)S(1)} %get-tuple-element.245), channel_id=1, source_target_pairs={{0,0},{8,16},{16,8},{24,32},{32,24},{40,48},{48,40},{56,56},{64,64... | collective-permute-start | bytes 1769480 | tf_op jit(solution)/shard_map/ppermute | solution.py:48
  406.2 12.8 %collective-permute-start.48 = (bf16[5,128,768]{2,1,0:T(8,128)(2,1)S(1)}, bf16[5,128,768]{2,1,0:T(8,128)(2,1)S(1)}, u32[]{:S(2)}, u32[]{:S(2)}) collective-permute-start(bf16[5,128,768]{2,1,0:T(8,128)(2,1)S(1)} %get-tuple-element.258), channel_id=1, source_target_pairs={{0,0},{8,16},{16,8},{24,32},{32,24},{40,48},{48,40},{56,56},{64,64... | collective-permute-start | bytes 2949128 | tf_op jit(solution)/shard_map/ppermute | solution.py:48
  407.0 15.8 %collective-permute-start.49 = (bf16[3,128,768]{2,1,0:T(8,128)(2,1)S(1)}, bf16[3,128,768]{2,1,0:T(8,128)(2,1)S(1)}, u32[]{:S(2)}, u32[]{:S(2)}) collective-permute-start(bf16[3,128,768]{2,1,0:T(8,128)(2,1)S(1)} %get-tuple-element.261), channel_id=1, source_target_pairs={{0,0},{8,16},{16,8},{24,32},{32,24},{40,48},{48,40},{56,56},{64,64... | collective-permute-start | bytes 1769480 | tf_op jit(solution)/shard_map/ppermute | solution.py:48
  455.1 13.1 %collective-permute-start.54 = (bf16[5,128,768]{2,1,0:T(8,128)(2,1)S(1)}, bf16[5,128,768]{2,1,0:T(8,128)(2,1)S(1)}, u32[]{:S(2)}, u32[]{:S(2)}) collective-permute-start(bf16[5,128,768]{2,1,0:T(8,128)(2,1)S(1)} %get-tuple-element.274), channel_id=1, source_target_pairs={{0,0},{8,16},{16,8},{24,32},{32,24},{40,48},{48,40},{56,56},{64,64... | collective-permute-start | bytes 2949128 | tf_op jit(solution)/shard_map/ppermute | solution.py:48
  455.8 16.1 %collective-permute-start.55 = (bf16[3,128,768]{2,1,0:T(8,128)(2,1)S(1)}, bf16[3,128,768]{2,1,0:T(8,128)(2,1)S(1)}, u32[]{:S(2)}, u32[]{:S(2)}) collective-permute-start(bf16[3,128,768]{2,1,0:T(8,128)(2,1)S(1)} %get-tuple-element.277), channel_id=1, source_target_pairs={{0,0},{8,16},{16,8},{24,32},{32,24},{40,48},{48,40},{56,56},{64,64... | collective-permute-start | bytes 1769480 | tf_op jit(solution)/shard_map/ppermute | solution.py:48
  474.4 44.7 %collective-permute-start.56 = (bf16[128,128]{1,0:T(8,128)(2,1)S(1)}, bf16[128,128]{1,0:T(8,128)(2,1)S(1)}, u32[]{:S(2)}, u32[]{:S(2)}) collective-permute-start(bf16[128,128]{1,0:T(8,128)(2,1)S(1)} %get-tuple-element.281), channel_id=1, source_target_pairs={{0,8},{8,0},{16,24},{24,16},{32,40},{40,32},{48,56},{56,48},{64,72... | collective-permute-start | bytes 98312 | tf_op jit(solution)/shard_map/ppermute | solution.py:48
  (44 other events, 390.3 us)

commit v6 on v5

--- a/solution.py
+++ b/solution.py
@@ -93,9 +93,15 @@
 def place_kernel(spots, given, index_ref, *refs):
     pieces, out_ref, sems = refs[:given], refs[-2], refs[-1]
     copies = []
-    for i, (piece, (slot, row)) in enumerate(zip(pieces, spots)):
-        goal = out_ref.at[index_ref[slot], pl.ds(row, piece.shape[0])]
-        copies.append(pltpu.make_async_copy(piece, goal, sems.at[i]))
+    for piece, (slot, runs) in zip(pieces, spots):
+        for source, length, goal in runs:
+            copies.append(
+                pltpu.make_async_copy(
+                    piece.at[pl.ds(source, length)],
+                    out_ref.at[index_ref[slot], pl.ds(goal, length)],
+                    sems.at[len(copies)],
+                )
+            )
     for copy in copies:
         copy.start()
     for copy in copies:
@@ -112,7 +118,7 @@
         + [pl.BlockSpec(memory_space=pl.ANY)] * (len(arrays) + len(more)),
         out_specs=pl.BlockSpec(memory_space=pl.ANY),
         out_shape=jax.ShapeDtypeStruct(shape, arrays[0].dtype),
-        scratch_shapes=[pltpu.SemaphoreType.DMA((len(arrays),))],
+        scratch_shapes=[pltpu.SemaphoreType.DMA((sum(len(runs) for _, runs in spots),))],
         input_output_aliases={1 + len(arrays): 0} if more else {},
         compiler_params=pltpu.CompilerParams(vmem_limit_bytes=1 << 20),
         cost_estimate=pl.CostEstimate(
@@ -134,10 +140,13 @@
     return lax.ppermute(value, "tensor", pairs)
 
 
-def gather_back(index, whole, halves, beside):
-    n, k = whole.shape
-    half = n // 2
-    low, high = halves
+def gather_both(index, back, top, beside):
+    n, k = back.shape
+    m = top.shape[0]
+    whole = jnp.concatenate([back[: n // 2], top[: m // 2], back[n // 2 :], top[m // 2 :]])
+    whole = lax.optimization_barrier(whole)
+    half = (n + m) // 2
+    low, high = lax.optimization_barrier((whole[:half], whole[half:]))
     other = across(whole, 0, 1)
     left_low, right_low = across(low, 1), across(low, -1)
     left_high, right_high = across(high, 1), across(high, -1)
@@ -147,18 +156,21 @@
     cross_left, cross_right = across(left_high, 0, 1), across(right_high, 0, 1)
     far_high, far_low = across(right_high, -1), across(left_low, 1)
     next_left, next_right = across(other[:half], 1), across(other[:half], -1)
+    whole, far_high = lax.optimization_barrier((whole, far_high))
+    lows = [(0, n // 2, 0), (n // 2, m // 2, n)]
+    highs = [(0, n // 2, n // 2), (n // 2, m // 2, n + m // 2)]
+    both = lows + [(half + source, length, goal) for source, length, goal in highs]
     early = [
-        (whole, 0, 0), (left_low, 1, 0), (left_high, 1, half),
-        (right_low, 2, 0), (right_high, 2, half), (other, 4, 0),
+        (whole, 0, both), (left_low, 1, lows), (left_high, 1, highs),
+        (right_low, 2, lows), (right_high, 2, highs), (other, 4, both),
     ]
     late = [
-        (far_low, 3, 0), (far_high, 3, half),
-        (next_left, 5, 0), (cross_left, 5, half), (next_right, 6, 0), (cross_right, 6, half),
-        (across(next_left, 1), 7, 0), (across(far_high, 0, 1), 7, half),
+        (far_low, 3, lows), (far_high, 3, highs),
+        (next_left, 5, lows), (cross_left, 5, highs),
+        (next_right, 6, lows), (cross_right, 6, highs),
+        (across(next_left, 1), 7, lows), (across(far_high, 0, 1), 7, highs),
     ]
-    shape = (lax.axis_size("tensor"), n, k)
-    whole, far_high = lax.optimization_barrier((whole, far_high))
-    early[0], late[1] = (whole, 0, 0), (far_high, 3, half)
+    shape = (lax.axis_size("tensor"), n + m, k)
     return put(index, late, shape, put(index, early, shape)), beside
 
 
@@ -253,8 +265,8 @@
     return pltpu.CompilerParams(vmem_limit_bytes=16 << 20)
 
 
-def plain_turn(section, place, rows, weight_t, probs_t, saved):
-    steps, count, tile = rows.shape
+def plain_turn(section, place, both, count, weight_t, probs_t, saved):
+    steps, length, tile = both.shape
     own = weight_t.shape[1]
     head_size = 128
     return pl.pallas_call(
@@ -262,7 +274,7 @@
         grid=(steps,),
         in_specs=[
             pl.BlockSpec(memory_space=pltpu.SMEM),
-            pl.BlockSpec((1, count, tile), lambda i: (i, 0, 0)),
+            pl.BlockSpec((1, count, tile), lambda i: (i, length // count - 1, 0)),
             pl.BlockSpec((tile, own), lambda i: (i, 0)),
             pl.BlockSpec(probs_t.shape, lambda i: (0, 0, 0)),
             pl.BlockSpec(memory_space=pl.ANY),
@@ -284,14 +296,14 @@
             transcendentals=0,
         ),
         name="plain_turn",
-    )(place, rows, weight_t, probs_t, saved)
+    )(place, both, weight_t, probs_t, saved)
 
 
 def turn(section, place, blocks, rows, back, weight_t, probs_t, saved, first=0, total=None, ends=True):
     count, tile = rows[0].shape[1:]
     own = weight_t.shape[1]
-    depth = back.shape[1]
     head_size = blocks.shape[2]
+    depth = blocks.shape[0] * head_size
     steps = [part.shape[0] for part in rows]
     parts = [pl.BlockSpec((1, count, tile), lambda i: (jnp.minimum(i, steps[0] - 1), 0, 0))]
     if len(rows) == 2:
@@ -455,28 +467,20 @@
         ]
     ).astype(jnp.int32)
     value_t = transposed(value_weight[0])
-    top, value_t = lax.optimization_barrier((grad_top.reshape(rows, feat_local), value_t))
-    whole = lax.ppermute(value_t, "section", [(i, i - 1) for i in range(1, sections)])
-    incoming = blocks_of_all(top)
+    back = lax.ppermute(value_t, "section", [(i, i - 1) for i in range(1, sections)])
+    back, index, spot, mine = lax.optimization_barrier((back, index, spot, mine))
     query_heads = query[0].reshape(micro_batch, length, group, head_size)
     probs = jax.vmap(causal_probs)(query_heads, keys[0])
     mixed = jnp.einsum("mgqp,mpd->mqgd", probs, values[0], preferred_element_type=F32)
     mixed_t = transposed(mixed.astype(BF16).reshape(rows, group * head_size), group * head_size)
     probs_t = probs.transpose(0, 3, 1, 2).reshape(micro_batch, length, group * length)
     weight_t = transposed(out_weight[0])
-    half = whole.shape[0] // 2
-    whole, incoming, index, spot, mine = lax.optimization_barrier(
-        (whole, incoming, index, spot, mine)
-    )
-    halves = lax.optimization_barrier((whole[:half], whole[half:]))
-    value_grad, saved = plain_turn(
-        sections - 1, spot, incoming, weight_t, probs_t, jnp.zeros_like(incoming)
-    )
-    beside = (incoming, value_grad, saved, mixed_t, probs_t, weight_t, value_t)
-    back, beside = gather_back(index, whole, halves, beside)
-    incoming, value_grad, saved, mixed_t, probs_t, weight_t, value_t = beside
-    back, value_grad = lax.optimization_barrier((back, value_grad))
-    parts = (incoming[:AHEAD], incoming[AHEAD:])
+    empty = jnp.zeros((lax.axis_size("tensor"), rows, feat_local), BF16)
+    beside = (mixed_t, probs_t, weight_t, value_t, empty)
+    both, beside = gather_both(index, back, grad_top.reshape(rows, feat_local), beside)
+    mixed_t, probs_t, weight_t, value_t, empty = beside
+    value_grad, saved = plain_turn(sections - 1, spot, both, rows, weight_t, probs_t, empty)
+    parts = (both[:AHEAD, -rows:], both[AHEAD:, -rows:])
     for section in range(sections - 1, 0, -1):
         moved = hand_down(value_grad, section)
         parts, moved = lax.optimization_barrier((parts, moved))
@@ -485,14 +489,14 @@
         below = section - 1
         if section % 2:
             parts, value_grad, saved = turn(
-                below, spot, blocks, parts, back, weight_t, probs_t, saved
+                below, spot, blocks, parts, both, weight_t, probs_t, saved
             )
         else:
             (ahead,), total, saved = turn(
-                below, spot, blocks, parts[:1], back, weight_t, probs_t, saved, ends=False
+                below, spot, blocks, parts[:1], both, weight_t, probs_t, saved, ends=False
             )
             (rest,), value_grad, saved = turn(
-                below, spot, blocks, parts[1:], back, weight_t, probs_t, saved, AHEAD, total
+                below, spot, blocks, parts[1:], both, weight_t, probs_t, saved, AHEAD, total
             )
             parts = (ahead, rest)
     above = shift(pick(mine, saved), "section", 1)

time: 565 us -> 558 us (0.988)
  waiting for transfers between devices: 101 us -> 75.8 us
  starting transfers between devices: 130 us -> 151 us
    ppermute x45, starting transfers between devices: 102 us -> 130 us  [hand_down(): return lax.ppermute(value, 'section', pairs)]
    all_to_all x2 -> x1, waiting for transfers between devices: 24.6 us -> 0.56 us  [blocks_of_all(): return lax.all_to_all(copies, 'tensor', 0, 0)]
    all_to_all x2 -> x1, starting transfers between devices: 11.2 us -> 3.41 us  [blocks_of_all(): return lax.all_to_all(copies, 'tensor', 0, 0)]
  transfers between devices with their start and end apart: 62 -> 61, of which waited for: 21 -> 18; matrix products, arithmetic and copies ran while one was open for 1% -> 1% of each run, Pallas kernels for 8% -> 7%
where the time goes in v6:
time: 558 us; the launch traced here: 549 us
  blocking collectives  189 us (34%)
  starting transfers between devices  151 us (27%)
  Pallas kernels  118 us (21%)
  waiting for transfers between devices  75.8 us (14%)
  local copies, waits for them, and re-layouts  12.2 us (2%)
    all_to_all x15, blocking collectives, blocks_of_all(): return lax.all_to_all(copies, 'tensor', 0, 0)  189 us
    ppermute x45, starting transfers between devices, hand_down(): return lax.ppermute(value, 'section', pairs)  130 us
    pallas_call x22, Pallas kernels, turn(): pl.pallas_call(functools.partial(turn_kernel, first, steps, section, tota...  96.4 us
    ppermute x13, waiting for transfers between devices, across(): return lax.ppermute(value, 'tensor', pairs)  64.3 us
    ppermute x13, starting transfers between devices, across(): return lax.ppermute(value, 'tensor', pairs)  15.7 us
  transfers between devices with their start and end apart: 61, of which 18 were waited for; matrix products, arithmetic and copies ran while one was open for 1% of the time, Pallas kernels for 7%

profile of v6, /device:TPU:0, one launch (start us, length us, event | category | flops | bytes accessed | tf_op | source)
XLA Modules:
  0.0 549.0 jit_solution(15367658766907178098)
XLA Ops:
  32.0 9.1 %collective-permute-done.5.refs_4_ = bf16[576,768]{1,0:T(8,128)(2,1)S(1)} collective-permute-done((bf16[576,768]{1,0:T(8,128)(2,1)}, bf16[576,768]{1,0:T(8,128)(2,1)S(1)}, u32[]{:S(2)}, u32[]{:S(2)}) %collective-permute-start.5) | collective-permute-done | bytes 884768 | tf_op jit(solution)/shard_map/ppermute | solution.py:140
  50.9 14.9 %collective-permute-done.7.refs_1_ = bf16[576,768]{1,0:T(8,128)(2,1)S(1)} collective-permute-done((bf16[576,768]{1,0:T(8,128)(2,1)S(1)}, bf16[576,768]{1,0:T(8,128)(2,1)S(1)}, u32[]{:S(2)}, u32[]{:S(2)}) %collective-permute-start.7) | collective-permute-done | bytes 884768 | tf_op jit(solution)/shard_map/ppermute | solution.py:140
  69.8 10.4 %collective-permute-done.10.refs_4_ = bf16[576,768]{1,0:T(8,128)(2,1)S(1)} collective-permute-done((bf16[576,768]{1,0:T(8,128)(2,1)S(1)}, bf16[576,768]{1,0:T(8,128)(2,1)S(1)}, u32[]{:S(2)}, u32[]{:S(2)}) %collective-permute-start.10) | collective-permute-done | bytes 884768 | tf_op jit(solution)/shard_map/ppermute | solution.py:140
  84.0 17.9 %collective-permute-done.12.refs_6_ = bf16[576,768]{1,0:T(8,128)(2,1)S(1)} collective-permute-done((bf16[576,768]{1,0:T(8,128)(2,1)S(1)}, bf16[576,768]{1,0:T(8,128)(2,1)S(1)}, u32[]{:S(2)}, u32[]{:S(2)}) %collective-permute-start.12) | collective-permute-done | bytes 884768 | tf_op jit(solution)/shard_map/ppermute | solution.py:140
  109.6 14.1 %collective-permute-start.14 = (bf16[128,128]{1,0:T(8,128)(2,1)S(1)}, bf16[128,128]{1,0:T(8,128)(2,1)S(1)}, u32[]{:S(2)}, u32[]{:S(2)}) collective-permute-start(bf16[128,128]{1,0:T(8,128)(2,1)S(1)} %get-tuple-element.155), channel_id=1, source_target_pairs={{0,8},{8,0},{16,24},{24,16},{32,40},{40,32},{48,56},{56,48},{64,72... | collective-permute-start | bytes 98312 | tf_op jit(solution)/shard_map/ppermute | solution.py:48
  125.1 13.4 %all_to_all.80.blocks_ref = bf16[8,128,128]{2,1,0:T(8,128)(2,1)S(1)} all-to-all(bf16[8,128,128]{2,1,0:T(8,128)(2,1)S(1)} %copies.16), channel_id=1, replica_groups=mesh['section'=16,'tensor'=8] {'tensor'}, dimensions={0} | all-to-all | bytes 524288 | tf_op jit(solution)/shard_map/all_to_all | solution.py:69
  147.0 11.5 %all_to_all.81.blocks_ref = bf16[8,128,128]{2,1,0:T(8,128)(2,1)S(1)} all-to-all(bf16[8,128,128]{2,1,0:T(8,128)(2,1)S(1)} %copies.17), channel_id=1, replica_groups=mesh['section'=16,'tensor'=8] {'tensor'}, dimensions={0} | all-to-all | bytes 524288 | tf_op jit(solution)/shard_map/all_to_all | solution.py:69
  164.7 29.6 %collective-permute-start.20 = (bf16[128,128]{1,0:T(8,128)(2,1)S(1)}, bf16[128,128]{1,0:T(8,128)(2,1)S(1)}, u32[]{:S(2)}, u32[]{:S(2)}) collective-permute-start(bf16[128,128]{1,0:T(8,128)(2,1)S(1)} %get-tuple-element.171), channel_id=1, source_target_pairs={{0,8},{8,0},{16,24},{24,16},{32,40},{40,32},{48,56},{56,48},{64,72... | collective-permute-start | bytes 98312 | tf_op jit(solution)/shard_map/ppermute | solution.py:48
  195.8 12.0 %all_to_all.82.blocks_ref = bf16[8,128,128]{2,1,0:T(8,128)(2,1)S(1)} all-to-all(bf16[8,128,128]{2,1,0:T(8,128)(2,1)S(1)} %copies.18), channel_id=1, replica_groups=mesh['section'=16,'tensor'=8] {'tensor'}, dimensions={0} | all-to-all | bytes 524288 | tf_op jit(solution)/shard_map/all_to_all | solution.py:69
  207.8 6.2 %turn.25 = (bf16[5,128,768]{2,1,0:T(8,128)(2,1)S(1)}, bf16[3,128,768]{2,1,0:T(8,128)(2,1)S(1)}, bf16[128,128]{1,0:T(8,128)(2,1)S(1)}, bf16[8,128,768]{2,1,0:T(8,128)(2,1)S(1)}) custom-call(s32[1]{0:T(128)} %bitcast.9.place_ref, bf16[8,128,128]{2,1,0:T(8,128)(2,1)S(1)} %all_to_all.82.blocks_ref, ...), custom_call_target="tpu_custom_call", output_to_operand_aliasing={{3}: (7, {})} | custom-call | flops 2818572288 | bytes 22020096 | tf_op jit(solution)/shard_map/turn/pallas_call | solution.py:320
  216.2 11.3 %all_to_all.83.blocks_ref = bf16[8,128,128]{2,1,0:T(8,128)(2,1)S(1)} all-to-all(bf16[8,128,128]{2,1,0:T(8,128)(2,1)S(1)} %copies.19), channel_id=1, replica_groups=mesh['section'=16,'tensor'=8] {'tensor'}, dimensions={0} | all-to-all | bytes 524288 | tf_op jit(solution)/shard_map/all_to_all | solution.py:69
  233.7 9.9 %collective-permute-start.26 = (bf16[128,128]{1,0:T(8,128)(2,1)S(1)}, bf16[128,128]{1,0:T(8,128)(2,1)S(1)}, u32[]{:S(2)}, u32[]{:S(2)}) collective-permute-start(bf16[128,128]{1,0:T(8,128)(2,1)S(1)} %get-tuple-element.187), channel_id=1, source_target_pairs={{0,8},{8,0},{16,24},{24,16},{32,40},{40,32},{48,56},{56,48},{64,72... | collective-permute-start | bytes 98312 | tf_op jit(solution)/shard_map/ppermute | solution.py:48
  245.1 12.0 %all_to_all.84.blocks_ref = bf16[8,128,128]{2,1,0:T(8,128)(2,1)S(1)} all-to-all(bf16[8,128,128]{2,1,0:T(8,128)(2,1)S(1)} %copies.20), channel_id=1, replica_groups=mesh['section'=16,'tensor'=8] {'tensor'}, dimensions={0} | all-to-all | bytes 524288 | tf_op jit(solution)/shard_map/all_to_all | solution.py:69
  257.1 6.2 %turn.28 = (bf16[5,128,768]{2,1,0:T(8,128)(2,1)S(1)}, bf16[3,128,768]{2,1,0:T(8,128)(2,1)S(1)}, bf16[128,128]{1,0:T(8,128)(2,1)S(1)}, bf16[8,128,768]{2,1,0:T(8,128)(2,1)S(1)}) custom-call(s32[1]{0:T(128)} %bitcast.9.place_ref, bf16[8,128,128]{2,1,0:T(8,128)(2,1)S(1)} %all_to_all.84.blocks_ref, ...), custom_call_target="tpu_custom_call", output_to_operand_aliasing={{3}: (7, {})} | custom-call | flops 2818572288 | bytes 22020096 | tf_op jit(solution)/shard_map/turn/pallas_call | solution.py:320
  265.5 11.3 %all_to_all.85.blocks_ref = bf16[8,128,128]{2,1,0:T(8,128)(2,1)S(1)} all-to-all(bf16[8,128,128]{2,1,0:T(8,128)(2,1)S(1)} %copies.21), channel_id=1, replica_groups=mesh['section'=16,'tensor'=8] {'tensor'}, dimensions={0} | all-to-all | bytes 524288 | tf_op jit(solution)/shard_map/all_to_all | solution.py:69
  283.0 9.9 %collective-permute-start.32 = (bf16[128,128]{1,0:T(8,128)(2,1)S(1)}, bf16[128,128]{1,0:T(8,128)(2,1)S(1)}, u32[]{:S(2)}, u32[]{:S(2)}) collective-permute-start(bf16[128,128]{1,0:T(8,128)(2,1)S(1)} %get-tuple-element.203), channel_id=1, source_target_pairs={{0,8},{8,0},{16,24},{24,16},{32,40},{40,32},{48,56},{56,48},{64,72... | collective-permute-start | bytes 98312 | tf_op jit(solution)/shard_map/ppermute | solution.py:48
  294.4 12.0 %all_to_all.86.blocks_ref = bf16[8,128,128]{2,1,0:T(8,128)(2,1)S(1)} all-to-all(bf16[8,128,128]{2,1,0:T(8,128)(2,1)S(1)} %copies.22), channel_id=1, replica_groups=mesh['section'=16,'tensor'=8] {'tensor'}, dimensions={0} | all-to-all | bytes 524288 | tf_op jit(solution)/shard_map/all_to_all | solution.py:69
  306.3 6.2 %turn.31 = (bf16[5,128,768]{2,1,0:T(8,128)(2,1)S(1)}, bf16[3,128,768]{2,1,0:T(8,128)(2,1)S(1)}, bf16[128,128]{1,0:T(8,128)(2,1)S(1)}, bf16[8,128,768]{2,1,0:T(8,128)(2,1)S(1)}) custom-call(s32[1]{0:T(128)} %bitcast.9.place_ref, bf16[8,128,128]{2,1,0:T(8,128)(2,1)S(1)} %all_to_all.86.blocks_ref, ...), custom_call_target="tpu_custom_call", output_to_operand_aliasing={{3}: (7, {})} | custom-call | flops 2818572288 | bytes 22020096 | tf_op jit(solution)/shard_map/turn/pallas_call | solution.py:320
  314.7 11.6 %all_to_all.87.blocks_ref = bf16[8,128,128]{2,1,0:T(8,128)(2,1)S(1)} all-to-all(bf16[8,128,128]{2,1,0:T(8,128)(2,1)S(1)} %copies.23), channel_id=1, replica_groups=mesh['section'=16,'tensor'=8] {'tensor'}, dimensions={0} | all-to-all | bytes 524288 | tf_op jit(solution)/shard_map/all_to_all | solution.py:69
  334.4 21.1 %all_to_all.88.blocks_ref = bf16[8,128,128]{2,1,0:T(8,128)(2,1)S(1)} all-to-all(bf16[8,128,128]{2,1,0:T(8,128)(2,1)S(1)} %copies.24), channel_id=1, replica_groups=mesh['section'=16,'tensor'=8] {'tensor'}, dimensions={0} | all-to-all | bytes 524288 | tf_op jit(solution)/shard_map/all_to_all | solution.py:69
  363.9 12.8 %all_to_all.89.blocks_ref = bf16[8,128,128]{2,1,0:T(8,128)(2,1)S(1)} all-to-all(bf16[8,128,128]{2,1,0:T(8,128)(2,1)S(1)} %copies.25), channel_id=1, replica_groups=mesh['section'=16,'tensor'=8] {'tensor'}, dimensions={0} | all-to-all | bytes 524288 | tf_op jit(solution)/shard_map/all_to_all | solution.py:69
  383.0 8.3 %collective-permute-start.44 = (bf16[128,128]{1,0:T(8,128)(2,1)S(1)}, bf16[128,128]{1,0:T(8,128)(2,1)S(1)}, u32[]{:S(2)}, u32[]{:S(2)}) collective-permute-start(bf16[128,128]{1,0:T(8,128)(2,1)S(1)} %get-tuple-element.235), channel_id=1, source_target_pairs={{0,8},{8,0},{16,24},{24,16},{32,40},{40,32},{48,56},{56,48},{64,72... | collective-permute-start | bytes 98312 | tf_op jit(solution)/shard_map/ppermute | solution.py:48
  392.7 13.3 %all_to_all.90.blocks_ref = bf16[8,128,128]{2,1,0:T(8,128)(2,1)S(1)} all-to-all(bf16[8,128,128]{2,1,0:T(8,128)(2,1)S(1)} %copies.26), channel_id=1, replica_groups=mesh['section'=16,'tensor'=8] {'tensor'}, dimensions={0} | all-to-all | bytes 524288 | tf_op jit(solution)/shard_map/all_to_all | solution.py:69
  406.0 6.2 %turn.37 = (bf16[5,128,768]{2,1,0:T(8,128)(2,1)S(1)}, bf16[3,128,768]{2,1,0:T(8,128)(2,1)S(1)}, bf16[128,128]{1,0:T(8,128)(2,1)S(1)}, bf16[8,128,768]{2,1,0:T(8,128)(2,1)S(1)}) custom-call(s32[1]{0:T(128)} %bitcast.9.place_ref, bf16[8,128,128]{2,1,0:T(8,128)(2,1)S(1)} %all_to_all.90.blocks_ref, ...), custom_call_target="tpu_custom_call", output_to_operand_aliasing={{3}: (7, {})} | custom-call | flops 2818572288 | bytes 22020096 | tf_op jit(solution)/shard_map/turn/pallas_call | solution.py:320
  414.4 11.3 %all_to_all.91.blocks_ref = bf16[8,128,128]{2,1,0:T(8,128)(2,1)S(1)} all-to-all(bf16[8,128,128]{2,1,0:T(8,128)(2,1)S(1)} %copies.27), channel_id=1, replica_groups=mesh['section'=16,'tensor'=8] {'tensor'}, dimensions={0} | all-to-all | bytes 524288 | tf_op jit(solution)/shard_map/all_to_all | solution.py:69
  432.0 9.5 %collective-permute-start.50 = (bf16[128,128]{1,0:T(8,128)(2,1)S(1)}, bf16[128,128]{1,0:T(8,128)(2,1)S(1)}, u32[]{:S(2)}, u32[]{:S(2)}) collective-permute-start(bf16[128,128]{1,0:T(8,128)(2,1)S(1)} %get-tuple-element.251), channel_id=1, source_target_pairs={{0,8},{8,0},{16,24},{24,16},{32,40},{40,32},{48,56},{56,48},{64,72... | collective-permute-start | bytes 98312 | tf_op jit(solution)/shard_map/ppermute | solution.py:48
  442.8 12.0 %all_to_all.92.blocks_ref = bf16[8,128,128]{2,1,0:T(8,128)(2,1)S(1)} all-to-all(bf16[8,128,128]{2,1,0:T(8,128)(2,1)S(1)} %copies.28), channel_id=1, replica_groups=mesh['section'=16,'tensor'=8] {'tensor'}, dimensions={0} | all-to-all | bytes 524288 | tf_op jit(solution)/shard_map/all_to_all | solution.py:69
  463.2 11.6 %all_to_all.93.blocks_ref = bf16[8,128,128]{2,1,0:T(8,128)(2,1)S(1)} all-to-all(bf16[8,128,128]{2,1,0:T(8,128)(2,1)S(1)} %copies.29), channel_id=1, replica_groups=mesh['section'=16,'tensor'=8] {'tensor'}, dimensions={0} | all-to-all | bytes 524288 | tf_op jit(solution)/shard_map/all_to_all | solution.py:69
  481.1 30.0 %collective-permute-start.56 = (bf16[128,128]{1,0:T(8,128)(2,1)S(1)}, bf16[128,128]{1,0:T(8,128)(2,1)S(1)}, u32[]{:S(2)}, u32[]{:S(2)}) collective-permute-start(bf16[128,128]{1,0:T(8,128)(2,1)S(1)} %get-tuple-element.267), channel_id=1, source_target_pairs={{0,8},{8,0},{16,24},{24,16},{32,40},{40,32},{48,56},{56,48},{64,72... | collective-permute-start | bytes 98312 | tf_op jit(solution)/shard_map/ppermute | solution.py:48
  512.4 12.0 %all_to_all.94.blocks_ref = bf16[8,128,128]{2,1,0:T(8,128)(2,1)S(1)} all-to-all(bf16[8,128,128]{2,1,0:T(8,128)(2,1)S(1)} %copies.30), channel_id=1, replica_groups=mesh['section'=16,'tensor'=8] {'tensor'}, dimensions={0} | all-to-all | bytes 524288 | tf_op jit(solution)/shard_map/all_to_all | solution.py:69
  524.4 9.3 %turn.43 = (bf16[5,128,768]{2,1,0:T(8,128)(2,1)}, bf16[3,128,768]{2,1,0:T(8,128)(2,1)}, bf16[128,128]{1,0:T(8,128)(2,1)S(1)}, bf16[8,128,768]{2,1,0:T(8,128)(2,1)S(1)}) custom-call(s32[1]{0:T(128)} %bitcast.9.place_ref, bf16[8,128,128]{2,1,0:T(8,128)(2,1)S(1)} %all_to_all.94.blocks_ref, ...), custom_call_target="tpu_custom_call", output_to_operand_aliasing={{3}: (7, {})} | custom-call | flops 2818572288 | bytes 22020096 | tf_op jit(solution)/shard_map/turn/pallas_call | solution.py:320
  539.0 6.3 %weight_grads.1 = bf16[768,6144]{1,0:T(8,128)(2,1)} custom-call(bf16[768,128]{1,0:T(8,128)(2,1)S(1)} %copy-done.7, bf16[8,128,768]{2,1,0:T(8,128)(2,1)S(1)} %get-tuple-element.273.rows_ref), custom_call_target="tpu_custom_call" | custom-call | flops 1207959552 | bytes 9437184 | tf_op jit(solution)/shard_map/weight_grads/pallas_call | solution.py:430
  (200 shorter events, 153.5 us)
Async XLA Ops:
  8.3 36.9 %collective-permute-start.1 = (bf16[1152,768]{1,0:T(8,128)(2,1)S(1)}, bf16[1152,768]{1,0:T(8,128)(2,1)}, u32[]{:S(2)}, u32[]{:S(2)}) collective-permute-start(bf16[1152,768]{1,0:T(8,128)(2,1)S(1)} %pad_maximum_fusion.refs_0_), channel_id=1, source_target_pairs={{0,4},{1,5},{2,6},{3,7},{4,0},{5,1},{6,2},{7,3},{8,12},{9,13},{10,... | collective-permute-start | bytes 5308424 | tf_op jit(solution)/shard_map/ppermute | solution.py:140
  14.7 15.1 %collective-permute-start.3 = (bf16[576,768]{1,0:T(8,128)(2,1)}, bf16[576,768]{1,0:T(8,128)(2,1)}, u32[]{:S(2)}, u32[]{:S(2)}) collective-permute-start(bf16[576,768]{1,0:T(8,128)(2,1)} %get-tuple-element.143), channel_id=1, source_target_pairs={{0,3},{1,0},{2,1},{3,2},{4,7},{5,4},{6,5},{7,6},{8,11},{9,8},{10,9... | collective-permute-start | bytes 2654216 | tf_op jit(solution)/shard_map/ppermute | solution.py:140
  17.5 14.6 %collective-permute-start.2 = (bf16[576,768]{1,0:T(8,128)(2,1)}, bf16[576,768]{1,0:T(8,128)(2,1)}, u32[]{:S(2)}, u32[]{:S(2)}) collective-permute-start(bf16[576,768]{1,0:T(8,128)(2,1)} %get-tuple-element.143), channel_id=1, source_target_pairs={{0,1},{1,2},{2,3},{3,0},{4,5},{5,6},{6,7},{7,4},{8,9},{9,10},{10,1... | collective-permute-start | bytes 2654216 | tf_op jit(solution)/shard_map/ppermute | solution.py:140
  17.5 23.7 %collective-permute-start.5 = (bf16[576,768]{1,0:T(8,128)(2,1)}, bf16[576,768]{1,0:T(8,128)(2,1)S(1)}, u32[]{:S(2)}, u32[]{:S(2)}) collective-permute-start(bf16[576,768]{1,0:T(8,128)(2,1)} %get-tuple-element.144), channel_id=1, source_target_pairs={{0,3},{1,0},{2,1},{3,2},{4,7},{5,4},{6,5},{7,6},{8,11},{9,8},{10,9... | collective-permute-start | bytes 2654216 | tf_op jit(solution)/shard_map/ppermute | solution.py:140
  20.7 24.4 %collective-permute-start.4 = (bf16[576,768]{1,0:T(8,128)(2,1)}, bf16[576,768]{1,0:T(8,128)(2,1)}, u32[]{:S(2)}, u32[]{:S(2)}) collective-permute-start(bf16[576,768]{1,0:T(8,128)(2,1)} %get-tuple-element.144), channel_id=1, source_target_pairs={{0,1},{1,2},{2,3},{3,0},{4,5},{5,6},{6,7},{7,4},{8,9},{9,10},{10,1... | collective-permute-start | bytes 2654216 | tf_op jit(solution)/shard_map/ppermute | solution.py:140
  45.1 20.7 %collective-permute-start.7 = (bf16[576,768]{1,0:T(8,128)(2,1)S(1)}, bf16[576,768]{1,0:T(8,128)(2,1)S(1)}, u32[]{:S(2)}, u32[]{:S(2)}) collective-permute-start(bf16[576,768]{1,0:T(8,128)(2,1)S(1)} %collective-permute-done.5.refs_4_), channel_id=1, source_target_pairs={{0,3},{1,0},{2,1},{3,2},{4,7},{5,4},{6,5},{7,6},{8,11},{9,8},{10,9... | collective-permute-start | bytes 2654216 | tf_op jit(solution)/shard_map/ppermute | solution.py:140
  46.4 23.5 %collective-permute-start.8 = (bf16[576,768]{1,0:T(8,128)(2,1)S(1)}, bf16[576,768]{1,0:T(8,128)(2,1)S(1)}, u32[]{:S(2)}, u32[]{:S(2)}) collective-permute-start(bf16[576,768]{1,0:T(8,128)(2,1)S(1)} %slice.42), channel_id=1, source_target_pairs={{0,1},{1,2},{2,3},{3,0},{4,5},{5,6},{6,7},{7,4},{8,9},{9,10},{10,1... | collective-permute-start | bytes 2654216 | tf_op jit(solution)/shard_map/ppermute | solution.py:140
  48.5 31.7 %collective-permute-start.10 = (bf16[576,768]{1,0:T(8,128)(2,1)S(1)}, bf16[576,768]{1,0:T(8,128)(2,1)S(1)}, u32[]{:S(2)}, u32[]{:S(2)}) collective-permute-start(bf16[576,768]{1,0:T(8,128)(2,1)S(1)} %slice.42), channel_id=1, source_target_pairs={{0,3},{1,0},{2,1},{3,2},{4,7},{5,4},{6,5},{7,6},{8,11},{9,8},{10,9... | collective-permute-start | bytes 2654216 | tf_op jit(solution)/shard_map/ppermute | solution.py:140
  49.7 34.3 %collective-permute-start.11 = (bf16[576,768]{1,0:T(8,128)(2,1)S(1)}, bf16[576,768]{1,0:T(8,128)(2,1)S(1)}, u32[]{:S(2)}, u32[]{:S(2)}) collective-permute-start(bf16[576,768]{1,0:T(8,128)(2,1)S(1)} %collective-permute-done.5.refs_4_), channel_id=1, source_target_pairs={{0,4},{1,5},{2,6},{3,7},{4,0},{5,1},{6,2},{7,3},{8,12},{9,13},{10,... | collective-permute-start | bytes 2654216 | tf_op jit(solution)/shard_map/ppermute | solution.py:140
  50.1 33.8 %collective-permute-start.6 = (bf16[576,768]{1,0:T(8,128)(2,1)}, bf16[576,768]{1,0:T(8,128)(2,1)S(1)}, u32[]{:S(2)}, u32[]{:S(2)}) collective-permute-start(bf16[576,768]{1,0:T(8,128)(2,1)} %collective-permute-done.2.refs_1_), channel_id=1, source_target_pairs={{0,1},{1,2},{2,3},{3,0},{4,5},{5,6},{6,7},{7,4},{8,9},{9,10},{10,1... | collective-permute-start | bytes 2654216 | tf_op jit(solution)/shard_map/ppermute | solution.py:140
  65.9 18.1 %collective-permute-start.9 = (bf16[576,768]{1,0:T(8,128)(2,1)}, bf16[576,768]{1,0:T(8,128)(2,1)S(1)}, u32[]{:S(2)}, u32[]{:S(2)}) collective-permute-start(bf16[576,768]{1,0:T(8,128)(2,1)} %collective-permute-done.4.refs_2_), channel_id=1, source_target_pairs={{0,4},{1,5},{2,6},{3,7},{4,0},{5,1},{6,2},{7,3},{8,12},{9,13},{10,... | collective-permute-start | bytes 2654216 | tf_op jit(solution)/shard_map/ppermute | solution.py:140
  69.8 32.0 %collective-permute-start.12 = (bf16[576,768]{1,0:T(8,128)(2,1)S(1)}, bf16[576,768]{1,0:T(8,128)(2,1)S(1)}, u32[]{:S(2)}, u32[]{:S(2)}) collective-permute-start(bf16[576,768]{1,0:T(8,128)(2,1)S(1)} %collective-permute-done.8.refs_2_), channel_id=1, source_target_pairs={{0,1},{1,2},{2,3},{3,0},{4,5},{5,6},{6,7},{7,4},{8,9},{9,10},{10,1... | collective-permute-start | bytes 2654216 | tf_op jit(solution)/shard_map/ppermute | solution.py:140
  80.2 24.1 %collective-permute-start.13 = (bf16[576,768]{1,0:T(8,128)(2,1)S(1)}, bf16[576,768]{1,0:T(8,128)(2,1)S(1)}, u32[]{:S(2)}, u32[]{:S(2)}) collective-permute-start(bf16[576,768]{1,0:T(8,128)(2,1)S(1)} %collective-permute-done.7.refs_1_), channel_id=1, source_target_pairs={{0,4},{1,5},{2,6},{3,7},{4,0},{5,1},{6,2},{7,3},{8,12},{9,13},{10,... | collective-permute-start | bytes 2654216 | tf_op jit(solution)/shard_map/ppermute | solution.py:140
  109.6 15.0 %collective-permute-start.14 = (bf16[128,128]{1,0:T(8,128)(2,1)S(1)}, bf16[128,128]{1,0:T(8,128)(2,1)S(1)}, u32[]{:S(2)}, u32[]{:S(2)}) collective-permute-start(bf16[128,128]{1,0:T(8,128)(2,1)S(1)} %get-tuple-element.155), channel_id=1, source_target_pairs={{0,8},{8,0},{16,24},{24,16},{32,40},{40,32},{48,56},{56,48},{64,72... | collective-permute-start | bytes 98312 | tf_op jit(solution)/shard_map/ppermute | solution.py:48
  124.6 14.0 %collective-permute-start.15 = (bf16[5,128,768]{2,1,0:T(8,128)(2,1)S(1)}, bf16[5,128,768]{2,1,0:T(8,128)(2,1)S(1)}, u32[]{:S(2)}, u32[]{:S(2)}) collective-permute-start(bf16[5,128,768]{2,1,0:T(8,128)(2,1)S(1)} %slice.47), channel_id=1, source_target_pairs={{0,8},{8,0},{16,24},{24,16},{32,40},{40,32},{48,56},{56,48},{64,72... | collective-permute-start | bytes 2949128 | tf_op jit(solution)/shard_map/ppermute | solution.py:48
  124.9 13.6 %collective-permute-start.16 = (bf16[3,128,768]{2,1,0:T(8,128)(2,1)S(1)}, bf16[3,128,768]{2,1,0:T(8,128)(2,1)S(1)}, u32[]{:S(2)}, u32[]{:S(2)}) collective-permute-start(bf16[3,128,768]{2,1,0:T(8,128)(2,1)S(1)} %slice.48), channel_id=1, source_target_pairs={{0,8},{8,0},{16,24},{24,16},{32,40},{40,32},{48,56},{56,48},{64,72... | collective-permute-start | bytes 1769480 | tf_op jit(solution)/shard_map/ppermute | solution.py:48
  146.2 16.0 %collective-permute-start.19 = (bf16[3,128,768]{2,1,0:T(8,128)(2,1)S(1)}, bf16[3,128,768]{2,1,0:T(8,128)(2,1)S(1)}, u32[]{:S(2)}, u32[]{:S(2)}) collective-permute-start(bf16[3,128,768]{2,1,0:T(8,128)(2,1)S(1)} %get-tuple-element.167), channel_id=1, source_target_pairs={{0,0},{8,16},{16,8},{24,32},{32,24},{40,48},{48,40},{56,56},{64,64... | collective-permute-start | bytes 1769480 | tf_op jit(solution)/shard_map/ppermute | solution.py:48
  164.7 30.5 %collective-permute-start.20 = (bf16[128,128]{1,0:T(8,128)(2,1)S(1)}, bf16[128,128]{1,0:T(8,128)(2,1)S(1)}, u32[]{:S(2)}, u32[]{:S(2)}) collective-permute-start(bf16[128,128]{1,0:T(8,128)(2,1)S(1)} %get-tuple-element.171), channel_id=1, source_target_pairs={{0,8},{8,0},{16,24},{24,16},{32,40},{40,32},{48,56},{56,48},{64,72... | collective-permute-start | bytes 98312 | tf_op jit(solution)/shard_map/ppermute | solution.py:48
  215.4 15.8 %collective-permute-start.25 = (bf16[3,128,768]{2,1,0:T(8,128)(2,1)S(1)}, bf16[3,128,768]{2,1,0:T(8,128)(2,1)S(1)}, u32[]{:S(2)}, u32[]{:S(2)}) collective-permute-start(bf16[3,128,768]{2,1,0:T(8,128)(2,1)S(1)} %get-tuple-element.183), channel_id=1, source_target_pairs={{0,0},{8,16},{16,8},{24,32},{32,24},{40,48},{48,40},{56,56},{64,64... | collective-permute-start | bytes 1769480 | tf_op jit(solution)/shard_map/ppermute | solution.py:48
  264.7 15.8 %collective-permute-start.31 = (bf16[3,128,768]{2,1,0:T(8,128)(2,1)S(1)}, bf16[3,128,768]{2,1,0:T(8,128)(2,1)S(1)}, u32[]{:S(2)}, u32[]{:S(2)}) collective-permute-start(bf16[3,128,768]{2,1,0:T(8,128)(2,1)S(1)} %get-tuple-element.199), channel_id=1, source_target_pairs={{0,0},{8,16},{16,8},{24,32},{32,24},{40,48},{48,40},{56,56},{64,64... | collective-permute-start | bytes 1769480 | tf_op jit(solution)/shard_map/ppermute | solution.py:48
  313.3 13.1 %collective-permute-start.36 = (bf16[5,128,768]{2,1,0:T(8,128)(2,1)S(1)}, bf16[5,128,768]{2,1,0:T(8,128)(2,1)S(1)}, u32[]{:S(2)}, u32[]{:S(2)}) collective-permute-start(bf16[5,128,768]{2,1,0:T(8,128)(2,1)S(1)} %get-tuple-element.212), channel_id=1, source_target_pairs={{0,0},{8,8},{16,16},{24,24},{32,32},{40,40},{48,48},{56,64},{64,56... | collective-permute-start | bytes 2949128 | tf_op jit(solution)/shard_map/ppermute | solution.py:48
  314.0 16.1 %collective-permute-start.37 = (bf16[3,128,768]{2,1,0:T(8,128)(2,1)S(1)}, bf16[3,128,768]{2,1,0:T(8,128)(2,1)S(1)}, u32[]{:S(2)}, u32[]{:S(2)}) collective-permute-start(bf16[3,128,768]{2,1,0:T(8,128)(2,1)S(1)} %get-tuple-element.215), channel_id=1, source_target_pairs={{0,0},{8,8},{16,16},{24,24},{32,32},{40,40},{48,48},{56,64},{64,56... | collective-permute-start | bytes 1769480 | tf_op jit(solution)/shard_map/ppermute | solution.py:48
  333.9 21.7 %collective-permute-start.39 = (bf16[5,128,768]{2,1,0:T(8,128)(2,1)S(1)}, bf16[5,128,768]{2,1,0:T(8,128)(2,1)S(1)}, u32[]{:S(2)}, u32[]{:S(2)}) collective-permute-start(bf16[5,128,768]{2,1,0:T(8,128)(2,1)S(1)} %get-tuple-element.221), channel_id=1, source_target_pairs={{0,8},{8,0},{16,24},{24,16},{32,40},{40,32},{48,56},{56,48},{64,72... | collective-permute-start | bytes 2949128 | tf_op jit(solution)/shard_map/ppermute | solution.py:48
  334.0 21.5 %collective-permute-start.40 = (bf16[3,128,768]{2,1,0:T(8,128)(2,1)S(1)}, bf16[3,128,768]{2,1,0:T(8,128)(2,1)S(1)}, u32[]{:S(2)}, u32[]{:S(2)}) collective-permute-start(bf16[3,128,768]{2,1,0:T(8,128)(2,1)S(1)} %get-tuple-element.222), channel_id=1, source_target_pairs={{0,8},{8,0},{16,24},{24,16},{32,40},{40,32},{48,56},{56,48},{64,72... | collective-permute-start | bytes 1769480 | tf_op jit(solution)/shard_map/ppermute | solution.py:48
  362.4 14.3 %collective-permute-start.42 = (bf16[5,128,768]{2,1,0:T(8,128)(2,1)S(1)}, bf16[5,128,768]{2,1,0:T(8,128)(2,1)S(1)}, u32[]{:S(2)}, u32[]{:S(2)}) collective-permute-start(bf16[5,128,768]{2,1,0:T(8,128)(2,1)S(1)} %get-tuple-element.228), channel_id=1, source_target_pairs={{0,0},{8,16},{16,8},{24,32},{32,24},{40,48},{48,40},{56,56},{64,64... | collective-permute-start | bytes 2949128 | tf_op jit(solution)/shard_map/ppermute | solution.py:48
  363.2 17.3 %collective-permute-start.43 = (bf16[3,128,768]{2,1,0:T(8,128)(2,1)S(1)}, bf16[3,128,768]{2,1,0:T(8,128)(2,1)S(1)}, u32[]{:S(2)}, u32[]{:S(2)}) collective-permute-start(bf16[3,128,768]{2,1,0:T(8,128)(2,1)S(1)} %get-tuple-element.231), channel_id=1, source_target_pairs={{0,0},{8,16},{16,8},{24,32},{32,24},{40,48},{48,40},{56,56},{64,64... | collective-permute-start | bytes 1769480 | tf_op jit(solution)/shard_map/ppermute | solution.py:48
  392.1 13.8 %collective-permute-start.45 = (bf16[5,128,768]{2,1,0:T(8,128)(2,1)S(1)}, bf16[5,128,768]{2,1,0:T(8,128)(2,1)S(1)}, u32[]{:S(2)}, u32[]{:S(2)}) collective-permute-start(bf16[5,128,768]{2,1,0:T(8,128)(2,1)S(1)} %get-tuple-element.237), channel_id=1, source_target_pairs={{0,8},{8,0},{16,24},{24,16},{32,40},{40,32},{48,56},{56,48},{64,72... | collective-permute-start | bytes 2949128 | tf_op jit(solution)/shard_map/ppermute | solution.py:48
  392.5 13.5 %collective-permute-start.46 = (bf16[3,128,768]{2,1,0:T(8,128)(2,1)S(1)}, bf16[3,128,768]{2,1,0:T(8,128)(2,1)S(1)}, u32[]{:S(2)}, u32[]{:S(2)}) collective-permute-start(bf16[3,128,768]{2,1,0:T(8,128)(2,1)S(1)} %get-tuple-element.238), channel_id=1, source_target_pairs={{0,8},{8,0},{16,24},{24,16},{32,40},{40,32},{48,56},{56,48},{64,72... | collective-permute-start | bytes 1769480 | tf_op jit(solution)/shard_map/ppermute | solution.py:48
  413.6 15.8 %collective-permute-start.49 = (bf16[3,128,768]{2,1,0:T(8,128)(2,1)S(1)}, bf16[3,128,768]{2,1,0:T(8,128)(2,1)S(1)}, u32[]{:S(2)}, u32[]{:S(2)}) collective-permute-start(bf16[3,128,768]{2,1,0:T(8,128)(2,1)S(1)} %get-tuple-element.247), channel_id=1, source_target_pairs={{0,0},{8,16},{16,8},{24,32},{32,24},{40,48},{48,40},{56,56},{64,64... | collective-permute-start | bytes 1769480 | tf_op jit(solution)/shard_map/ppermute | solution.py:48
  461.7 13.1 %collective-permute-start.54 = (bf16[5,128,768]{2,1,0:T(8,128)(2,1)S(1)}, bf16[5,128,768]{2,1,0:T(8,128)(2,1)S(1)}, u32[]{:S(2)}, u32[]{:S(2)}) collective-permute-start(bf16[5,128,768]{2,1,0:T(8,128)(2,1)S(1)} %get-tuple-element.260), channel_id=1, source_target_pairs={{0,0},{8,16},{16,8},{24,32},{32,24},{40,48},{48,40},{56,56},{64,64... | collective-permute-start | bytes 2949128 | tf_op jit(solution)/shard_map/ppermute | solution.py:48
  462.5 16.1 %collective-permute-start.55 = (bf16[3,128,768]{2,1,0:T(8,128)(2,1)S(1)}, bf16[3,128,768]{2,1,0:T(8,128)(2,1)S(1)}, u32[]{:S(2)}, u32[]{:S(2)}) collective-permute-start(bf16[3,128,768]{2,1,0:T(8,128)(2,1)S(1)} %get-tuple-element.263), channel_id=1, source_target_pairs={{0,0},{8,16},{16,8},{24,32},{32,24},{40,48},{48,40},{56,56},{64,64... | collective-permute-start | bytes 1769480 | tf_op jit(solution)/shard_map/ppermute | solution.py:48
  481.1 30.8 %collective-permute-start.56 = (bf16[128,128]{1,0:T(8,128)(2,1)S(1)}, bf16[128,128]{1,0:T(8,128)(2,1)S(1)}, u32[]{:S(2)}, u32[]{:S(2)}) collective-permute-start(bf16[128,128]{1,0:T(8,128)(2,1)S(1)} %get-tuple-element.267), channel_id=1, source_target_pairs={{0,8},{8,0},{16,24},{24,16},{32,40},{40,32},{48,56},{56,48},{64,72... | collective-permute-start | bytes 98312 | tf_op jit(solution)/shard_map/ppermute | solution.py:48
  (43 other events, 328.2 us)

commit v7 on v6

--- a/solution.py
+++ b/solution.py
@@ -188,15 +188,24 @@
         ).astype(BF16)
 
 
-def keep(step, block, saved_ref, sem):
-    copy = pltpu.make_async_copy(block, saved_ref.at[step], sem)
-    copy.start()
-    copy.wait()
+def keep(active, step, steps, first, block, kept, saved_ref, sems):
+    def copy(j):
+        return pltpu.make_async_copy(kept.at[j], saved_ref.at[first + j], sems.at[j])
+
+    @pl.when(active)
+    def _():
+        kept[step] = block
+        copy(step).start()
+
+    @pl.when(active & (step == steps - 1))
+    def _():
+        for j in range(steps):
+            copy(j).wait()
 
 
 def plain_kernel(
     steps, section, place_ref, rows_ref, weight_ref, probs_t_ref, kept_ref,
-    value_ref, saved_ref, total, sem,
+    value_ref, saved_ref, total, kept, sems,
 ):
     step = pl.program_id(0)
 
@@ -206,13 +215,11 @@
 
     total[...] += lax.dot_general(rows_ref[0], weight_ref[...], NN, preferred_element_type=F32)
 
-    @pl.when(place_ref[0] == section)
-    def _():
-        keep(step, rows_ref.at[0], saved_ref, sem)
-
     @pl.when(step == steps - 1)
     def _():
         value_grad_of(total[...], probs_t_ref, value_ref)
+
+    keep(place_ref[0] == section, step, steps, 0, rows_ref[0], kept, saved_ref, sems)
 
 
 def turn_kernel(
@@ -224,7 +231,7 @@
     back_ref, weight_ref, probs_t_ref, kept_ref = (refs.pop(0) for _ in range(4))
     total_ref = refs.pop(0) if has_total else None
     new_refs = [refs.pop(0) for _ in range(count)]
-    result_ref, saved_ref, heads, total, sem = refs
+    result_ref, saved_ref, heads, total, kept, sems = refs
     step = pl.program_id(0)
     head_size = blocks_ref.shape[2]
 
@@ -242,10 +249,8 @@
         total[...] += lax.dot_general(
             new_rows, weight_ref[...], NN, preferred_element_type=F32
         )
-
-        @pl.when(place_ref[0] == section)
-        def _():
-            keep(first + step, new_ref.at[0], saved_ref, sem)
+        active = place_ref[0] == section
+        keep(active, step, sum(steps), first, new_rows, kept, saved_ref, sems)
 
     if count == 1:
         finish(rows_refs[0], new_refs[0])
@@ -287,7 +292,11 @@
             jax.ShapeDtypeStruct((count, head_size), BF16),
             jax.ShapeDtypeStruct(saved.shape, BF16),
         ],
-        scratch_shapes=[pltpu.VMEM((count, own), F32), pltpu.SemaphoreType.DMA],
+        scratch_shapes=[
+            pltpu.VMEM((count, own), F32),
+            pltpu.VMEM((steps, count, tile), BF16),
+            pltpu.SemaphoreType.DMA((steps,)),
+        ],
         input_output_aliases={4: 1},
         compiler_params=params(),
         cost_estimate=pl.CostEstimate(
@@ -343,7 +352,8 @@
         scratch_shapes=[
             pltpu.VMEM((count, depth), BF16),
             pltpu.VMEM((count, own), F32),
-            pltpu.SemaphoreType.DMA,
+            pltpu.VMEM((sum(steps), count, tile), BF16),
+            pltpu.SemaphoreType.DMA((sum(steps),)),
         ],
         input_output_aliases={alias: len(rows) + 1},
         compiler_params=params(),

time: 558 us -> 560 us (level)
  no operation moved by 1% of the time
where the time goes in v7:
time: 560 us; the launch traced here: 551 us
  blocking collectives  189 us (34%)
  starting transfers between devices  151 us (27%)
  Pallas kernels  120 us (21%)
  waiting for transfers between devices  75.8 us (14%)
  local copies, waits for them, and re-layouts  12.2 us (2%)
    all_to_all x15, blocking collectives, blocks_of_all(): return lax.all_to_all(copies, 'tensor', 0, 0)  189 us
    ppermute x45, starting transfers between devices, hand_down(): return lax.ppermute(value, 'section', pairs)  130 us
    pallas_call x22, Pallas kernels, turn(): pl.pallas_call(functools.partial(turn_kernel, first, steps, section, tota...  97.9 us
    ppermute x13, waiting for transfers between devices, across(): return lax.ppermute(value, 'tensor', pairs)  64.3 us
    ppermute x13, starting transfers between devices, across(): return lax.ppermute(value, 'tensor', pairs)  15.7 us
  transfers between devices with their start and end apart: 61, of which 18 were waited for; matrix products, arithmetic and copies ran while one was open for 1% of the time, Pallas kernels for 7%

profile of v7, /device:TPU:0, one launch (start us, length us, event | category | flops | bytes accessed | tf_op | source)
XLA Modules:
  0.0 550.8 jit_solution(6235622971070284627)
XLA Ops:
  32.0 9.1 %collective-permute-done.5.refs_4_ = bf16[576,768]{1,0:T(8,128)(2,1)S(1)} collective-permute-done((bf16[576,768]{1,0:T(8,128)(2,1)}, bf16[576,768]{1,0:T(8,128)(2,1)S(1)}, u32[]{:S(2)}, u32[]{:S(2)}) %collective-permute-start.5) | collective-permute-done | bytes 884768 | tf_op jit(solution)/shard_map/ppermute | solution.py:140
  50.9 14.9 %collective-permute-done.7.refs_1_ = bf16[576,768]{1,0:T(8,128)(2,1)S(1)} collective-permute-done((bf16[576,768]{1,0:T(8,128)(2,1)S(1)}, bf16[576,768]{1,0:T(8,128)(2,1)S(1)}, u32[]{:S(2)}, u32[]{:S(2)}) %collective-permute-start.7) | collective-permute-done | bytes 884768 | tf_op jit(solution)/shard_map/ppermute | solution.py:140
  69.8 10.4 %collective-permute-done.10.refs_4_ = bf16[576,768]{1,0:T(8,128)(2,1)S(1)} collective-permute-done((bf16[576,768]{1,0:T(8,128)(2,1)S(1)}, bf16[576,768]{1,0:T(8,128)(2,1)S(1)}, u32[]{:S(2)}, u32[]{:S(2)}) %collective-permute-start.10) | collective-permute-done | bytes 884768 | tf_op jit(solution)/shard_map/ppermute | solution.py:140
  84.0 17.9 %collective-permute-done.12.refs_6_ = bf16[576,768]{1,0:T(8,128)(2,1)S(1)} collective-permute-done((bf16[576,768]{1,0:T(8,128)(2,1)S(1)}, bf16[576,768]{1,0:T(8,128)(2,1)S(1)}, u32[]{:S(2)}, u32[]{:S(2)}) %collective-permute-start.12) | collective-permute-done | bytes 884768 | tf_op jit(solution)/shard_map/ppermute | solution.py:140
  109.7 14.1 %collective-permute-start.14 = (bf16[128,128]{1,0:T(8,128)(2,1)S(1)}, bf16[128,128]{1,0:T(8,128)(2,1)S(1)}, u32[]{:S(2)}, u32[]{:S(2)}) collective-permute-start(bf16[128,128]{1,0:T(8,128)(2,1)S(1)} %get-tuple-element.155), channel_id=1, source_target_pairs={{0,8},{8,0},{16,24},{24,16},{32,40},{40,32},{48,56},{56,48},{64,72... | collective-permute-start | bytes 98312 | tf_op jit(solution)/shard_map/ppermute | solution.py:48
  125.3 13.4 %all_to_all.80.blocks_ref = bf16[8,128,128]{2,1,0:T(8,128)(2,1)S(1)} all-to-all(bf16[8,128,128]{2,1,0:T(8,128)(2,1)S(1)} %copies.16), channel_id=1, replica_groups=mesh['section'=16,'tensor'=8] {'tensor'}, dimensions={0} | all-to-all | bytes 524288 | tf_op jit(solution)/shard_map/all_to_all | solution.py:69
  147.2 11.5 %all_to_all.81.blocks_ref = bf16[8,128,128]{2,1,0:T(8,128)(2,1)S(1)} all-to-all(bf16[8,128,128]{2,1,0:T(8,128)(2,1)S(1)} %copies.17), channel_id=1, replica_groups=mesh['section'=16,'tensor'=8] {'tensor'}, dimensions={0} | all-to-all | bytes 524288 | tf_op jit(solution)/shard_map/all_to_all | solution.py:69
  165.1 29.6 %collective-permute-start.20 = (bf16[128,128]{1,0:T(8,128)(2,1)S(1)}, bf16[128,128]{1,0:T(8,128)(2,1)S(1)}, u32[]{:S(2)}, u32[]{:S(2)}) collective-permute-start(bf16[128,128]{1,0:T(8,128)(2,1)S(1)} %get-tuple-element.171), channel_id=1, source_target_pairs={{0,8},{8,0},{16,24},{24,16},{32,40},{40,32},{48,56},{56,48},{64,72... | collective-permute-start | bytes 98312 | tf_op jit(solution)/shard_map/ppermute | solution.py:48
  196.1 12.0 %all_to_all.82.blocks_ref = bf16[8,128,128]{2,1,0:T(8,128)(2,1)S(1)} all-to-all(bf16[8,128,128]{2,1,0:T(8,128)(2,1)S(1)} %copies.18), channel_id=1, replica_groups=mesh['section'=16,'tensor'=8] {'tensor'}, dimensions={0} | all-to-all | bytes 524288 | tf_op jit(solution)/shard_map/all_to_all | solution.py:69
  208.1 6.3 %turn.25 = (bf16[5,128,768]{2,1,0:T(8,128)(2,1)S(1)}, bf16[3,128,768]{2,1,0:T(8,128)(2,1)S(1)}, bf16[128,128]{1,0:T(8,128)(2,1)S(1)}, bf16[8,128,768]{2,1,0:T(8,128)(2,1)S(1)}) custom-call(s32[1]{0:T(128)} %bitcast.9.place_ref, bf16[8,128,128]{2,1,0:T(8,128)(2,1)S(1)} %all_to_all.82.blocks_ref, ...), custom_call_target="tpu_custom_call", output_to_operand_aliasing={{3}: (7, {})} | custom-call | flops 2818572288 | bytes 22020096 | tf_op jit(solution)/shard_map/turn/pallas_call | solution.py:329
  216.6 11.3 %all_to_all.83.blocks_ref = bf16[8,128,128]{2,1,0:T(8,128)(2,1)S(1)} all-to-all(bf16[8,128,128]{2,1,0:T(8,128)(2,1)S(1)} %copies.19), channel_id=1, replica_groups=mesh['section'=16,'tensor'=8] {'tensor'}, dimensions={0} | all-to-all | bytes 524288 | tf_op jit(solution)/shard_map/all_to_all | solution.py:69
  234.2 9.9 %collective-permute-start.26 = (bf16[128,128]{1,0:T(8,128)(2,1)S(1)}, bf16[128,128]{1,0:T(8,128)(2,1)S(1)}, u32[]{:S(2)}, u32[]{:S(2)}) collective-permute-start(bf16[128,128]{1,0:T(8,128)(2,1)S(1)} %get-tuple-element.187), channel_id=1, source_target_pairs={{0,8},{8,0},{16,24},{24,16},{32,40},{40,32},{48,56},{56,48},{64,72... | collective-permute-start | bytes 98312 | tf_op jit(solution)/shard_map/ppermute | solution.py:48
  245.5 12.0 %all_to_all.84.blocks_ref = bf16[8,128,128]{2,1,0:T(8,128)(2,1)S(1)} all-to-all(bf16[8,128,128]{2,1,0:T(8,128)(2,1)S(1)} %copies.20), channel_id=1, replica_groups=mesh['section'=16,'tensor'=8] {'tensor'}, dimensions={0} | all-to-all | bytes 524288 | tf_op jit(solution)/shard_map/all_to_all | solution.py:69
  257.5 6.3 %turn.28 = (bf16[5,128,768]{2,1,0:T(8,128)(2,1)S(1)}, bf16[3,128,768]{2,1,0:T(8,128)(2,1)S(1)}, bf16[128,128]{1,0:T(8,128)(2,1)S(1)}, bf16[8,128,768]{2,1,0:T(8,128)(2,1)S(1)}) custom-call(s32[1]{0:T(128)} %bitcast.9.place_ref, bf16[8,128,128]{2,1,0:T(8,128)(2,1)S(1)} %all_to_all.84.blocks_ref, ...), custom_call_target="tpu_custom_call", output_to_operand_aliasing={{3}: (7, {})} | custom-call | flops 2818572288 | bytes 22020096 | tf_op jit(solution)/shard_map/turn/pallas_call | solution.py:329
  266.0 11.3 %all_to_all.85.blocks_ref = bf16[8,128,128]{2,1,0:T(8,128)(2,1)S(1)} all-to-all(bf16[8,128,128]{2,1,0:T(8,128)(2,1)S(1)} %copies.21), channel_id=1, replica_groups=mesh['section'=16,'tensor'=8] {'tensor'}, dimensions={0} | all-to-all | bytes 524288 | tf_op jit(solution)/shard_map/all_to_all | solution.py:69
  283.6 9.9 %collective-permute-start.32 = (bf16[128,128]{1,0:T(8,128)(2,1)S(1)}, bf16[128,128]{1,0:T(8,128)(2,1)S(1)}, u32[]{:S(2)}, u32[]{:S(2)}) collective-permute-start(bf16[128,128]{1,0:T(8,128)(2,1)S(1)} %get-tuple-element.203), channel_id=1, source_target_pairs={{0,8},{8,0},{16,24},{24,16},{32,40},{40,32},{48,56},{56,48},{64,72... | collective-permute-start | bytes 98312 | tf_op jit(solution)/shard_map/ppermute | solution.py:48
  294.9 12.0 %all_to_all.86.blocks_ref = bf16[8,128,128]{2,1,0:T(8,128)(2,1)S(1)} all-to-all(bf16[8,128,128]{2,1,0:T(8,128)(2,1)S(1)} %copies.22), channel_id=1, replica_groups=mesh['section'=16,'tensor'=8] {'tensor'}, dimensions={0} | all-to-all | bytes 524288 | tf_op jit(solution)/shard_map/all_to_all | solution.py:69
  306.9 6.3 %turn.31 = (bf16[5,128,768]{2,1,0:T(8,128)(2,1)S(1)}, bf16[3,128,768]{2,1,0:T(8,128)(2,1)S(1)}, bf16[128,128]{1,0:T(8,128)(2,1)S(1)}, bf16[8,128,768]{2,1,0:T(8,128)(2,1)S(1)}) custom-call(s32[1]{0:T(128)} %bitcast.9.place_ref, bf16[8,128,128]{2,1,0:T(8,128)(2,1)S(1)} %all_to_all.86.blocks_ref, ...), custom_call_target="tpu_custom_call", output_to_operand_aliasing={{3}: (7, {})} | custom-call | flops 2818572288 | bytes 22020096 | tf_op jit(solution)/shard_map/turn/pallas_call | solution.py:329
  315.4 11.6 %all_to_all.87.blocks_ref = bf16[8,128,128]{2,1,0:T(8,128)(2,1)S(1)} all-to-all(bf16[8,128,128]{2,1,0:T(8,128)(2,1)S(1)} %copies.23), channel_id=1, replica_groups=mesh['section'=16,'tensor'=8] {'tensor'}, dimensions={0} | all-to-all | bytes 524288 | tf_op jit(solution)/shard_map/all_to_all | solution.py:69
  335.1 21.3 %all_to_all.88.blocks_ref = bf16[8,128,128]{2,1,0:T(8,128)(2,1)S(1)} all-to-all(bf16[8,128,128]{2,1,0:T(8,128)(2,1)S(1)} %copies.24), channel_id=1, replica_groups=mesh['section'=16,'tensor'=8] {'tensor'}, dimensions={0} | all-to-all | bytes 524288 | tf_op jit(solution)/shard_map/all_to_all | solution.py:69
  356.5 6.3 %turn.34 = (bf16[5,128,768]{2,1,0:T(8,128)(2,1)S(1)}, bf16[3,128,768]{2,1,0:T(8,128)(2,1)S(1)}, bf16[128,128]{1,0:T(8,128)(2,1)S(1)}, bf16[8,128,768]{2,1,0:T(8,128)(2,1)S(1)}) custom-call(s32[1]{0:T(128)} %bitcast.9.place_ref, bf16[8,128,128]{2,1,0:T(8,128)(2,1)S(1)} %all_to_all.88.blocks_ref, ...), custom_call_target="tpu_custom_call", output_to_operand_aliasing={{3}: (7, {})} | custom-call | flops 2818572288 | bytes 22020096 | tf_op jit(solution)/shard_map/turn/pallas_call | solution.py:329
  365.0 12.8 %all_to_all.89.blocks_ref = bf16[8,128,128]{2,1,0:T(8,128)(2,1)S(1)} all-to-all(bf16[8,128,128]{2,1,0:T(8,128)(2,1)S(1)} %copies.25), channel_id=1, replica_groups=mesh['section'=16,'tensor'=8] {'tensor'}, dimensions={0} | all-to-all | bytes 524288 | tf_op jit(solution)/shard_map/all_to_all | solution.py:69
  384.1 8.3 %collective-permute-start.44 = (bf16[128,128]{1,0:T(8,128)(2,1)S(1)}, bf16[128,128]{1,0:T(8,128)(2,1)S(1)}, u32[]{:S(2)}, u32[]{:S(2)}) collective-permute-start(bf16[128,128]{1,0:T(8,128)(2,1)S(1)} %get-tuple-element.235), channel_id=1, source_target_pairs={{0,8},{8,0},{16,24},{24,16},{32,40},{40,32},{48,56},{56,48},{64,72... | collective-permute-start | bytes 98312 | tf_op jit(solution)/shard_map/ppermute | solution.py:48
  393.8 13.3 %all_to_all.90.blocks_ref = bf16[8,128,128]{2,1,0:T(8,128)(2,1)S(1)} all-to-all(bf16[8,128,128]{2,1,0:T(8,128)(2,1)S(1)} %copies.26), channel_id=1, replica_groups=mesh['section'=16,'tensor'=8] {'tensor'}, dimensions={0} | all-to-all | bytes 524288 | tf_op jit(solution)/shard_map/all_to_all | solution.py:69
  415.6 11.3 %all_to_all.91.blocks_ref = bf16[8,128,128]{2,1,0:T(8,128)(2,1)S(1)} all-to-all(bf16[8,128,128]{2,1,0:T(8,128)(2,1)S(1)} %copies.27), channel_id=1, replica_groups=mesh['section'=16,'tensor'=8] {'tensor'}, dimensions={0} | all-to-all | bytes 524288 | tf_op jit(solution)/shard_map/all_to_all | solution.py:69
  433.2 9.4 %collective-permute-start.50 = (bf16[128,128]{1,0:T(8,128)(2,1)S(1)}, bf16[128,128]{1,0:T(8,128)(2,1)S(1)}, u32[]{:S(2)}, u32[]{:S(2)}) collective-permute-start(bf16[128,128]{1,0:T(8,128)(2,1)S(1)} %get-tuple-element.251), channel_id=1, source_target_pairs={{0,8},{8,0},{16,24},{24,16},{32,40},{40,32},{48,56},{56,48},{64,72... | collective-permute-start | bytes 98312 | tf_op jit(solution)/shard_map/ppermute | solution.py:48
  444.0 12.0 %all_to_all.92.blocks_ref = bf16[8,128,128]{2,1,0:T(8,128)(2,1)S(1)} all-to-all(bf16[8,128,128]{2,1,0:T(8,128)(2,1)S(1)} %copies.28), channel_id=1, replica_groups=mesh['section'=16,'tensor'=8] {'tensor'}, dimensions={0} | all-to-all | bytes 524288 | tf_op jit(solution)/shard_map/all_to_all | solution.py:69
  464.5 11.6 %all_to_all.93.blocks_ref = bf16[8,128,128]{2,1,0:T(8,128)(2,1)S(1)} all-to-all(bf16[8,128,128]{2,1,0:T(8,128)(2,1)S(1)} %copies.29), channel_id=1, replica_groups=mesh['section'=16,'tensor'=8] {'tensor'}, dimensions={0} | all-to-all | bytes 524288 | tf_op jit(solution)/shard_map/all_to_all | solution.py:69
  482.5 30.2 %collective-permute-start.56 = (bf16[128,128]{1,0:T(8,128)(2,1)S(1)}, bf16[128,128]{1,0:T(8,128)(2,1)S(1)}, u32[]{:S(2)}, u32[]{:S(2)}) collective-permute-start(bf16[128,128]{1,0:T(8,128)(2,1)S(1)} %get-tuple-element.267), channel_id=1, source_target_pairs={{0,8},{8,0},{16,24},{24,16},{32,40},{40,32},{48,56},{56,48},{64,72... | collective-permute-start | bytes 98312 | tf_op jit(solution)/shard_map/ppermute | solution.py:48
  514.1 12.0 %all_to_all.94.blocks_ref = bf16[8,128,128]{2,1,0:T(8,128)(2,1)S(1)} all-to-all(bf16[8,128,128]{2,1,0:T(8,128)(2,1)S(1)} %copies.30), channel_id=1, replica_groups=mesh['section'=16,'tensor'=8] {'tensor'}, dimensions={0} | all-to-all | bytes 524288 | tf_op jit(solution)/shard_map/all_to_all | solution.py:69
  526.1 9.4 %turn.43 = (bf16[5,128,768]{2,1,0:T(8,128)(2,1)}, bf16[3,128,768]{2,1,0:T(8,128)(2,1)}, bf16[128,128]{1,0:T(8,128)(2,1)S(1)}, bf16[8,128,768]{2,1,0:T(8,128)(2,1)S(1)}) custom-call(s32[1]{0:T(128)} %bitcast.9.place_ref, bf16[8,128,128]{2,1,0:T(8,128)(2,1)S(1)} %all_to_all.94.blocks_ref, ...), custom_call_target="tpu_custom_call", output_to_operand_aliasing={{3}: (7, {})} | custom-call | flops 2818572288 | bytes 22020096 | tf_op jit(solution)/shard_map/turn/pallas_call | solution.py:329
  540.8 6.3 %weight_grads.1 = bf16[768,6144]{1,0:T(8,128)(2,1)} custom-call(bf16[768,128]{1,0:T(8,128)(2,1)S(1)} %copy-done.7, bf16[8,128,768]{2,1,0:T(8,128)(2,1)S(1)} %get-tuple-element.273.rows_ref), custom_call_target="tpu_custom_call" | custom-call | flops 1207959552 | bytes 9437184 | tf_op jit(solution)/shard_map/weight_grads/pallas_call | solution.py:440
  (200 shorter events, 154.6 us)
Async XLA Ops:
  8.3 36.9 %collective-permute-start.1 = (bf16[1152,768]{1,0:T(8,128)(2,1)S(1)}, bf16[1152,768]{1,0:T(8,128)(2,1)}, u32[]{:S(2)}, u32[]{:S(2)}) collective-permute-start(bf16[1152,768]{1,0:T(8,128)(2,1)S(1)} %pad_maximum_fusion.refs_0_), channel_id=1, source_target_pairs={{0,4},{1,5},{2,6},{3,7},{4,0},{5,1},{6,2},{7,3},{8,12},{9,13},{10,... | collective-permute-start | bytes 5308424 | tf_op jit(solution)/shard_map/ppermute | solution.py:140
  14.7 15.1 %collective-permute-start.3 = (bf16[576,768]{1,0:T(8,128)(2,1)}, bf16[576,768]{1,0:T(8,128)(2,1)}, u32[]{:S(2)}, u32[]{:S(2)}) collective-permute-start(bf16[576,768]{1,0:T(8,128)(2,1)} %get-tuple-element.143), channel_id=1, source_target_pairs={{0,3},{1,0},{2,1},{3,2},{4,7},{5,4},{6,5},{7,6},{8,11},{9,8},{10,9... | collective-permute-start | bytes 2654216 | tf_op jit(solution)/shard_map/ppermute | solution.py:140
  17.5 14.6 %collective-permute-start.2 = (bf16[576,768]{1,0:T(8,128)(2,1)}, bf16[576,768]{1,0:T(8,128)(2,1)}, u32[]{:S(2)}, u32[]{:S(2)}) collective-permute-start(bf16[576,768]{1,0:T(8,128)(2,1)} %get-tuple-element.143), channel_id=1, source_target_pairs={{0,1},{1,2},{2,3},{3,0},{4,5},{5,6},{6,7},{7,4},{8,9},{9,10},{10,1... | collective-permute-start | bytes 2654216 | tf_op jit(solution)/shard_map/ppermute | solution.py:140
  17.5 23.7 %collective-permute-start.5 = (bf16[576,768]{1,0:T(8,128)(2,1)}, bf16[576,768]{1,0:T(8,128)(2,1)S(1)}, u32[]{:S(2)}, u32[]{:S(2)}) collective-permute-start(bf16[576,768]{1,0:T(8,128)(2,1)} %get-tuple-element.144), channel_id=1, source_target_pairs={{0,3},{1,0},{2,1},{3,2},{4,7},{5,4},{6,5},{7,6},{8,11},{9,8},{10,9... | collective-permute-start | bytes 2654216 | tf_op jit(solution)/shard_map/ppermute | solution.py:140
  20.7 24.4 %collective-permute-start.4 = (bf16[576,768]{1,0:T(8,128)(2,1)}, bf16[576,768]{1,0:T(8,128)(2,1)}, u32[]{:S(2)}, u32[]{:S(2)}) collective-permute-start(bf16[576,768]{1,0:T(8,128)(2,1)} %get-tuple-element.144), channel_id=1, source_target_pairs={{0,1},{1,2},{2,3},{3,0},{4,5},{5,6},{6,7},{7,4},{8,9},{9,10},{10,1... | collective-permute-start | bytes 2654216 | tf_op jit(solution)/shard_map/ppermute | solution.py:140
  45.1 20.7 %collective-permute-start.7 = (bf16[576,768]{1,0:T(8,128)(2,1)S(1)}, bf16[576,768]{1,0:T(8,128)(2,1)S(1)}, u32[]{:S(2)}, u32[]{:S(2)}) collective-permute-start(bf16[576,768]{1,0:T(8,128)(2,1)S(1)} %collective-permute-done.5.refs_4_), channel_id=1, source_target_pairs={{0,3},{1,0},{2,1},{3,2},{4,7},{5,4},{6,5},{7,6},{8,11},{9,8},{10,9... | collective-permute-start | bytes 2654216 | tf_op jit(solution)/shard_map/ppermute | solution.py:140
  46.4 23.5 %collective-permute-start.8 = (bf16[576,768]{1,0:T(8,128)(2,1)S(1)}, bf16[576,768]{1,0:T(8,128)(2,1)S(1)}, u32[]{:S(2)}, u32[]{:S(2)}) collective-permute-start(bf16[576,768]{1,0:T(8,128)(2,1)S(1)} %slice.42), channel_id=1, source_target_pairs={{0,1},{1,2},{2,3},{3,0},{4,5},{5,6},{6,7},{7,4},{8,9},{9,10},{10,1... | collective-permute-start | bytes 2654216 | tf_op jit(solution)/shard_map/ppermute | solution.py:140
  48.5 31.7 %collective-permute-start.10 = (bf16[576,768]{1,0:T(8,128)(2,1)S(1)}, bf16[576,768]{1,0:T(8,128)(2,1)S(1)}, u32[]{:S(2)}, u32[]{:S(2)}) collective-permute-start(bf16[576,768]{1,0:T(8,128)(2,1)S(1)} %slice.42), channel_id=1, source_target_pairs={{0,3},{1,0},{2,1},{3,2},{4,7},{5,4},{6,5},{7,6},{8,11},{9,8},{10,9... | collective-permute-start | bytes 2654216 | tf_op jit(solution)/shard_map/ppermute | solution.py:140
  49.7 34.3 %collective-permute-start.11 = (bf16[576,768]{1,0:T(8,128)(2,1)S(1)}, bf16[576,768]{1,0:T(8,128)(2,1)S(1)}, u32[]{:S(2)}, u32[]{:S(2)}) collective-permute-start(bf16[576,768]{1,0:T(8,128)(2,1)S(1)} %collective-permute-done.5.refs_4_), channel_id=1, source_target_pairs={{0,4},{1,5},{2,6},{3,7},{4,0},{5,1},{6,2},{7,3},{8,12},{9,13},{10,... | collective-permute-start | bytes 2654216 | tf_op jit(solution)/shard_map/ppermute | solution.py:140
  50.1 33.8 %collective-permute-start.6 = (bf16[576,768]{1,0:T(8,128)(2,1)}, bf16[576,768]{1,0:T(8,128)(2,1)S(1)}, u32[]{:S(2)}, u32[]{:S(2)}) collective-permute-start(bf16[576,768]{1,0:T(8,128)(2,1)} %collective-permute-done.2.refs_1_), channel_id=1, source_target_pairs={{0,1},{1,2},{2,3},{3,0},{4,5},{5,6},{6,7},{7,4},{8,9},{9,10},{10,1... | collective-permute-start | bytes 2654216 | tf_op jit(solution)/shard_map/ppermute | solution.py:140
  65.9 18.1 %collective-permute-start.9 = (bf16[576,768]{1,0:T(8,128)(2,1)}, bf16[576,768]{1,0:T(8,128)(2,1)S(1)}, u32[]{:S(2)}, u32[]{:S(2)}) collective-permute-start(bf16[576,768]{1,0:T(8,128)(2,1)} %collective-permute-done.4.refs_2_), channel_id=1, source_target_pairs={{0,4},{1,5},{2,6},{3,7},{4,0},{5,1},{6,2},{7,3},{8,12},{9,13},{10,... | collective-permute-start | bytes 2654216 | tf_op jit(solution)/shard_map/ppermute | solution.py:140
  69.8 32.0 %collective-permute-start.12 = (bf16[576,768]{1,0:T(8,128)(2,1)S(1)}, bf16[576,768]{1,0:T(8,128)(2,1)S(1)}, u32[]{:S(2)}, u32[]{:S(2)}) collective-permute-start(bf16[576,768]{1,0:T(8,128)(2,1)S(1)} %collective-permute-done.8.refs_2_), channel_id=1, source_target_pairs={{0,1},{1,2},{2,3},{3,0},{4,5},{5,6},{6,7},{7,4},{8,9},{9,10},{10,1... | collective-permute-start | bytes 2654216 | tf_op jit(solution)/shard_map/ppermute | solution.py:140
  80.2 24.1 %collective-permute-start.13 = (bf16[576,768]{1,0:T(8,128)(2,1)S(1)}, bf16[576,768]{1,0:T(8,128)(2,1)S(1)}, u32[]{:S(2)}, u32[]{:S(2)}) collective-permute-start(bf16[576,768]{1,0:T(8,128)(2,1)S(1)} %collective-permute-done.7.refs_1_), channel_id=1, source_target_pairs={{0,4},{1,5},{2,6},{3,7},{4,0},{5,1},{6,2},{7,3},{8,12},{9,13},{10,... | collective-permute-start | bytes 2654216 | tf_op jit(solution)/shard_map/ppermute | solution.py:140
  109.7 15.0 %collective-permute-start.14 = (bf16[128,128]{1,0:T(8,128)(2,1)S(1)}, bf16[128,128]{1,0:T(8,128)(2,1)S(1)}, u32[]{:S(2)}, u32[]{:S(2)}) collective-permute-start(bf16[128,128]{1,0:T(8,128)(2,1)S(1)} %get-tuple-element.155), channel_id=1, source_target_pairs={{0,8},{8,0},{16,24},{24,16},{32,40},{40,32},{48,56},{56,48},{64,72... | collective-permute-start | bytes 98312 | tf_op jit(solution)/shard_map/ppermute | solution.py:48
  124.7 14.0 %collective-permute-start.15 = (bf16[5,128,768]{2,1,0:T(8,128)(2,1)S(1)}, bf16[5,128,768]{2,1,0:T(8,128)(2,1)S(1)}, u32[]{:S(2)}, u32[]{:S(2)}) collective-permute-start(bf16[5,128,768]{2,1,0:T(8,128)(2,1)S(1)} %slice.47), channel_id=1, source_target_pairs={{0,8},{8,0},{16,24},{24,16},{32,40},{40,32},{48,56},{56,48},{64,72... | collective-permute-start | bytes 2949128 | tf_op jit(solution)/shard_map/ppermute | solution.py:48
  125.1 13.6 %collective-permute-start.16 = (bf16[3,128,768]{2,1,0:T(8,128)(2,1)S(1)}, bf16[3,128,768]{2,1,0:T(8,128)(2,1)S(1)}, u32[]{:S(2)}, u32[]{:S(2)}) collective-permute-start(bf16[3,128,768]{2,1,0:T(8,128)(2,1)S(1)} %slice.48), channel_id=1, source_target_pairs={{0,8},{8,0},{16,24},{24,16},{32,40},{40,32},{48,56},{56,48},{64,72... | collective-permute-start | bytes 1769480 | tf_op jit(solution)/shard_map/ppermute | solution.py:48
  146.5 16.1 %collective-permute-start.19 = (bf16[3,128,768]{2,1,0:T(8,128)(2,1)S(1)}, bf16[3,128,768]{2,1,0:T(8,128)(2,1)S(1)}, u32[]{:S(2)}, u32[]{:S(2)}) collective-permute-start(bf16[3,128,768]{2,1,0:T(8,128)(2,1)S(1)} %get-tuple-element.167), channel_id=1, source_target_pairs={{0,0},{8,16},{16,8},{24,32},{32,24},{40,48},{48,40},{56,56},{64,64... | collective-permute-start | bytes 1769480 | tf_op jit(solution)/shard_map/ppermute | solution.py:48
  165.1 30.5 %collective-permute-start.20 = (bf16[128,128]{1,0:T(8,128)(2,1)S(1)}, bf16[128,128]{1,0:T(8,128)(2,1)S(1)}, u32[]{:S(2)}, u32[]{:S(2)}) collective-permute-start(bf16[128,128]{1,0:T(8,128)(2,1)S(1)} %get-tuple-element.171), channel_id=1, source_target_pairs={{0,8},{8,0},{16,24},{24,16},{32,40},{40,32},{48,56},{56,48},{64,72... | collective-permute-start | bytes 98312 | tf_op jit(solution)/shard_map/ppermute | solution.py:48
  215.8 15.9 %collective-permute-start.25 = (bf16[3,128,768]{2,1,0:T(8,128)(2,1)S(1)}, bf16[3,128,768]{2,1,0:T(8,128)(2,1)S(1)}, u32[]{:S(2)}, u32[]{:S(2)}) collective-permute-start(bf16[3,128,768]{2,1,0:T(8,128)(2,1)S(1)} %get-tuple-element.183), channel_id=1, source_target_pairs={{0,0},{8,16},{16,8},{24,32},{32,24},{40,48},{48,40},{56,56},{64,64... | collective-permute-start | bytes 1769480 | tf_op jit(solution)/shard_map/ppermute | solution.py:48
  265.2 15.9 %collective-permute-start.31 = (bf16[3,128,768]{2,1,0:T(8,128)(2,1)S(1)}, bf16[3,128,768]{2,1,0:T(8,128)(2,1)S(1)}, u32[]{:S(2)}, u32[]{:S(2)}) collective-permute-start(bf16[3,128,768]{2,1,0:T(8,128)(2,1)S(1)} %get-tuple-element.199), channel_id=1, source_target_pairs={{0,0},{8,16},{16,8},{24,32},{32,24},{40,48},{48,40},{56,56},{64,64... | collective-permute-start | bytes 1769480 | tf_op jit(solution)/shard_map/ppermute | solution.py:48
  313.9 13.0 %collective-permute-start.36 = (bf16[5,128,768]{2,1,0:T(8,128)(2,1)S(1)}, bf16[5,128,768]{2,1,0:T(8,128)(2,1)S(1)}, u32[]{:S(2)}, u32[]{:S(2)}) collective-permute-start(bf16[5,128,768]{2,1,0:T(8,128)(2,1)S(1)} %get-tuple-element.212), channel_id=1, source_target_pairs={{0,0},{8,8},{16,16},{24,24},{32,32},{40,40},{48,48},{56,64},{64,56... | collective-permute-start | bytes 2949128 | tf_op jit(solution)/shard_map/ppermute | solution.py:48
  314.7 16.1 %collective-permute-start.37 = (bf16[3,128,768]{2,1,0:T(8,128)(2,1)S(1)}, bf16[3,128,768]{2,1,0:T(8,128)(2,1)S(1)}, u32[]{:S(2)}, u32[]{:S(2)}) collective-permute-start(bf16[3,128,768]{2,1,0:T(8,128)(2,1)S(1)} %get-tuple-element.215), channel_id=1, source_target_pairs={{0,0},{8,8},{16,16},{24,24},{32,32},{40,40},{48,48},{56,64},{64,56... | collective-permute-start | bytes 1769480 | tf_op jit(solution)/shard_map/ppermute | solution.py:48
  334.6 21.9 %collective-permute-start.39 = (bf16[5,128,768]{2,1,0:T(8,128)(2,1)S(1)}, bf16[5,128,768]{2,1,0:T(8,128)(2,1)S(1)}, u32[]{:S(2)}, u32[]{:S(2)}) collective-permute-start(bf16[5,128,768]{2,1,0:T(8,128)(2,1)S(1)} %get-tuple-element.221), channel_id=1, source_target_pairs={{0,8},{8,0},{16,24},{24,16},{32,40},{40,32},{48,56},{56,48},{64,72... | collective-permute-start | bytes 2949128 | tf_op jit(solution)/shard_map/ppermute | solution.py:48
  334.8 21.7 %collective-permute-start.40 = (bf16[3,128,768]{2,1,0:T(8,128)(2,1)S(1)}, bf16[3,128,768]{2,1,0:T(8,128)(2,1)S(1)}, u32[]{:S(2)}, u32[]{:S(2)}) collective-permute-start(bf16[3,128,768]{2,1,0:T(8,128)(2,1)S(1)} %get-tuple-element.222), channel_id=1, source_target_pairs={{0,8},{8,0},{16,24},{24,16},{32,40},{40,32},{48,56},{56,48},{64,72... | collective-permute-start | bytes 1769480 | tf_op jit(solution)/shard_map/ppermute | solution.py:48
  363.5 14.3 %collective-permute-start.42 = (bf16[5,128,768]{2,1,0:T(8,128)(2,1)S(1)}, bf16[5,128,768]{2,1,0:T(8,128)(2,1)S(1)}, u32[]{:S(2)}, u32[]{:S(2)}) collective-permute-start(bf16[5,128,768]{2,1,0:T(8,128)(2,1)S(1)} %get-tuple-element.228), channel_id=1, source_target_pairs={{0,0},{8,16},{16,8},{24,32},{32,24},{40,48},{48,40},{56,56},{64,64... | collective-permute-start | bytes 2949128 | tf_op jit(solution)/shard_map/ppermute | solution.py:48
  364.2 17.4 %collective-permute-start.43 = (bf16[3,128,768]{2,1,0:T(8,128)(2,1)S(1)}, bf16[3,128,768]{2,1,0:T(8,128)(2,1)S(1)}, u32[]{:S(2)}, u32[]{:S(2)}) collective-permute-start(bf16[3,128,768]{2,1,0:T(8,128)(2,1)S(1)} %get-tuple-element.231), channel_id=1, source_target_pairs={{0,0},{8,16},{16,8},{24,32},{32,24},{40,48},{48,40},{56,56},{64,64... | collective-permute-start | bytes 1769480 | tf_op jit(solution)/shard_map/ppermute | solution.py:48
  393.2 13.8 %collective-permute-start.45 = (bf16[5,128,768]{2,1,0:T(8,128)(2,1)S(1)}, bf16[5,128,768]{2,1,0:T(8,128)(2,1)S(1)}, u32[]{:S(2)}, u32[]{:S(2)}) collective-permute-start(bf16[5,128,768]{2,1,0:T(8,128)(2,1)S(1)} %get-tuple-element.237), channel_id=1, source_target_pairs={{0,8},{8,0},{16,24},{24,16},{32,40},{40,32},{48,56},{56,48},{64,72... | collective-permute-start | bytes 2949128 | tf_op jit(solution)/shard_map/ppermute | solution.py:48
  393.6 13.5 %collective-permute-start.46 = (bf16[3,128,768]{2,1,0:T(8,128)(2,1)S(1)}, bf16[3,128,768]{2,1,0:T(8,128)(2,1)S(1)}, u32[]{:S(2)}, u32[]{:S(2)}) collective-permute-start(bf16[3,128,768]{2,1,0:T(8,128)(2,1)S(1)} %get-tuple-element.238), channel_id=1, source_target_pairs={{0,8},{8,0},{16,24},{24,16},{32,40},{40,32},{48,56},{56,48},{64,72... | collective-permute-start | bytes 1769480 | tf_op jit(solution)/shard_map/ppermute | solution.py:48
  414.8 15.9 %collective-permute-start.49 = (bf16[3,128,768]{2,1,0:T(8,128)(2,1)S(1)}, bf16[3,128,768]{2,1,0:T(8,128)(2,1)S(1)}, u32[]{:S(2)}, u32[]{:S(2)}) collective-permute-start(bf16[3,128,768]{2,1,0:T(8,128)(2,1)S(1)} %get-tuple-element.247), channel_id=1, source_target_pairs={{0,0},{8,16},{16,8},{24,32},{32,24},{40,48},{48,40},{56,56},{64,64... | collective-permute-start | bytes 1769480 | tf_op jit(solution)/shard_map/ppermute | solution.py:48
  463.0 13.1 %collective-permute-start.54 = (bf16[5,128,768]{2,1,0:T(8,128)(2,1)S(1)}, bf16[5,128,768]{2,1,0:T(8,128)(2,1)S(1)}, u32[]{:S(2)}, u32[]{:S(2)}) collective-permute-start(bf16[5,128,768]{2,1,0:T(8,128)(2,1)S(1)} %get-tuple-element.260), channel_id=1, source_target_pairs={{0,0},{8,16},{16,8},{24,32},{32,24},{40,48},{48,40},{56,56},{64,64... | collective-permute-start | bytes 2949128 | tf_op jit(solution)/shard_map/ppermute | solution.py:48
  463.8 16.2 %collective-permute-start.55 = (bf16[3,128,768]{2,1,0:T(8,128)(2,1)S(1)}, bf16[3,128,768]{2,1,0:T(8,128)(2,1)S(1)}, u32[]{:S(2)}, u32[]{:S(2)}) collective-permute-start(bf16[3,128,768]{2,1,0:T(8,128)(2,1)S(1)} %get-tuple-element.263), channel_id=1, source_target_pairs={{0,0},{8,16},{16,8},{24,32},{32,24},{40,48},{48,40},{56,56},{64,64... | collective-permute-start | bytes 1769480 | tf_op jit(solution)/shard_map/ppermute | solution.py:48
  482.5 31.1 %collective-permute-start.56 = (bf16[128,128]{1,0:T(8,128)(2,1)S(1)}, bf16[128,128]{1,0:T(8,128)(2,1)S(1)}, u32[]{:S(2)}, u32[]{:S(2)}) collective-permute-start(bf16[128,128]{1,0:T(8,128)(2,1)S(1)} %get-tuple-element.267), channel_id=1, source_target_pairs={{0,8},{8,0},{16,24},{24,16},{32,40},{40,32},{48,56},{56,48},{64,72... | collective-permute-start | bytes 98312 | tf_op jit(solution)/shard_map/ppermute | solution.py:48
  (43 other events, 327.9 us)

commit v8 on v6

--- a/solution.py
+++ b/solution.py
@@ -13,7 +13,7 @@
 NN = (((1,), (0,)), ((), ()))
 
 
-AHEAD = 5
+AHEAD = 6
 
 
 def causal_probs(query_heads, key_rows):

time: 558 us -> 635 us (1.14)
  blocking collectives: 189 us -> 101 us
  local copies, waits for them, and re-layouts: 12.2 us -> 77.6 us
  waiting for transfers between devices: 75.8 us -> 125 us
  starting transfers between devices: 151 us -> 190 us
  Pallas kernels: 118 us -> 128 us
    all_to_all x15 -> x8, blocking collectives: 189 us -> 101 us  [blocks_of_all(): return lax.all_to_all(copies, 'tensor', 0, 0)]
    unnamed x29 -> x73, local copies, waits for them, and re-layouts: 7.79 us -> 73.9 us
    all_to_all x1 -> x8, waiting for transfers between devices: 0.56 us -> 49.7 us  [blocks_of_all(): return lax.all_to_all(copies, 'tensor', 0, 0)]
    all_to_all x1 -> x8, starting transfers between devices: 3.41 us -> 28.1 us  [blocks_of_all(): return lax.all_to_all(copies, 'tensor', 0, 0)]
    ppermute x45, starting transfers between devices: 130 us -> 145 us  [hand_down(): return lax.ppermute(value, 'section', pairs)]
  transfers between devices with their start and end apart: 61 -> 68, of which waited for: 18 -> 25; matrix products, arithmetic and copies ran while one was open for 1% -> 1% of each run, Pallas kernels for 7% -> 8%
where the time goes in v8:
time: 635 us; the launch traced here: 625 us
  starting transfers between devices  190 us (30%)
  Pallas kernels  128 us (20%)
  waiting for transfers between devices  125 us (20%)
  blocking collectives  101 us (16%)
  local copies, waits for them, and re-layouts  77.6 us (12%)
    ppermute x45, starting transfers between devices, hand_down(): return lax.ppermute(value, 'section', pairs)  145 us
    pallas_call x22, Pallas kernels, turn(): pl.pallas_call(functools.partial(turn_kernel, first, steps, section, tota...  101 us
    all_to_all x8, blocking collectives, blocks_of_all(): return lax.all_to_all(copies, 'tensor', 0, 0)  101 us
    unnamed x73, local copies, waits for them, and re-layouts  73.9 us
    ppermute x13, waiting for transfers between devices, across(): return lax.ppermute(value, 'tensor', pairs)  64.2 us
    all_to_all x8, waiting for transfers between devices, blocks_of_all(): return lax.all_to_all(copies, 'tensor', 0, 0)  49.7 us
    all_to_all x8, starting transfers between devices, blocks_of_all(): return lax.all_to_all(copies, 'tensor', 0, 0)  28.1 us
    ppermute x13, starting transfers between devices, across(): return lax.ppermute(value, 'tensor', pairs)  15.7 us
  transfers between devices with their start and end apart: 68, of which 25 were waited for; matrix products, arithmetic and copies ran while one was open for 1% of the time, Pallas kernels for 8%

profile of v8, /device:TPU:0, one launch (start us, length us, event | category | flops | bytes accessed | tf_op | source)
XLA Modules:
  0.0 624.7 jit_solution(17951030951491074116)
XLA Ops:
  31.3 9.1 %collective-permute-done.5.refs_4_ = bf16[576,768]{1,0:T(8,128)(2,1)S(1)} collective-permute-done((bf16[576,768]{1,0:T(8,128)(2,1)}, bf16[576,768]{1,0:T(8,128)(2,1)S(1)}, u32[]{:S(2)}, u32[]{:S(2)}) %collective-permute-start.5) | collective-permute-done | bytes 884768 | tf_op jit(solution)/shard_map/ppermute | solution.py:140
  50.2 14.9 %collective-permute-done.7.refs_1_ = bf16[576,768]{1,0:T(8,128)(2,1)S(1)} collective-permute-done((bf16[576,768]{1,0:T(8,128)(2,1)S(1)}, bf16[576,768]{1,0:T(8,128)(2,1)S(1)}, u32[]{:S(2)}, u32[]{:S(2)}) %collective-permute-start.7) | collective-permute-done | bytes 884768 | tf_op jit(solution)/shard_map/ppermute | solution.py:140
  69.1 10.4 %collective-permute-done.10.refs_4_ = bf16[576,768]{1,0:T(8,128)(2,1)S(1)} collective-permute-done((bf16[576,768]{1,0:T(8,128)(2,1)S(1)}, bf16[576,768]{1,0:T(8,128)(2,1)S(1)}, u32[]{:S(2)}, u32[]{:S(2)}) %collective-permute-start.10) | collective-permute-done | bytes 884768 | tf_op jit(solution)/shard_map/ppermute | solution.py:140
  83.2 17.9 %collective-permute-done.12.refs_6_ = bf16[576,768]{1,0:T(8,128)(2,1)S(1)} collective-permute-done((bf16[576,768]{1,0:T(8,128)(2,1)S(1)}, bf16[576,768]{1,0:T(8,128)(2,1)S(1)}, u32[]{:S(2)}, u32[]{:S(2)}) %collective-permute-start.12) | collective-permute-done | bytes 884768 | tf_op jit(solution)/shard_map/ppermute | solution.py:140
  108.8 14.1 %collective-permute-start.14 = (bf16[128,128]{1,0:T(8,128)(2,1)S(1)}, bf16[128,128]{1,0:T(8,128)(2,1)S(1)}, u32[]{:S(2)}, u32[]{:S(2)}) collective-permute-start(bf16[128,128]{1,0:T(8,128)(2,1)S(1)} %get-tuple-element.155), channel_id=1, source_target_pairs={{0,8},{8,0},{16,24},{24,16},{32,40},{40,32},{48,56},{56,48},{64,72... | collective-permute-start | bytes 98312 | tf_op jit(solution)/shard_map/ppermute | solution.py:48
  124.4 13.4 %all_to_all.80.blocks_ref = bf16[8,128,128]{2,1,0:T(8,128)(2,1)S(1)} all-to-all(bf16[8,128,128]{2,1,0:T(8,128)(2,1)S(1)} %copies.16), channel_id=1, replica_groups=mesh['section'=16,'tensor'=8] {'tensor'}, dimensions={0} | all-to-all | bytes 524288 | tf_op jit(solution)/shard_map/all_to_all | solution.py:69
  137.8 7.2 %turn.22 = (bf16[6,128,768]{2,1,0:T(8,128)(2,1)}, bf16[2,128,768]{2,1,0:T(8,128)(2,1)S(1)}, bf16[128,128]{1,0:T(8,128)(2,1)S(1)}, bf16[8,128,768]{2,1,0:T(8,128)(2,1)S(1)}) custom-call(s32[1]{0:T(128)} %bitcast.9.place_ref, bf16[8,128,128]{2,1,0:T(8,128)(2,1)S(1)} %all_to_all.80.blocks_ref, ...), custom_call_target="tpu_custom_call", output_to_operand_aliasing={{3}: (7, {})} | custom-call | flops 2818572288 | bytes 22020096 | tf_op jit(solution)/shard_map/turn/pallas_call | solution.py:320
  154.3 6.9 %all-to-all-done.1.blocks_ref = bf16[8,128,128]{2,1,0:T(8,128)(2,1)S(1)} async-done(((bf16[8,128,128]{2,1,0:T(8,128)(2,1)}), bf16[8,128,128]{2,1,0:T(8,128)(2,1)S(1)}, u32[]{:S(2)}, u32[]{:S(2)}) %all-to-all-start.1) | async-done | bytes 262176 | tf_op jit(solution)/shard_map/all_to_all | solution.py:69
  176.2 27.6 %collective-permute-start.20 = (bf16[128,128]{1,0:T(8,128)(2,1)S(1)}, bf16[128,128]{1,0:T(8,128)(2,1)S(1)}, u32[]{:S(2)}, u32[]{:S(2)}) collective-permute-start(bf16[128,128]{1,0:T(8,128)(2,1)S(1)} %get-tuple-element.171), channel_id=1, source_target_pairs={{0,8},{8,0},{16,24},{24,16},{32,40},{40,32},{48,56},{56,48},{64,72... | collective-permute-start | bytes 98312 | tf_op jit(solution)/shard_map/ppermute | solution.py:48
  205.2 12.0 %all_to_all.81.blocks_ref = bf16[8,128,128]{2,1,0:T(8,128)(2,1)S(1)} all-to-all(bf16[8,128,128]{2,1,0:T(8,128)(2,1)S(1)} %copies.18), channel_id=1, replica_groups=mesh['section'=16,'tensor'=8] {'tensor'}, dimensions={0} | all-to-all | bytes 524288 | tf_op jit(solution)/shard_map/all_to_all | solution.py:69
  217.2 7.0 %turn.25 = (bf16[6,128,768]{2,1,0:T(8,128)(2,1)}, bf16[2,128,768]{2,1,0:T(8,128)(2,1)S(1)}, bf16[128,128]{1,0:T(8,128)(2,1)S(1)}, bf16[8,128,768]{2,1,0:T(8,128)(2,1)S(1)}) custom-call(s32[1]{0:T(128)} %bitcast.9.place_ref, bf16[8,128,128]{2,1,0:T(8,128)(2,1)S(1)} %all_to_all.81.blocks_ref, ...), custom_call_target="tpu_custom_call", output_to_operand_aliasing={{3}: (7, {})} | custom-call | flops 2818572288 | bytes 22020096 | tf_op jit(solution)/shard_map/turn/pallas_call | solution.py:320
  233.3 7.1 %all-to-all-done.3.blocks_ref = bf16[8,128,128]{2,1,0:T(8,128)(2,1)S(1)} async-done(((bf16[8,128,128]{2,1,0:T(8,128)(2,1)}), bf16[8,128,128]{2,1,0:T(8,128)(2,1)S(1)}, u32[]{:S(2)}, u32[]{:S(2)}) %all-to-all-start.3) | async-done | bytes 262176 | tf_op jit(solution)/shard_map/all_to_all | solution.py:69
  255.3 7.9 %collective-permute-start.26 = (bf16[128,128]{1,0:T(8,128)(2,1)S(1)}, bf16[128,128]{1,0:T(8,128)(2,1)S(1)}, u32[]{:S(2)}, u32[]{:S(2)}) collective-permute-start(bf16[128,128]{1,0:T(8,128)(2,1)S(1)} %get-tuple-element.187), channel_id=1, source_target_pairs={{0,8},{8,0},{16,24},{24,16},{32,40},{40,32},{48,56},{56,48},{64,72... | collective-permute-start | bytes 98312 | tf_op jit(solution)/shard_map/ppermute | solution.py:48
  264.6 12.0 %all_to_all.82.blocks_ref = bf16[8,128,128]{2,1,0:T(8,128)(2,1)S(1)} all-to-all(bf16[8,128,128]{2,1,0:T(8,128)(2,1)S(1)} %copies.20), channel_id=1, replica_groups=mesh['section'=16,'tensor'=8] {'tensor'}, dimensions={0} | all-to-all | bytes 524288 | tf_op jit(solution)/shard_map/all_to_all | solution.py:69
  276.6 7.0 %turn.28 = (bf16[6,128,768]{2,1,0:T(8,128)(2,1)}, bf16[2,128,768]{2,1,0:T(8,128)(2,1)S(1)}, bf16[128,128]{1,0:T(8,128)(2,1)S(1)}, bf16[8,128,768]{2,1,0:T(8,128)(2,1)S(1)}) custom-call(s32[1]{0:T(128)} %bitcast.9.place_ref, bf16[8,128,128]{2,1,0:T(8,128)(2,1)S(1)} %all_to_all.82.blocks_ref, ...), custom_call_target="tpu_custom_call", output_to_operand_aliasing={{3}: (7, {})} | custom-call | flops 2818572288 | bytes 22020096 | tf_op jit(solution)/shard_map/turn/pallas_call | solution.py:320
  292.8 7.1 %all-to-all-done.5.blocks_ref = bf16[8,128,128]{2,1,0:T(8,128)(2,1)S(1)} async-done(((bf16[8,128,128]{2,1,0:T(8,128)(2,1)}), bf16[8,128,128]{2,1,0:T(8,128)(2,1)S(1)}, u32[]{:S(2)}, u32[]{:S(2)}) %all-to-all-start.5) | async-done | bytes 262176 | tf_op jit(solution)/shard_map/all_to_all | solution.py:69
  314.7 7.9 %collective-permute-start.32 = (bf16[128,128]{1,0:T(8,128)(2,1)S(1)}, bf16[128,128]{1,0:T(8,128)(2,1)S(1)}, u32[]{:S(2)}, u32[]{:S(2)}) collective-permute-start(bf16[128,128]{1,0:T(8,128)(2,1)S(1)} %get-tuple-element.203), channel_id=1, source_target_pairs={{0,8},{8,0},{16,24},{24,16},{32,40},{40,32},{48,56},{56,48},{64,72... | collective-permute-start | bytes 98312 | tf_op jit(solution)/shard_map/ppermute | solution.py:48
  324.1 12.0 %all_to_all.83.blocks_ref = bf16[8,128,128]{2,1,0:T(8,128)(2,1)S(1)} all-to-all(bf16[8,128,128]{2,1,0:T(8,128)(2,1)S(1)} %copies.22), channel_id=1, replica_groups=mesh['section'=16,'tensor'=8] {'tensor'}, dimensions={0} | all-to-all | bytes 524288 | tf_op jit(solution)/shard_map/all_to_all | solution.py:69
  336.1 7.0 %turn.31 = (bf16[6,128,768]{2,1,0:T(8,128)(2,1)}, bf16[2,128,768]{2,1,0:T(8,128)(2,1)S(1)}, bf16[128,128]{1,0:T(8,128)(2,1)S(1)}, bf16[8,128,768]{2,1,0:T(8,128)(2,1)S(1)}) custom-call(s32[1]{0:T(128)} %bitcast.9.place_ref, bf16[8,128,128]{2,1,0:T(8,128)(2,1)S(1)} %all_to_all.83.blocks_ref, ...), custom_call_target="tpu_custom_call", output_to_operand_aliasing={{3}: (7, {})} | custom-call | flops 2818572288 | bytes 22020096 | tf_op jit(solution)/shard_map/turn/pallas_call | solution.py:320
  352.4 7.0 %all-to-all-done.7.blocks_ref = bf16[8,128,128]{2,1,0:T(8,128)(2,1)S(1)} async-done(((bf16[8,128,128]{2,1,0:T(8,128)(2,1)}), bf16[8,128,128]{2,1,0:T(8,128)(2,1)S(1)}, u32[]{:S(2)}, u32[]{:S(2)}) %all-to-all-start.7) | async-done | bytes 262176 | tf_op jit(solution)/shard_map/all_to_all | solution.py:69
  376.2 14.2 %all_to_all.84.blocks_ref = bf16[8,128,128]{2,1,0:T(8,128)(2,1)S(1)} all-to-all(bf16[8,128,128]{2,1,0:T(8,128)(2,1)S(1)} %copies.24), channel_id=1, replica_groups=mesh['section'=16,'tensor'=8] {'tensor'}, dimensions={0} | all-to-all | bytes 524288 | tf_op jit(solution)/shard_map/all_to_all | solution.py:69
  390.3 7.0 %turn.34 = (bf16[6,128,768]{2,1,0:T(8,128)(2,1)}, bf16[2,128,768]{2,1,0:T(8,128)(2,1)S(1)}, bf16[128,128]{1,0:T(8,128)(2,1)S(1)}, bf16[8,128,768]{2,1,0:T(8,128)(2,1)S(1)}) custom-call(s32[1]{0:T(128)} %bitcast.9.place_ref, bf16[8,128,128]{2,1,0:T(8,128)(2,1)S(1)} %all_to_all.84.blocks_ref, ...), custom_call_target="tpu_custom_call", output_to_operand_aliasing={{3}: (7, {})} | custom-call | flops 2818572288 | bytes 22020096 | tf_op jit(solution)/shard_map/turn/pallas_call | solution.py:320
  407.2 7.2 %all-to-all-done.9.blocks_ref = bf16[8,128,128]{2,1,0:T(8,128)(2,1)S(1)} async-done(((bf16[8,128,128]{2,1,0:T(8,128)(2,1)}), bf16[8,128,128]{2,1,0:T(8,128)(2,1)S(1)}, u32[]{:S(2)}, u32[]{:S(2)}) %all-to-all-start.9) | async-done | bytes 262176 | tf_op jit(solution)/shard_map/all_to_all | solution.py:69
  437.4 13.3 %all_to_all.85.blocks_ref = bf16[8,128,128]{2,1,0:T(8,128)(2,1)S(1)} all-to-all(bf16[8,128,128]{2,1,0:T(8,128)(2,1)S(1)} %copies.26), channel_id=1, replica_groups=mesh['section'=16,'tensor'=8] {'tensor'}, dimensions={0} | all-to-all | bytes 524288 | tf_op jit(solution)/shard_map/all_to_all | solution.py:69
  450.7 7.0 %turn.37 = (bf16[6,128,768]{2,1,0:T(8,128)(2,1)}, bf16[2,128,768]{2,1,0:T(8,128)(2,1)S(1)}, bf16[128,128]{1,0:T(8,128)(2,1)S(1)}, bf16[8,128,768]{2,1,0:T(8,128)(2,1)S(1)}) custom-call(s32[1]{0:T(128)} %bitcast.9.place_ref, bf16[8,128,128]{2,1,0:T(8,128)(2,1)S(1)} %all_to_all.85.blocks_ref, ...), custom_call_target="tpu_custom_call", output_to_operand_aliasing={{3}: (7, {})} | custom-call | flops 2818572288 | bytes 22020096 | tf_op jit(solution)/shard_map/turn/pallas_call | solution.py:320
  466.8 7.1 %all-to-all-done.11.blocks_ref = bf16[8,128,128]{2,1,0:T(8,128)(2,1)S(1)} async-done(((bf16[8,128,128]{2,1,0:T(8,128)(2,1)}), bf16[8,128,128]{2,1,0:T(8,128)(2,1)S(1)}, u32[]{:S(2)}, u32[]{:S(2)}) %all-to-all-start.11) | async-done | bytes 262176 | tf_op jit(solution)/shard_map/all_to_all | solution.py:69
  488.8 7.2 %collective-permute-start.50 = (bf16[128,128]{1,0:T(8,128)(2,1)S(1)}, bf16[128,128]{1,0:T(8,128)(2,1)S(1)}, u32[]{:S(2)}, u32[]{:S(2)}) collective-permute-start(bf16[128,128]{1,0:T(8,128)(2,1)S(1)} %get-tuple-element.251), channel_id=1, source_target_pairs={{0,8},{8,0},{16,24},{24,16},{32,40},{40,32},{48,56},{56,48},{64,72... | collective-permute-start | bytes 98312 | tf_op jit(solution)/shard_map/ppermute | solution.py:48
  497.5 12.0 %all_to_all.86.blocks_ref = bf16[8,128,128]{2,1,0:T(8,128)(2,1)S(1)} all-to-all(bf16[8,128,128]{2,1,0:T(8,128)(2,1)S(1)} %copies.28), channel_id=1, replica_groups=mesh['section'=16,'tensor'=8] {'tensor'}, dimensions={0} | all-to-all | bytes 524288 | tf_op jit(solution)/shard_map/all_to_all | solution.py:69
  509.4 7.0 %turn.40 = (bf16[6,128,768]{2,1,0:T(8,128)(2,1)}, bf16[2,128,768]{2,1,0:T(8,128)(2,1)S(1)}, bf16[128,128]{1,0:T(8,128)(2,1)S(1)}, bf16[8,128,768]{2,1,0:T(8,128)(2,1)S(1)}) custom-call(s32[1]{0:T(128)} %bitcast.9.place_ref, bf16[8,128,128]{2,1,0:T(8,128)(2,1)S(1)} %all_to_all.86.blocks_ref, ...), custom_call_target="tpu_custom_call", output_to_operand_aliasing={{3}: (7, {})} | custom-call | flops 2818572288 | bytes 22020096 | tf_op jit(solution)/shard_map/turn/pallas_call | solution.py:320
  547.6 39.3 %collective-permute-start.56 = (bf16[128,128]{1,0:T(8,128)(2,1)S(1)}, bf16[128,128]{1,0:T(8,128)(2,1)S(1)}, u32[]{:S(2)}, u32[]{:S(2)}) collective-permute-start(bf16[128,128]{1,0:T(8,128)(2,1)S(1)} %get-tuple-element.267), channel_id=1, source_target_pairs={{0,8},{8,0},{16,24},{24,16},{32,40},{40,32},{48,56},{56,48},{64,72... | collective-permute-start | bytes 98312 | tf_op jit(solution)/shard_map/ppermute | solution.py:48
  588.3 12.0 %all_to_all.87.blocks_ref = bf16[8,128,128]{2,1,0:T(8,128)(2,1)S(1)} all-to-all(bf16[8,128,128]{2,1,0:T(8,128)(2,1)S(1)} %copies.30), channel_id=1, replica_groups=mesh['section'=16,'tensor'=8] {'tensor'}, dimensions={0} | all-to-all | bytes 524288 | tf_op jit(solution)/shard_map/all_to_all | solution.py:69
  600.2 9.1 %turn.43 = (bf16[6,128,768]{2,1,0:T(8,128)(2,1)}, bf16[2,128,768]{2,1,0:T(8,128)(2,1)}, bf16[128,128]{1,0:T(8,128)(2,1)S(1)}, bf16[8,128,768]{2,1,0:T(8,128)(2,1)S(1)}) custom-call(s32[1]{0:T(128)} %bitcast.9.place_ref, bf16[8,128,128]{2,1,0:T(8,128)(2,1)S(1)} %all_to_all.87.blocks_ref, ...), custom_call_target="tpu_custom_call", output_to_operand_aliasing={{3}: (7, {})} | custom-call | flops 2818572288 | bytes 22020096 | tf_op jit(solution)/shard_map/turn/pallas_call | solution.py:320
  (251 shorter events, 265.0 us)
Async XLA Ops:
  8.3 36.1 %collective-permute-start.1 = (bf16[1152,768]{1,0:T(8,128)(2,1)S(1)}, bf16[1152,768]{1,0:T(8,128)(2,1)}, u32[]{:S(2)}, u32[]{:S(2)}) collective-permute-start(bf16[1152,768]{1,0:T(8,128)(2,1)S(1)} %pad_maximum_fusion.refs_0_), channel_id=1, source_target_pairs={{0,4},{1,5},{2,6},{3,7},{4,0},{5,1},{6,2},{7,3},{8,12},{9,13},{10,... | collective-permute-start | bytes 5308424 | tf_op jit(solution)/shard_map/ppermute | solution.py:140
  14.0 15.1 %collective-permute-start.3 = (bf16[576,768]{1,0:T(8,128)(2,1)}, bf16[576,768]{1,0:T(8,128)(2,1)}, u32[]{:S(2)}, u32[]{:S(2)}) collective-permute-start(bf16[576,768]{1,0:T(8,128)(2,1)} %get-tuple-element.143), channel_id=1, source_target_pairs={{0,3},{1,0},{2,1},{3,2},{4,7},{5,4},{6,5},{7,6},{8,11},{9,8},{10,9... | collective-permute-start | bytes 2654216 | tf_op jit(solution)/shard_map/ppermute | solution.py:140
  16.7 14.6 %collective-permute-start.2 = (bf16[576,768]{1,0:T(8,128)(2,1)}, bf16[576,768]{1,0:T(8,128)(2,1)}, u32[]{:S(2)}, u32[]{:S(2)}) collective-permute-start(bf16[576,768]{1,0:T(8,128)(2,1)} %get-tuple-element.143), channel_id=1, source_target_pairs={{0,1},{1,2},{2,3},{3,0},{4,5},{5,6},{6,7},{7,4},{8,9},{9,10},{10,1... | collective-permute-start | bytes 2654216 | tf_op jit(solution)/shard_map/ppermute | solution.py:140
  16.7 23.7 %collective-permute-start.5 = (bf16[576,768]{1,0:T(8,128)(2,1)}, bf16[576,768]{1,0:T(8,128)(2,1)S(1)}, u32[]{:S(2)}, u32[]{:S(2)}) collective-permute-start(bf16[576,768]{1,0:T(8,128)(2,1)} %get-tuple-element.144), channel_id=1, source_target_pairs={{0,3},{1,0},{2,1},{3,2},{4,7},{5,4},{6,5},{7,6},{8,11},{9,8},{10,9... | collective-permute-start | bytes 2654216 | tf_op jit(solution)/shard_map/ppermute | solution.py:140
  20.0 24.4 %collective-permute-start.4 = (bf16[576,768]{1,0:T(8,128)(2,1)}, bf16[576,768]{1,0:T(8,128)(2,1)}, u32[]{:S(2)}, u32[]{:S(2)}) collective-permute-start(bf16[576,768]{1,0:T(8,128)(2,1)} %get-tuple-element.144), channel_id=1, source_target_pairs={{0,1},{1,2},{2,3},{3,0},{4,5},{5,6},{6,7},{7,4},{8,9},{9,10},{10,1... | collective-permute-start | bytes 2654216 | tf_op jit(solution)/shard_map/ppermute | solution.py:140
  44.4 20.7 %collective-permute-start.7 = (bf16[576,768]{1,0:T(8,128)(2,1)S(1)}, bf16[576,768]{1,0:T(8,128)(2,1)S(1)}, u32[]{:S(2)}, u32[]{:S(2)}) collective-permute-start(bf16[576,768]{1,0:T(8,128)(2,1)S(1)} %collective-permute-done.5.refs_4_), channel_id=1, source_target_pairs={{0,3},{1,0},{2,1},{3,2},{4,7},{5,4},{6,5},{7,6},{8,11},{9,8},{10,9... | collective-permute-start | bytes 2654216 | tf_op jit(solution)/shard_map/ppermute | solution.py:140
  45.6 23.5 %collective-permute-start.8 = (bf16[576,768]{1,0:T(8,128)(2,1)S(1)}, bf16[576,768]{1,0:T(8,128)(2,1)S(1)}, u32[]{:S(2)}, u32[]{:S(2)}) collective-permute-start(bf16[576,768]{1,0:T(8,128)(2,1)S(1)} %slice.42), channel_id=1, source_target_pairs={{0,1},{1,2},{2,3},{3,0},{4,5},{5,6},{6,7},{7,4},{8,9},{9,10},{10,1... | collective-permute-start | bytes 2654216 | tf_op jit(solution)/shard_map/ppermute | solution.py:140
  47.7 31.7 %collective-permute-start.10 = (bf16[576,768]{1,0:T(8,128)(2,1)S(1)}, bf16[576,768]{1,0:T(8,128)(2,1)S(1)}, u32[]{:S(2)}, u32[]{:S(2)}) collective-permute-start(bf16[576,768]{1,0:T(8,128)(2,1)S(1)} %slice.42), channel_id=1, source_target_pairs={{0,3},{1,0},{2,1},{3,2},{4,7},{5,4},{6,5},{7,6},{8,11},{9,8},{10,9... | collective-permute-start | bytes 2654216 | tf_op jit(solution)/shard_map/ppermute | solution.py:140
  48.9 34.3 %collective-permute-start.11 = (bf16[576,768]{1,0:T(8,128)(2,1)S(1)}, bf16[576,768]{1,0:T(8,128)(2,1)S(1)}, u32[]{:S(2)}, u32[]{:S(2)}) collective-permute-start(bf16[576,768]{1,0:T(8,128)(2,1)S(1)} %collective-permute-done.5.refs_4_), channel_id=1, source_target_pairs={{0,4},{1,5},{2,6},{3,7},{4,0},{5,1},{6,2},{7,3},{8,12},{9,13},{10,... | collective-permute-start | bytes 2654216 | tf_op jit(solution)/shard_map/ppermute | solution.py:140
  49.4 33.8 %collective-permute-start.6 = (bf16[576,768]{1,0:T(8,128)(2,1)}, bf16[576,768]{1,0:T(8,128)(2,1)S(1)}, u32[]{:S(2)}, u32[]{:S(2)}) collective-permute-start(bf16[576,768]{1,0:T(8,128)(2,1)} %collective-permute-done.2.refs_1_), channel_id=1, source_target_pairs={{0,1},{1,2},{2,3},{3,0},{4,5},{5,6},{6,7},{7,4},{8,9},{9,10},{10,1... | collective-permute-start | bytes 2654216 | tf_op jit(solution)/shard_map/ppermute | solution.py:140
  65.1 18.1 %collective-permute-start.9 = (bf16[576,768]{1,0:T(8,128)(2,1)}, bf16[576,768]{1,0:T(8,128)(2,1)S(1)}, u32[]{:S(2)}, u32[]{:S(2)}) collective-permute-start(bf16[576,768]{1,0:T(8,128)(2,1)} %collective-permute-done.4.refs_2_), channel_id=1, source_target_pairs={{0,4},{1,5},{2,6},{3,7},{4,0},{5,1},{6,2},{7,3},{8,12},{9,13},{10,... | collective-permute-start | bytes 2654216 | tf_op jit(solution)/shard_map/ppermute | solution.py:140
  69.1 32.0 %collective-permute-start.12 = (bf16[576,768]{1,0:T(8,128)(2,1)S(1)}, bf16[576,768]{1,0:T(8,128)(2,1)S(1)}, u32[]{:S(2)}, u32[]{:S(2)}) collective-permute-start(bf16[576,768]{1,0:T(8,128)(2,1)S(1)} %collective-permute-done.8.refs_2_), channel_id=1, source_target_pairs={{0,1},{1,2},{2,3},{3,0},{4,5},{5,6},{6,7},{7,4},{8,9},{9,10},{10,1... | collective-permute-start | bytes 2654216 | tf_op jit(solution)/shard_map/ppermute | solution.py:140
  79.5 24.1 %collective-permute-start.13 = (bf16[576,768]{1,0:T(8,128)(2,1)S(1)}, bf16[576,768]{1,0:T(8,128)(2,1)S(1)}, u32[]{:S(2)}, u32[]{:S(2)}) collective-permute-start(bf16[576,768]{1,0:T(8,128)(2,1)S(1)} %collective-permute-done.7.refs_1_), channel_id=1, source_target_pairs={{0,4},{1,5},{2,6},{3,7},{4,0},{5,1},{6,2},{7,3},{8,12},{9,13},{10,... | collective-permute-start | bytes 2654216 | tf_op jit(solution)/shard_map/ppermute | solution.py:140
  108.8 15.0 %collective-permute-start.14 = (bf16[128,128]{1,0:T(8,128)(2,1)S(1)}, bf16[128,128]{1,0:T(8,128)(2,1)S(1)}, u32[]{:S(2)}, u32[]{:S(2)}) collective-permute-start(bf16[128,128]{1,0:T(8,128)(2,1)S(1)} %get-tuple-element.155), channel_id=1, source_target_pairs={{0,8},{8,0},{16,24},{24,16},{32,40},{40,32},{48,56},{56,48},{64,72... | collective-permute-start | bytes 98312 | tf_op jit(solution)/shard_map/ppermute | solution.py:48
  146.4 14.8 %collective-permute-start.18 = (bf16[6,128,768]{2,1,0:T(8,128)(2,1)}, bf16[6,128,768]{2,1,0:T(8,128)(2,1)S(1)}, u32[]{:S(2)}, u32[]{:S(2)}) collective-permute-start(bf16[6,128,768]{2,1,0:T(8,128)(2,1)} %get-tuple-element.164), channel_id=1, source_target_pairs={{0,0},{8,16},{16,8},{24,32},{32,24},{40,48},{48,40},{56,56},{64,64... | collective-permute-start | bytes 3538952 | tf_op jit(solution)/shard_map/ppermute | solution.py:48
  152.5 21.9 %collective-permute-start.19 = (bf16[2,128,768]{2,1,0:T(8,128)(2,1)}, bf16[2,128,768]{2,1,0:T(8,128)(2,1)S(1)}, u32[]{:S(2)}, u32[]{:S(2)}) collective-permute-start(bf16[2,128,768]{2,1,0:T(8,128)(2,1)} %copy-done.26), channel_id=1, source_target_pairs={{0,0},{8,16},{16,8},{24,32},{32,24},{40,48},{48,40},{56,56},{64,64... | collective-permute-start | bytes 1179656 | tf_op jit(solution)/shard_map/ppermute | solution.py:48
  176.2 28.5 %collective-permute-start.20 = (bf16[128,128]{1,0:T(8,128)(2,1)S(1)}, bf16[128,128]{1,0:T(8,128)(2,1)S(1)}, u32[]{:S(2)}, u32[]{:S(2)}) collective-permute-start(bf16[128,128]{1,0:T(8,128)(2,1)S(1)} %get-tuple-element.171), channel_id=1, source_target_pairs={{0,8},{8,0},{16,24},{24,16},{32,40},{40,32},{48,56},{56,48},{64,72... | collective-permute-start | bytes 98312 | tf_op jit(solution)/shard_map/ppermute | solution.py:48
  225.6 14.8 %collective-permute-start.24 = (bf16[6,128,768]{2,1,0:T(8,128)(2,1)}, bf16[6,128,768]{2,1,0:T(8,128)(2,1)S(1)}, u32[]{:S(2)}, u32[]{:S(2)}) collective-permute-start(bf16[6,128,768]{2,1,0:T(8,128)(2,1)} %get-tuple-element.180), channel_id=1, source_target_pairs={{0,0},{8,16},{16,8},{24,32},{32,24},{40,48},{48,40},{56,56},{64,64... | collective-permute-start | bytes 3538952 | tf_op jit(solution)/shard_map/ppermute | solution.py:48
  231.7 21.9 %collective-permute-start.25 = (bf16[2,128,768]{2,1,0:T(8,128)(2,1)}, bf16[2,128,768]{2,1,0:T(8,128)(2,1)S(1)}, u32[]{:S(2)}, u32[]{:S(2)}) collective-permute-start(bf16[2,128,768]{2,1,0:T(8,128)(2,1)} %copy-done.27), channel_id=1, source_target_pairs={{0,0},{8,16},{16,8},{24,32},{32,24},{40,48},{48,40},{56,56},{64,64... | collective-permute-start | bytes 1179656 | tf_op jit(solution)/shard_map/ppermute | solution.py:48
  285.0 14.8 %collective-permute-start.30 = (bf16[6,128,768]{2,1,0:T(8,128)(2,1)}, bf16[6,128,768]{2,1,0:T(8,128)(2,1)S(1)}, u32[]{:S(2)}, u32[]{:S(2)}) collective-permute-start(bf16[6,128,768]{2,1,0:T(8,128)(2,1)} %get-tuple-element.196), channel_id=1, source_target_pairs={{0,0},{8,16},{16,8},{24,32},{32,24},{40,48},{48,40},{56,56},{64,64... | collective-permute-start | bytes 3538952 | tf_op jit(solution)/shard_map/ppermute | solution.py:48
  291.1 21.9 %collective-permute-start.31 = (bf16[2,128,768]{2,1,0:T(8,128)(2,1)}, bf16[2,128,768]{2,1,0:T(8,128)(2,1)S(1)}, u32[]{:S(2)}, u32[]{:S(2)}) collective-permute-start(bf16[2,128,768]{2,1,0:T(8,128)(2,1)} %copy-done.28), channel_id=1, source_target_pairs={{0,0},{8,16},{16,8},{24,32},{32,24},{40,48},{48,40},{56,56},{64,64... | collective-permute-start | bytes 1179656 | tf_op jit(solution)/shard_map/ppermute | solution.py:48
  344.4 15.0 %collective-permute-start.36 = (bf16[6,128,768]{2,1,0:T(8,128)(2,1)}, bf16[6,128,768]{2,1,0:T(8,128)(2,1)S(1)}, u32[]{:S(2)}, u32[]{:S(2)}) collective-permute-start(bf16[6,128,768]{2,1,0:T(8,128)(2,1)} %get-tuple-element.212), channel_id=1, source_target_pairs={{0,0},{8,8},{16,16},{24,24},{32,32},{40,40},{48,48},{56,64},{64,56... | collective-permute-start | bytes 3538952 | tf_op jit(solution)/shard_map/ppermute | solution.py:48
  350.5 22.0 %collective-permute-start.37 = (bf16[2,128,768]{2,1,0:T(8,128)(2,1)}, bf16[2,128,768]{2,1,0:T(8,128)(2,1)S(1)}, u32[]{:S(2)}, u32[]{:S(2)}) collective-permute-start(bf16[2,128,768]{2,1,0:T(8,128)(2,1)} %copy-done.29), channel_id=1, source_target_pairs={{0,0},{8,8},{16,16},{24,24},{32,32},{40,40},{48,48},{56,64},{64,56... | collective-permute-start | bytes 1179656 | tf_op jit(solution)/shard_map/ppermute | solution.py:48
  375.6 14.7 %collective-permute-start.39 = (bf16[6,128,768]{2,1,0:T(8,128)(2,1)S(1)}, bf16[6,128,768]{2,1,0:T(8,128)(2,1)S(1)}, u32[]{:S(2)}, u32[]{:S(2)}) collective-permute-start(bf16[6,128,768]{2,1,0:T(8,128)(2,1)S(1)} %get-tuple-element.221), channel_id=1, source_target_pairs={{0,8},{8,0},{16,24},{24,16},{32,40},{40,32},{48,56},{56,48},{64,72... | collective-permute-start | bytes 3538952 | tf_op jit(solution)/shard_map/ppermute | solution.py:48
  375.8 14.6 %collective-permute-start.40 = (bf16[2,128,768]{2,1,0:T(8,128)(2,1)S(1)}, bf16[2,128,768]{2,1,0:T(8,128)(2,1)S(1)}, u32[]{:S(2)}, u32[]{:S(2)}) collective-permute-start(bf16[2,128,768]{2,1,0:T(8,128)(2,1)S(1)} %get-tuple-element.222), channel_id=1, source_target_pairs={{0,8},{8,0},{16,24},{24,16},{32,40},{40,32},{48,56},{56,48},{64,72... | collective-permute-start | bytes 1179656 | tf_op jit(solution)/shard_map/ppermute | solution.py:48
  398.7 15.7 %collective-permute-start.42 = (bf16[6,128,768]{2,1,0:T(8,128)(2,1)}, bf16[6,128,768]{2,1,0:T(8,128)(2,1)S(1)}, u32[]{:S(2)}, u32[]{:S(2)}) collective-permute-start(bf16[6,128,768]{2,1,0:T(8,128)(2,1)} %get-tuple-element.228), channel_id=1, source_target_pairs={{0,0},{8,16},{16,8},{24,32},{32,24},{40,48},{48,40},{56,56},{64,64... | collective-permute-start | bytes 3538952 | tf_op jit(solution)/shard_map/ppermute | solution.py:48
  405.6 22.0 %collective-permute-start.43 = (bf16[2,128,768]{2,1,0:T(8,128)(2,1)}, bf16[2,128,768]{2,1,0:T(8,128)(2,1)S(1)}, u32[]{:S(2)}, u32[]{:S(2)}) collective-permute-start(bf16[2,128,768]{2,1,0:T(8,128)(2,1)} %copy-done.30), channel_id=1, source_target_pairs={{0,0},{8,16},{16,8},{24,32},{32,24},{40,48},{48,40},{56,56},{64,64... | collective-permute-start | bytes 1179656 | tf_op jit(solution)/shard_map/ppermute | solution.py:48
  459.1 14.8 %collective-permute-start.48 = (bf16[6,128,768]{2,1,0:T(8,128)(2,1)}, bf16[6,128,768]{2,1,0:T(8,128)(2,1)S(1)}, u32[]{:S(2)}, u32[]{:S(2)}) collective-permute-start(bf16[6,128,768]{2,1,0:T(8,128)(2,1)} %get-tuple-element.244), channel_id=1, source_target_pairs={{0,0},{8,16},{16,8},{24,32},{32,24},{40,48},{48,40},{56,56},{64,64... | collective-permute-start | bytes 3538952 | tf_op jit(solution)/shard_map/ppermute | solution.py:48
  465.2 21.9 %collective-permute-start.49 = (bf16[2,128,768]{2,1,0:T(8,128)(2,1)}, bf16[2,128,768]{2,1,0:T(8,128)(2,1)S(1)}, u32[]{:S(2)}, u32[]{:S(2)}) collective-permute-start(bf16[2,128,768]{2,1,0:T(8,128)(2,1)} %copy-done.31), channel_id=1, source_target_pairs={{0,0},{8,16},{16,8},{24,32},{32,24},{40,48},{48,40},{56,56},{64,64... | collective-permute-start | bytes 1179656 | tf_op jit(solution)/shard_map/ppermute | solution.py:48
  517.8 14.8 %collective-permute-start.54 = (bf16[6,128,768]{2,1,0:T(8,128)(2,1)}, bf16[6,128,768]{2,1,0:T(8,128)(2,1)S(1)}, u32[]{:S(2)}, u32[]{:S(2)}) collective-permute-start(bf16[6,128,768]{2,1,0:T(8,128)(2,1)} %get-tuple-element.260), channel_id=1, source_target_pairs={{0,0},{8,16},{16,8},{24,32},{32,24},{40,48},{48,40},{56,56},{64,64... | collective-permute-start | bytes 3538952 | tf_op jit(solution)/shard_map/ppermute | solution.py:48
  523.9 21.9 %collective-permute-start.55 = (bf16[2,128,768]{2,1,0:T(8,128)(2,1)}, bf16[2,128,768]{2,1,0:T(8,128)(2,1)S(1)}, u32[]{:S(2)}, u32[]{:S(2)}) collective-permute-start(bf16[2,128,768]{2,1,0:T(8,128)(2,1)} %copy-done.32), channel_id=1, source_target_pairs={{0,0},{8,16},{16,8},{24,32},{32,24},{40,48},{48,40},{56,56},{64,64... | collective-permute-start | bytes 1179656 | tf_op jit(solution)/shard_map/ppermute | solution.py:48
  547.6 40.1 %collective-permute-start.56 = (bf16[128,128]{1,0:T(8,128)(2,1)S(1)}, bf16[128,128]{1,0:T(8,128)(2,1)S(1)}, u32[]{:S(2)}, u32[]{:S(2)}) collective-permute-start(bf16[128,128]{1,0:T(8,128)(2,1)S(1)} %get-tuple-element.267), channel_id=1, source_target_pairs={{0,8},{8,0},{16,24},{24,16},{32,40},{40,32},{48,56},{56,48},{64,72... | collective-permute-start | bytes 98312 | tf_op jit(solution)/shard_map/ppermute | solution.py:48
  (72 other events, 608.7 us)
